TPU v7x, 32 devices: a whole 2x2x4 slice. The times are simulated.
32 devices in a mesh: dp: 8 (over z, core), fsdp: 4 (over y, x).
Axes of the slice: x: 2, y: 2, z: 4, core: 2. Of those that a mesh axis runs over, the one named last changes fastest.
Arguments:
- activations: bfloat16 [6144, 8192], P(('dp', 'fsdp')), may hold values from -6 to 6
- cotangent: bfloat16 [6144, 4096], P(('dp', 'fsdp')), may hold values from -0.059814453 to 0.059814453
- basis: bfloat16 [8192, 256], P('fsdp'), may hold values from -0.0625 to 0.0625
- first_moment: float32 [4096, 256], P(('dp', 'fsdp')), may hold values from -1.2 to 1.2
- second_moment: float32 [4096, 256], P(('dp', 'fsdp')), may hold values from 0.005 to 0.05
Outputs:
- update: bfloat16 [8192, 4096], P('fsdp', 'dp')
- new_first: float32 [4096, 256], P(('dp', 'fsdp'))
- new_second: float32 [4096, 256], P(('dp', 'fsdp'))
All inputs are finite; a program needn't handle non-finite values.
Results may differ from a plain program's by a relative error of at most 0.0052.
Values may be sent and summed in bfloat16 or wider, within the bound.
No kernel may reach another device: no remote copies, remote signals or barrier semaphores. Data moves between devices by JAX's collectives and lax.ppermute only.
A program may use at most 64 MiB of HBM per device.

v0:
```python
import jax
import jax.numpy as jnp
from jax import lax
from jax.sharding import PartitionSpec as P

ADAM_STEP = 10


def local(activations, cotangent, basis, first_moment, second_moment):
    projected = jnp.dot(
        activations,
        lax.all_gather(basis, "fsdp", axis=0, tiled=True),
        preferred_element_type=jnp.float32,
    ).astype(jnp.bfloat16)
    grad = lax.psum_scatter(
        lax.dot_general(
            cotangent, projected, (((0,), (0,)), ((), ())), preferred_element_type=jnp.float32
        ),
        ("dp", "fsdp"),
        scatter_dimension=0,
        tiled=True,
    )
    new_first = 0.9 * first_moment + 0.1 * grad
    new_second = 0.999 * second_moment + 0.001 * grad * grad
    bias_one = 1.0 - 0.9**ADAM_STEP
    bias_two = 1.0 - 0.999**ADAM_STEP
    step = (new_first / bias_one / (jnp.sqrt(new_second / bias_two) + 1e-08)).astype(jnp.bfloat16)
    update = lax.dot_general(
        basis,
        lax.all_gather(step, "fsdp", axis=0, tiled=True),
        (((1,), (1,)), ((), ())),
        preferred_element_type=jnp.float32,
    )
    return ((16.0 * update).astype(jnp.bfloat16), new_first, new_second)


def solution(mesh):
    in_specs = (
        P(("dp", "fsdp"), None),
        P(("dp", "fsdp"), None),
        P("fsdp", None),
        P(("dp", "fsdp"), None),
        P(("dp", "fsdp"), None),
    )
    out_specs = (P("fsdp", "dp"), P(("dp", "fsdp"), None), P(("dp", "fsdp"), None))
    return jax.shard_map(local, mesh=mesh, in_specs=in_specs, out_specs=out_specs, check_vma=False)
```

profile of v0, /device:TPU:0, one launch (start us, length us, event | category | flops | bytes accessed | tf_op | source)
XLA Modules:
  0.0 240.5 jit_solution(16267514615788489126)
XLA Ops:
  7.2 0.0 copy-start
  7.2 0.0 all-gather.2.cloned.1.call-start
  7.2 0.7 all-gather.2.cloned.1.call-update
  7.9 0.0 reduce-scatter.2.cloned.1.call-start
  8.0 57.3 %all-gather.2.cloned.1.call-done = bf16[8192,256]{1,0:T(8,128)(2,1)} async-done(((bf16[2048,256]{1,0:T(8,128)(2,1)}), bf16[8192,256]{1,0:T(8,128)(2,1)}) %all-gather.2.cloned.1.call-update) | async-done | bytes 4194320 | tf_op jit(solution)/shard_map/all_gather | solution.py:12
  65.3 0.0 copy-done
  65.3 7.4 %convolution_bitcast_fusion = f32[4096,256]{0,1:T(8,128)} fusion(bf16[192,4096]{1,0:T(8,128)(2,1)} %param.6, bf16[192,8192]{1,0:T(8,128)(2,1)S(1)} %copy-done, bf16[8192,256]{1,0:T(8,128)(2,1)} %all-gather.2.cloned.1.call-done), kind=kOutput, calls=%fused_computation | convolution fusion | flops 1208008704 | bytes 13107200 | tf_op jit(solution)/shard_map/dot_general | solution.py:16
  72.7 0.0 copy-start.1
  72.7 0.0 copy-start.2
  72.7 0.0 reduce-scatter.2.cloned.1.call-update
  72.7 0.9 copy-done.1
  73.6 0.1 copy.8
  73.7 0.0 copy-done.2
  73.7 0.1 copy.9
  73.8 140.2 %reduce-scatter.2.cloned.1.call-done = f32[128,256]{0,1:T(8,128)} async-done(((f32[4096,256]{0,1:T(8,128)}), f32[128,256]{0,1:T(8,128)}) %reduce-scatter.2.cloned.1.call-update) | async-done | bytes 131088 | tf_op jit(solution)/shard_map/reduce_scatter | solution.py:15
  214.0 1.7 divide_convert_fusion
  215.7 1.7 copy.11
  217.3 0.8 copy.12
  218.1 8.3 %all_gather.7 = bf16[512,256]{0,1:T(8,128)(2,1)S(1)} all-gather(bf16[128,256]{0,1:T(8,128)(2,1)} %get-tuple-element.6), channel_id=1, replica_groups=mesh['dp'=8,'fsdp'=4] {'fsdp'}, dimensions={0}, use_global_device_ids=true | all-gather | bytes 327680 | tf_op jit(solution)/shard_map/all_gather | solution.py:30
  226.4 3.3 %fusion = bf16[2048,512]{0,1:T(8,128)(2,1)} fusion(bf16[512,256]{0,1:T(8,128)(2,1)S(1)} %all_gather.7, bf16[2048,256]{1,0:T(8,128)(2,1)} %param.7), kind=kOutput, calls=%fused_computation.2 | convolution fusion | flops 538968064 | bytes 3407872 | tf_op jit(solution)/shard_map/dot_general | solution.py:28
  229.7 3.9 %copy.10 = bf16[2048,512]{1,0:T(8,128)(2,1)} copy(bf16[2048,512]{0,1:T(8,128)(2,1)} %fusion) | data formatting | bytes 4194304
Async XLA Ops:
  7.2 58.1 %copy-start = (bf16[192,8192]{1,0:T(8,128)(2,1)S(1)}, bf16[192,8192]{1,0:T(8,128)(2,1)}, u32[]{:S(2)}) copy-start(bf16[192,8192]{1,0:T(8,128)(2,1)} %param.5) | copy-start | bytes 9437188
  7.2 58.1 %all-gather.2.cloned.1.call-start = ((), (), s32[]{:S(2)}) async-start(), calls=%async_computation.1 | async-start | bytes 5242880 | tf_op jit(solution)/shard_map/all_gather | solution.py:12
  7.9 206.1 %reduce-scatter.2.cloned.1.call-start = ((), (), s32[]{:S(2)}) async-start(), calls=%async_computation.2 | async-start | bytes 4325376 | tf_op jit(solution)/shard_map/reduce_scatter | solution.py:15
  72.7 0.9 copy-start.1
  72.7 1.0 copy-start.2
Sparse Core Ops, SparseCore 0:
  9.9 55.3 all-gather.1
  72.8 141.1 reduce-scatter.1
where the time goes:
time: 241 us; the launch traced here: 240 us
  waiting for transfers between devices  198 us (82%)
  between operations  14.1 us (6%)
  matrix products  10.7 us (4%)
  blocking collectives  8.28 us (3%)
  local copies, waits for them, and re-layouts  7.39 us (3%)
    reduce_scatter x1, waiting for transfers between devices, local(): lax.psum_scatter(lax.dot_general(cotangent, projected, (((0,), (0,)), (()...  140 us
    all_gather x1, waiting for transfers between devices, local(): lax.all_gather(basis, 'fsdp', axis=0, tiled=True)  57.3 us
    all_gather x1, blocking collectives, local(): lax.all_gather(step, 'fsdp', axis=0, tiled=True)  8.28 us
    unnamed x11, local copies, waits for them, and re-layouts  7.39 us
    dot_general x1, matrix products, local(): lax.dot_general(cotangent, projected, (((0,), (0,)), ((), ())), preferred...  7.37 us
  transfers between devices with their start and end apart: 2, of which 2 were waited for; matrix products, arithmetic and copies ran while one was open for 0% of the time, Pallas kernels for 0%

commit v1 on v0

v1 whole, which is shorter than its diff:
```python
import jax
import jax.numpy as jnp
from jax import lax
from jax.sharding import PartitionSpec as P

ADAM_STEP = 10


def dot(a, b):
    return jnp.dot(a, b, preferred_element_type=jnp.float32)


def solution(mesh):
    dp, fsdp = mesh.shape["dp"], mesh.shape["fsdp"]
    pairs = dp // 2

    def swap(value, across_pairs=0, across_fsdp=0, across_core=0):
        mask = across_pairs * 2 + across_core
        steps = [
            (d * fsdp + f, (d ^ mask) * fsdp + (f ^ across_fsdp))
            for d in range(dp)
            for f in range(fsdp)
        ]
        return lax.ppermute(value, ("dp", "fsdp"), steps)

    def local(activations, cotangent, basis, first_moment, second_moment):
        tokens, depth, rank = activations.shape[0], basis.shape[0], basis.shape[1]
        half, rows = depth // 2, first_moment.shape[0]
        mine, here = lax.axis_index("dp"), lax.axis_index("fsdp")
        core, pair = mine % 2, mine // 2

        part = lax.dynamic_slice(basis, (core * half, 0), (half, rank))
        parts = [part] + [swap(part, across_fsdp=k) for k in range(1, fsdp)]
        shared = [activations, swap(activations, across_core=1)]
        features = jnp.concatenate([cotangent, swap(cotangent, across_core=1)], axis=0)

        features = features.T.reshape(pairs, 2, fsdp, rows, 2 * tokens)
        features = lax.dynamic_index_in_dim(features, core, 1, keepdims=False)
        features = jnp.take(features, jnp.arange(pairs) ^ pair, axis=0)
        features = jnp.take(features, jnp.arange(fsdp) ^ here, axis=1)
        features = features.swapaxes(0, 1)

        projected = []
        for block in shared:
            total = 0.0
            for k, piece in enumerate(parts):
                start = (here ^ k) * depth + core * half
                total += dot(lax.dynamic_slice(block, (0, start), (tokens, half)), piece)
            projected.append(total)
        projected = jnp.concatenate(projected, axis=0)
        other = swap(projected.astype(jnp.bfloat16), across_core=1)
        other = jnp.concatenate([other[tokens:], other[:tokens]], axis=0)
        projected = (projected + other.astype(jnp.float32)).astype(jnp.bfloat16)

        def term(k):
            return dot(features[k].reshape(-1, 2 * tokens), projected).reshape(pairs, rows, rank)

        arrived = [swap(term(k).astype(jnp.bfloat16), across_fsdp=k) for k in range(1, fsdp)]
        plane = term(0)
        for value in arrived:
            plane += value.astype(jnp.float32)
        arrived = [swap(plane[k].astype(jnp.bfloat16), across_pairs=k) for k in range(1, pairs)]
        grad = plane[0]
        for value in arrived:
            grad += value.astype(jnp.float32)

        new_first = 0.9 * first_moment + 0.1 * grad
        new_second = 0.999 * second_moment + 0.001 * grad * grad
        bias_one = 1.0 - 0.9**ADAM_STEP
        bias_two = 1.0 - 0.999**ADAM_STEP
        step = (new_first / bias_one / (jnp.sqrt(new_second / bias_two) + 1e-08)).astype(jnp.bfloat16)
        update = lax.dot_general(
            basis,
            lax.all_gather(step, "fsdp", axis=0, tiled=True),
            (((1,), (1,)), ((), ())),
            preferred_element_type=jnp.float32,
        )
        return ((16.0 * update).astype(jnp.bfloat16), new_first, new_second)

    in_specs = (
        P(("dp", "fsdp"), None),
        P(("dp", "fsdp"), None),
        P("fsdp", None),
        P(("dp", "fsdp"), None),
        P(("dp", "fsdp"), None),
    )
    out_specs = (P("fsdp", "dp"), P(("dp", "fsdp"), None), P(("dp", "fsdp"), None))
    return jax.shard_map(local, mesh=mesh, in_specs=in_specs, out_specs=out_specs, check_vma=False)
```

time: 241 us -> 97.7 us (0.41)
  waiting for transfers between devices: 198 us -> 37.5 us
  starting transfers between devices: 0.08 us -> 13.3 us
  between operations: 14.1 us -> 0.94 us
  local copies, waits for them, and re-layouts: 7.39 us -> 18.3 us
  other arithmetic: 1.66 us -> 6.02 us
    reduce_scatter x1 -> x0, waiting for transfers between devices: 140 us -> none  [local(): lax.psum_scatter(lax.dot_general(cotangent, projected, (((0,), (0,)), (()...]
    all_gather x1 -> x0, waiting for transfers between devices: 57.3 us -> none  [local(): lax.all_gather(basis, 'fsdp', axis=0, tiled=True)]
    ppermute x0 -> x12, waiting for transfers between devices: none -> 37.5 us  [swap(): return lax.ppermute(value, ('dp', 'fsdp'), steps)]
    ppermute x0 -> x12, starting transfers between devices: none -> 13.3 us  [swap(): return lax.ppermute(value, ('dp', 'fsdp'), steps)]
    reshape x0 -> x1, local copies, waits for them, and re-layouts: none -> 6.08 us  [local(): features = features.T.reshape(pairs, 2, fsdp, rows, 2 * tokens)]
    dot_general x1 -> x12, matrix products: 7.37 us -> 12.3 us  [dot(): return jnp.dot(a, b, preferred_element_type=jnp.float32)]
    gather x0 -> x2, local copies, waits for them, and re-layouts: none -> 4.6 us  [the longest x1 2.3 us: local(): features = jnp.take(features, jnp.arange(pairs) ^ pair, axis=0)]
    transpose x0 -> x1, other arithmetic: none -> 3.45 us  [local(): features = features.T.reshape(pairs, 2, fsdp, rows, 2 * tokens)]
  transfers between devices with their start and end apart: 2 -> 12, of which waited for: 2 -> 7; matrix products, arithmetic and copies ran while one was open for 0% -> 27% of each run, Pallas kernels for 0% -> 0%
where the time goes in v1:
time: 97.7 us; the launch traced here: 97.1 us
  waiting for transfers between devices  37.5 us (38%)
  local copies, waits for them, and re-layouts  18.3 us (19%)
  starting transfers between devices  13.3 us (14%)
  matrix products  13 us (13%)
  blocking collectives  7.97 us (8%)
  other arithmetic  6.02 us (6%)
    ppermute x12, waiting for transfers between devices, swap(): return lax.ppermute(value, ('dp', 'fsdp'), steps)  37.5 us
    ppermute x12, starting transfers between devices, swap(): return lax.ppermute(value, ('dp', 'fsdp'), steps)  13.3 us
    dot_general x12, matrix products, dot(): return jnp.dot(a, b, preferred_element_type=jnp.float32)  12.3 us
    all_gather x1, blocking collectives, local(): lax.all_gather(step, 'fsdp', axis=0, tiled=True)  7.97 us
    reshape x1, local copies, waits for them, and re-layouts, local(): features = features.T.reshape(pairs, 2, fsdp, rows, 2 * tokens)  6.08 us
    unnamed x18, local copies, waits for them, and re-layouts  5.64 us
    transpose x1, other arithmetic, local(): features = features.T.reshape(pairs, 2, fsdp, rows, 2 * tokens)  3.45 us
    gather x1, local copies, waits for them, and re-layouts, local(): features = jnp.take(features, jnp.arange(pairs) ^ pair, axis=0)  2.3 us
  transfers between devices with their start and end apart: 12, of which 7 were waited for; matrix products, arithmetic and copies ran while one was open for 27% of the time, Pallas kernels for 0%

profile of v1, /device:TPU:0, one launch (start us, length us, event | category | flops | bytes accessed | tf_op | source)
XLA Modules:
  0.0 97.1 jit_solution(11642457059178547527)
XLA Ops:
  1.2 0.6 copy-done
  1.9 4.0 %collective-permute-start.3 = (bf16[1024,256]{1,0:T(8,128)(2,1)S(1)}, bf16[1024,256]{1,0:T(8,128)(2,1)S(1)}, u32[]{:S(2)}, u32[]{:S(2)}) collective-permute-start(bf16[1024,256]{1,0:T(8,128)(2,1)S(1)} %constant_dynamic-slice_fusion), channel_id=1, source_target_pairs={{0,3},{1,2},{2,1},{3,0},{4,7},{5,6},{6,5},{7,4},{8,11},{9,10},{10,... | collective-permute-start | bytes 1572872 | tf_op jit(solution)/shard_map/ppermute | solution.py:24
  6.5 1.3 %fusion.16 = f32[192,256]{1,0:T(8,128)S(1)} fusion(bf16[1024,256]{1,0:T(8,128)(2,1)S(1)} %constant_dynamic-slice_fusion, bf16[192,8192]{1,0:T(8,128)(2,1)} %param.5, s32[]{:T(128)S(6)} %select_n.87), kind=kOutput, calls=%fused_computation.35 | convolution fusion | flops 100663296 | bytes 1114116 | tf_op jit(solution)/shard_map/dot_general | solution.py:10
  7.9 10.8 %collective-permute-done.3 = bf16[1024,256]{1,0:T(8,128)(2,1)S(1)} collective-permute-done((bf16[1024,256]{1,0:T(8,128)(2,1)S(1)}, bf16[1024,256]{1,0:T(8,128)(2,1)S(1)}, u32[]{:S(2)}, u32[]{:S(2)}) %collective-permute-start.3) | collective-permute-done | bytes 524320 | tf_op jit(solution)/shard_map/ppermute | solution.py:24
  18.7 1.5 %fusion.12 = f32[192,256]{1,0:T(8,128)S(1)} fusion(bf16[1024,256]{1,0:T(8,128)(2,1)S(1)} %collective-permute-done.3, bf16[192,8192]{1,0:T(8,128)(2,1)} %param.5, s32[]{:T(128)S(6)} %select_n.91), kind=kOutput, calls=%fused_computation.31 | convolution fusion | flops 100663296 | bytes 1114116 | tf_op jit(solution)/shard_map/dot_general | solution.py:10
  20.1 9.2 %collective-permute-done.1 = bf16[1024,256]{1,0:T(8,128)(2,1)S(1)} collective-permute-done((bf16[1024,256]{1,0:T(8,128)(2,1)S(1)}, bf16[1024,256]{1,0:T(8,128)(2,1)S(1)}, u32[]{:S(2)}, u32[]{:S(2)}) %collective-permute-start.1) | collective-permute-done | bytes 524320 | tf_op jit(solution)/shard_map/ppermute | solution.py:24
  29.3 1.5 %convolution_add_fusion.2 = f32[192,256]{1,0:T(8,128)S(1)} fusion(f32[192,256]{1,0:T(8,128)S(1)} %fusion.16, bf16[1024,256]{1,0:T(8,128)(2,1)S(1)} %collective-permute-done.1, bf16[192,8192]{1,0:T(8,128)(2,1)} %param.5, s32[]{:T(128)S(6)} %select_n.89), kind=kOutput, calls=%fused_computation.12 | convolution fusion | flops 100712448 | bytes 1310724 | tf_op jit(solution)/shard_map/dot_general | solution.py:10
  30.8 1.5 %fusion.1 = f32[192,256]{1,0:T(8,128)S(1)} fusion(f32[192,256]{1,0:T(8,128)S(1)} %fusion.12, f32[192,256]{1,0:T(8,128)S(1)} %convolution_add_fusion.2, bf16[1024,256]{1,0:T(8,128)(2,1)S(1)} %collective-permute-done.2, bf16[192,8192]{1,0:T(8,128)(2,1)} %param.5, s32[]{:T(128)S(6)} %select_n.90), kind=kOutput, calls=%fused_computation.13 | convolution fusion | flops 100761600 | bytes 1507332 | tf_op jit(solution)/shard_map/dot_general | solution.py:10
  32.3 3.5 %maximum_bitcast_fusion = bf16[4096,384]{0,1:T(8,128)(2,1)} fusion(bf16[192,4096]{1,0:T(8,128)(2,1)} %collective-permute-done, bf16[192,4096]{1,0:T(8,128)(2,1)S(1)} %copy-done.5), kind=kLoop, calls=%fused_computation.3 | loop fusion | flops 6291456 | bytes 6291456 | tf_op jit(solution)/shard_map/transpose | solution.py:37
  35.7 6.1 %reshape.66 = bf16[4,2,4,128,384]{3,2,1,0,4:T(4,128)(2,1)} reshape(bf16[4096,384]{0,1:T(8,128)(2,1)} %maximum_bitcast_fusion) | data formatting | bytes 6291456 | tf_op jit(solution)/shard_map/reshape | solution.py:37
  41.8 1.9 %constant_dynamic-slice_fusion.1 = bf16[4,1,4,128,384]{3,2,1,0,4:T(4,128)(2,1)S(1)} fusion(bf16[4,2,4,128,384]{3,2,1,0,4:T(4,128)(2,1)} %reshape.66, s32[]{:T(128)S(6)} %select_n.81), kind=kLoop, calls=%fused_computation.65 | loop fusion | bytes 3145732 | tf_op jit(solution)/shard_map/jit(dynamic_index_in_dim)/dynamic_slice | solution.py:38
  43.8 2.5 %copy.11 = bf16[4,1,4,128,384]{4,3,2,0,1:T(8,128)(2,1)} copy(bf16[4,1,4,128,384]{3,2,1,0,4:T(4,128)(2,1)S(1)} %constant_dynamic-slice_fusion.1) | data formatting | bytes 3145728
  46.3 2.3 %gather_fusion = bf16[4,4,128,384]{3,2,1,0:T(8,128)(2,1)S(1)} fusion(bf16[4,4,128,384]{3,2,1,0:T(8,128)(2,1)} %bitcast.63, s32[1024]{0:T(1024)S(1)} %pad_clamp_fusion.1), kind=kCustom, calls=%fused_computation | custom fusion | bytes 3145744 | tf_op jit(solution)/shard_map/jit(_take)/gather | solution.py:39
  48.6 1.4 %broadcast_select_fusion.1 = bf16[4,4,128,384]{3,2,1,0:T(8,128)(2,1)} fusion(bf16[4,4,128,384]{3,2,1,0:T(8,128)(2,1)S(1)} %gather_fusion, pred[4]{0:T(512)(128)(4,1)S(1)} %compare_and_fusion), kind=kLoop, calls=%fused_computation.6 | loop fusion | flops 786432 | bytes 3145732 | tf_op jit(solution)/shard_map/jit(_take)/select_n | solution.py:39
  50.0 2.3 %gather_fusion.1 = bf16[4,4,128,384]{3,2,1,0:T(8,128)(2,1)S(1)} fusion(bf16[4,4,128,384]{3,2,1,0:T(8,128)(2,1)} %broadcast_select_fusion.1, s32[1024]{0:T(1024)S(1)} %pad_clamp_fusion), kind=kCustom, calls=%fused_computation.1 | custom fusion | bytes 3145744 | tf_op jit(solution)/shard_map/jit(_take)/gather | solution.py:40
  52.3 1.5 %fusion.5 = f32[192,256]{1,0:T(8,128)S(1)} fusion(bf16[1024,256]{1,0:T(8,128)(2,1)} %copy-done.3, bf16[192,8192]{1,0:T(8,128)(2,1)} %collective-permute-done.4, s32[]{:T(128)S(6)} %select_n.91), kind=kOutput, calls=%fused_computation.24 | convolution fusion | flops 100663296 | bytes 1114116 | tf_op jit(solution)/shard_map/dot_general | solution.py:10
  53.8 1.4 %fusion.7 = f32[192,256]{1,0:T(8,128)S(1)} fusion(bf16[1024,256]{1,0:T(8,128)(2,1)} %copy-done.4, bf16[192,8192]{1,0:T(8,128)(2,1)} %collective-permute-done.4, s32[]{:T(128)S(6)} %select_n.90), kind=kOutput, calls=%fused_computation.26 | convolution fusion | flops 100663296 | bytes 1114116 | tf_op jit(solution)/shard_map/dot_general | solution.py:10
  55.2 1.3 %fusion.9 = f32[192,256]{1,0:T(8,128)S(1)} fusion(bf16[1024,256]{1,0:T(8,128)(2,1)S(1)} %copy-done.2, bf16[192,8192]{1,0:T(8,128)(2,1)} %collective-permute-done.4, s32[]{:T(128)S(6)} %select_n.89), kind=kOutput, calls=%fused_computation.28 | convolution fusion | flops 100663296 | bytes 1114116 | tf_op jit(solution)/shard_map/dot_general | solution.py:10
  56.5 1.3 %fusion.3 = f32[192,256]{1,0:T(8,128)S(1)} fusion(f32[192,256]{1,0:T(8,128)S(1)} %fusion.5, f32[192,256]{1,0:T(8,128)S(1)} %fusion.7, f32[192,256]{1,0:T(8,128)S(1)} %fusion.9, bf16[1024,256]{1,0:T(8,128)(2,1)S(1)} %constant_dynamic-slice_fusion, bf16[192,8192]{1,0:T(8,128)(2,1)} %collective-permute-done.4, s32[]{:T(128)S(6)} %select_n.87), kind=kOutput, calls=%fused_computation.15 | convolution fusion | flops 100810752 | bytes 1703940 | tf_op jit(solution)/shard_map/dot_general | solution.py:10
  58.2 1.2 %collective-permute-done.5 = bf16[384,256]{1,0:T(8,128)(2,1)S(1)} collective-permute-done((bf16[384,256]{1,0:T(8,128)(2,1)S(1)}, bf16[384,256]{1,0:T(8,128)(2,1)S(1)}, u32[]{:S(2)}, u32[]{:S(2)}) %collective-permute-start.5) | collective-permute-done | bytes 196640 | tf_op jit(solution)/shard_map/ppermute | solution.py:24
  60.3 1.5 %collective-permute-start.8 = (bf16[4,128,256]{2,1,0:T(8,128)(2,1)S(1)}, bf16[4,128,256]{2,1,0:T(8,128)(2,1)S(1)}, u32[]{:S(2)}, u32[]{:S(2)}) collective-permute-start(bf16[4,128,256]{2,1,0:T(8,128)(2,1)S(1)} %convolution_convert_fusion), channel_id=1, source_target_pairs={{0,3},{1,2},{2,1},{3,0},{4,7},{5,6},{6,5},{7,4},{8,11},{9,10},{10,... | collective-permute-start | bytes 786440 | tf_op jit(solution)/shard_map/ppermute | solution.py:24
  61.8 1.5 %collective-permute-start.7 = (bf16[4,128,256]{2,1,0:T(8,128)(2,1)S(1)}, bf16[4,128,256]{2,1,0:T(8,128)(2,1)S(1)}, u32[]{:S(2)}, u32[]{:S(2)}) collective-permute-start(bf16[4,128,256]{2,1,0:T(8,128)(2,1)S(1)} %convolution_convert_fusion.1), channel_id=1, source_target_pairs={{0,2},{1,3},{2,0},{3,1},{4,6},{5,7},{6,4},{7,5},{8,10},{9,11},{10,... | collective-permute-start | bytes 786440 | tf_op jit(solution)/shard_map/ppermute | solution.py:24
  63.9 6.6 %collective-permute-done.8 = bf16[4,128,256]{2,1,0:T(8,128)(2,1)S(1)} collective-permute-done((bf16[4,128,256]{2,1,0:T(8,128)(2,1)S(1)}, bf16[4,128,256]{2,1,0:T(8,128)(2,1)S(1)}, u32[]{:S(2)}, u32[]{:S(2)}) %collective-permute-start.8) | collective-permute-done | bytes 262176 | tf_op jit(solution)/shard_map/ppermute | solution.py:24
  70.5 4.8 %collective-permute-done.7 = bf16[4,128,256]{2,1,0:T(8,128)(2,1)S(1)} collective-permute-done((bf16[4,128,256]{2,1,0:T(8,128)(2,1)S(1)}, bf16[4,128,256]{2,1,0:T(8,128)(2,1)S(1)}, u32[]{:S(2)}, u32[]{:S(2)}) %collective-permute-start.7) | collective-permute-done | bytes 262176 | tf_op jit(solution)/shard_map/ppermute | solution.py:24
  75.6 3.7 %collective-permute-start.11 = (bf16[128,256]{1,0:T(8,128)(2,1)S(1)}, bf16[128,256]{1,0:T(8,128)(2,1)S(1)}, u32[]{:S(2)}, u32[]{:S(2)}) collective-permute-start(bf16[128,256]{1,0:T(8,128)(2,1)S(1)} %get-tuple-element.13), channel_id=1, source_target_pairs={{0,24},{1,25},{2,26},{3,27},{4,28},{5,29},{6,30},{7,31},{8,16},{9,... | collective-permute-start | bytes 196616 | tf_op jit(solution)/shard_map/ppermute | solution.py:24
  79.3 0.8 collective-permute-start.9
  80.0 2.1 %collective-permute-done.11 = bf16[128,256]{1,0:T(8,128)(2,1)S(1)} collective-permute-done((bf16[128,256]{1,0:T(8,128)(2,1)S(1)}, bf16[128,256]{1,0:T(8,128)(2,1)S(1)}, u32[]{:S(2)}, u32[]{:S(2)}) %collective-permute-start.11) | collective-permute-done | bytes 65568 | tf_op jit(solution)/shard_map/ppermute | solution.py:24
  82.1 2.9 %collective-permute-done.10 = bf16[128,256]{1,0:T(8,128)(2,1)S(1)} collective-permute-done((bf16[128,256]{1,0:T(8,128)(2,1)S(1)}, bf16[128,256]{1,0:T(8,128)(2,1)S(1)}, u32[]{:S(2)}, u32[]{:S(2)}) %collective-permute-start.10) | collective-permute-done | bytes 65568 | tf_op jit(solution)/shard_map/ppermute | solution.py:24
  85.1 0.8 divide_convert_fusion
  85.9 8.0 %all_gather.3 = bf16[512,256]{1,0:T(8,128)(2,1)S(1)} all-gather(bf16[128,256]{1,0:T(8,128)(2,1)S(1)} %get-tuple-element.9), channel_id=1, replica_groups=mesh['dp'=8,'fsdp'=4] {'fsdp'}, dimensions={0}, use_global_device_ids=true | all-gather | bytes 327680 | tf_op jit(solution)/shard_map/all_gather | solution.py:74
  93.8 0.7 fusion
  94.6 2.5 %copy.10 = bf16[2048,512]{1,0:T(8,128)(2,1)} copy(bf16[2048,512]{0,1:T(8,128)(2,1)S(1)} %fusion) | data formatting | bytes 4194304
  (42 shorter events, 3.5 us)
Async XLA Ops:
  0.6 1.2 %copy-start = (bf16[2048,256]{1,0:T(8,128)(2,1)S(1)}, bf16[2048,256]{1,0:T(8,128)(2,1)}, u32[]{:S(2)}) copy-start(bf16[2048,256]{1,0:T(8,128)(2,1)} %param.7) | copy-start | bytes 3145732
  0.6 51.6 %collective-permute-start.4 = (bf16[192,8192]{1,0:T(8,128)(2,1)}, bf16[192,8192]{1,0:T(8,128)(2,1)}, u32[]{:S(2)}, u32[]{:S(2)}) collective-permute-start(bf16[192,8192]{1,0:T(8,128)(2,1)} %param.5), channel_id=1, source_target_pairs={{0,4},{1,5},{2,6},{3,7},{4,0},{5,1},{6,2},{7,3},{8,12},{9,13},{10,... | collective-permute-start | bytes 9437192 | tf_op jit(solution)/shard_map/ppermute | solution.py:24
  1.2 31.1 %collective-permute-start = (bf16[192,4096]{1,0:T(8,128)(2,1)}, bf16[192,4096]{1,0:T(8,128)(2,1)}, u32[]{:S(2)}, u32[]{:S(2)}) collective-permute-start(bf16[192,4096]{1,0:T(8,128)(2,1)} %param.6), channel_id=1, source_target_pairs={{0,4},{1,5},{2,6},{3,7},{4,0},{5,1},{6,2},{7,3},{8,12},{9,13},{10,... | collective-permute-start | bytes 4718600 | tf_op jit(solution)/shard_map/ppermute | solution.py:24
  1.9 16.8 %collective-permute-start.3 = (bf16[1024,256]{1,0:T(8,128)(2,1)S(1)}, bf16[1024,256]{1,0:T(8,128)(2,1)S(1)}, u32[]{:S(2)}, u32[]{:S(2)}) collective-permute-start(bf16[1024,256]{1,0:T(8,128)(2,1)S(1)} %constant_dynamic-slice_fusion), channel_id=1, source_target_pairs={{0,3},{1,2},{2,1},{3,0},{4,7},{5,6},{6,5},{7,4},{8,11},{9,10},{10,... | collective-permute-start | bytes 1572872 | tf_op jit(solution)/shard_map/ppermute | solution.py:24
  5.9 24.9 %collective-permute-start.2 = (bf16[1024,256]{1,0:T(8,128)(2,1)S(1)}, bf16[1024,256]{1,0:T(8,128)(2,1)S(1)}, u32[]{:S(2)}, u32[]{:S(2)}) collective-permute-start(bf16[1024,256]{1,0:T(8,128)(2,1)S(1)} %constant_dynamic-slice_fusion), channel_id=1, source_target_pairs={{0,2},{1,3},{2,0},{3,1},{4,6},{5,7},{6,4},{7,5},{8,10},{9,11},{10,... | collective-permute-start | bytes 1572872 | tf_op jit(solution)/shard_map/ppermute | solution.py:24
  6.4 22.9 %collective-permute-start.1 = (bf16[1024,256]{1,0:T(8,128)(2,1)S(1)}, bf16[1024,256]{1,0:T(8,128)(2,1)S(1)}, u32[]{:S(2)}, u32[]{:S(2)}) collective-permute-start(bf16[1024,256]{1,0:T(8,128)(2,1)S(1)} %constant_dynamic-slice_fusion), channel_id=1, source_target_pairs={{0,1},{1,0},{2,3},{3,2},{4,5},{5,4},{6,7},{7,6},{8,9},{9,8},{10,11... | collective-permute-start | bytes 1572872 | tf_op jit(solution)/shard_map/ppermute | solution.py:24
  7.9 24.4 %copy-start.5 = (bf16[192,4096]{1,0:T(8,128)(2,1)S(1)}, bf16[192,4096]{1,0:T(8,128)(2,1)}, u32[]{:S(2)}) copy-start(bf16[192,4096]{1,0:T(8,128)(2,1)} %param.6) | copy-start | bytes 4718596
  18.7 17.1 %copy-start.3 = (bf16[1024,256]{1,0:T(8,128)(2,1)}, bf16[1024,256]{1,0:T(8,128)(2,1)S(1)}, u32[]{:S(2)}) copy-start(bf16[1024,256]{1,0:T(8,128)(2,1)S(1)} %collective-permute-done.3) | copy-start | bytes 1572868
  29.3 6.4 %copy-start.1 = (bf16[1024,256]{1,0:T(8,128)(2,1)}, bf16[1024,256]{1,0:T(8,128)(2,1)S(1)}, u32[]{:S(2)}) copy-start(bf16[1024,256]{1,0:T(8,128)(2,1)S(1)} %collective-permute-done.1) | copy-start | bytes 1572868
  30.8 5.0 %copy-start.4 = (bf16[1024,256]{1,0:T(8,128)(2,1)}, bf16[1024,256]{1,0:T(8,128)(2,1)S(1)}, u32[]{:S(2)}) copy-start(bf16[1024,256]{1,0:T(8,128)(2,1)S(1)} %collective-permute-done.2) | copy-start | bytes 1572868
  52.3 3.0 %copy-start.2 = (bf16[1024,256]{1,0:T(8,128)(2,1)S(1)}, bf16[1024,256]{1,0:T(8,128)(2,1)}, u32[]{:S(2)}) copy-start(bf16[1024,256]{1,0:T(8,128)(2,1)} %copy-done.1) | copy-start | bytes 1572868
  57.8 1.5 %collective-permute-start.5 = (bf16[384,256]{1,0:T(8,128)(2,1)S(1)}, bf16[384,256]{1,0:T(8,128)(2,1)S(1)}, u32[]{:S(2)}, u32[]{:S(2)}) collective-permute-start(bf16[384,256]{1,0:T(8,128)(2,1)S(1)} %fusion.18), channel_id=1, source_target_pairs={{0,4},{1,5},{2,6},{3,7},{4,0},{5,1},{6,2},{7,3},{8,12},{9,13},{10,... | collective-permute-start | bytes 589832 | tf_op jit(solution)/shard_map/ppermute | solution.py:24
  59.7 25.3 %copy-start.6 = (f32[128,256]{1,0:T(8,128)S(1)}, f32[128,256]{1,0:T(8,128)}, u32[]{:S(2)}) copy-start(f32[128,256]{1,0:T(8,128)} %param.8) | copy-start | bytes 393220
  59.7 25.3 %copy-start.7 = (f32[128,256]{1,0:T(8,128)S(1)}, f32[128,256]{1,0:T(8,128)}, u32[]{:S(2)}) copy-start(f32[128,256]{1,0:T(8,128)} %param.9) | copy-start | bytes 393220
  60.3 10.2 %collective-permute-start.8 = (bf16[4,128,256]{2,1,0:T(8,128)(2,1)S(1)}, bf16[4,128,256]{2,1,0:T(8,128)(2,1)S(1)}, u32[]{:S(2)}, u32[]{:S(2)}) collective-permute-start(bf16[4,128,256]{2,1,0:T(8,128)(2,1)S(1)} %convolution_convert_fusion), channel_id=1, source_target_pairs={{0,3},{1,2},{2,1},{3,0},{4,7},{5,6},{6,5},{7,4},{8,11},{9,10},{10,... | collective-permute-start | bytes 786440 | tf_op jit(solution)/shard_map/ppermute | solution.py:24
  61.8 13.4 %collective-permute-start.7 = (bf16[4,128,256]{2,1,0:T(8,128)(2,1)S(1)}, bf16[4,128,256]{2,1,0:T(8,128)(2,1)S(1)}, u32[]{:S(2)}, u32[]{:S(2)}) collective-permute-start(bf16[4,128,256]{2,1,0:T(8,128)(2,1)S(1)} %convolution_convert_fusion.1), channel_id=1, source_target_pairs={{0,2},{1,3},{2,0},{3,1},{4,6},{5,7},{6,4},{7,5},{8,10},{9,11},{10,... | collective-permute-start | bytes 786440 | tf_op jit(solution)/shard_map/ppermute | solution.py:24
  63.4 11.9 %collective-permute-start.6 = (bf16[4,128,256]{2,1,0:T(8,128)(2,1)S(1)}, bf16[4,128,256]{2,1,0:T(8,128)(2,1)S(1)}, u32[]{:S(2)}, u32[]{:S(2)}) collective-permute-start(bf16[4,128,256]{2,1,0:T(8,128)(2,1)S(1)} %convolution_convert_fusion.2), channel_id=1, source_target_pairs={{0,1},{1,0},{2,3},{3,2},{4,5},{5,4},{6,7},{7,6},{8,9},{9,8},{10,11... | collective-permute-start | bytes 786440 | tf_op jit(solution)/shard_map/ppermute | solution.py:24
  75.6 6.5 %collective-permute-start.11 = (bf16[128,256]{1,0:T(8,128)(2,1)S(1)}, bf16[128,256]{1,0:T(8,128)(2,1)S(1)}, u32[]{:S(2)}, u32[]{:S(2)}) collective-permute-start(bf16[128,256]{1,0:T(8,128)(2,1)S(1)} %get-tuple-element.13), channel_id=1, source_target_pairs={{0,24},{1,25},{2,26},{3,27},{4,28},{5,29},{6,30},{7,31},{8,16},{9,... | collective-permute-start | bytes 196616 | tf_op jit(solution)/shard_map/ppermute | solution.py:24
  79.3 5.8 %collective-permute-start.10 = (bf16[128,256]{1,0:T(8,128)(2,1)S(1)}, bf16[128,256]{1,0:T(8,128)(2,1)S(1)}, u32[]{:S(2)}, u32[]{:S(2)}) collective-permute-start(bf16[128,256]{1,0:T(8,128)(2,1)S(1)} %get-tuple-element.14), channel_id=1, source_target_pairs={{0,16},{1,17},{2,18},{3,19},{4,20},{5,21},{6,22},{7,23},{8,24},{9,... | collective-permute-start | bytes 196616 | tf_op jit(solution)/shard_map/ppermute | solution.py:24
  79.3 5.8 %collective-permute-start.9 = (bf16[128,256]{1,0:T(8,128)(2,1)S(1)}, bf16[128,256]{1,0:T(8,128)(2,1)S(1)}, u32[]{:S(2)}, u32[]{:S(2)}) collective-permute-start(bf16[128,256]{1,0:T(8,128)(2,1)S(1)} %get-tuple-element.12), channel_id=1, source_target_pairs={{0,8},{1,9},{2,10},{3,11},{4,12},{5,13},{6,14},{7,15},{8,0},{9,1},... | collective-permute-start | bytes 196616 | tf_op jit(solution)/shard_map/ppermute | solution.py:24

commit v2 on v1

v2 whole, which is shorter than its diff:
```python
import functools

import jax
import jax.numpy as jnp
from jax import lax
from jax.experimental import pallas as pl
from jax.experimental.pallas import tpu as pltpu
from jax.sharding import PartitionSpec as P

ADAM_STEP = 10
ANY = pl.BlockSpec(memory_space=pl.ANY)


def dot(a, b):
    return jnp.dot(a, b, preferred_element_type=jnp.float32)


def copy_all(copies):
    for copy in copies:
        copy.start()
    for copy in copies:
        copy.wait()


def halves_kernel(core, source, first, second, sem):
    half = first.shape[0]
    begins = (core[0] * half, (1 - core[0]) * half)
    copy_all(
        [
            pltpu.make_async_copy(source.at[pl.ds(pl.multiple_of(begin, 16), half), :], out, sem.at[i])
            for i, (begin, out) in enumerate(zip(begins, (first, second)))
        ]
    )


def halves_of(basis, core):
    half, rank = basis.shape[0] // 2, basis.shape[1]
    return pl.pallas_call(
        halves_kernel,
        out_shape=[pltpu.VMEM((half, rank), basis.dtype)] * 2,
        in_specs=[pl.BlockSpec(memory_space=pltpu.SMEM), ANY],
        out_specs=[pl.BlockSpec(memory_space=pltpu.VMEM)] * 2,
        scratch_shapes=[pltpu.SemaphoreType.DMA((2,))],
        name="halves",
    )(core.reshape(1), basis)


def pack_kernel(tokens, starts, own, other, *refs):
    outs, sem = refs[:-1], refs[-1]
    copies = []
    for index, out in enumerate(outs):
        columns = pl.ds(pl.multiple_of(starts[index], 128), out.shape[1])
        for side, source in enumerate((own, other)):
            copies.append(
                pltpu.make_async_copy(
                    source.at[:, columns], out.at[pl.ds(side * tokens, tokens), :], sem.at[2 * index + side]
                )
            )
    copy_all(copies)


def pack(own, other, starts, width):
    tokens, count = own.shape[0], len(starts)
    return pl.pallas_call(
        functools.partial(pack_kernel, tokens),
        out_shape=[pltpu.VMEM((2 * tokens, width), own.dtype)] * count,
        in_specs=[pl.BlockSpec(memory_space=pltpu.SMEM), ANY, ANY],
        out_specs=[pl.BlockSpec(memory_space=pltpu.VMEM)] * count,
        scratch_shapes=[pltpu.SemaphoreType.DMA((2 * count,))],
        name="pack_activations",
    )(jnp.stack(starts), own, other)


def turn_kernel(rows, order, own, other, out):
    for index in range(out.shape[0]):
        columns = pl.ds(pl.multiple_of(order[index] * rows, rows), rows)
        out[index] = jnp.concatenate([own[:, columns], other[:, columns]], axis=0).T


def turn(own, other, order, rows):
    tokens, count = own.shape[0], order.shape[0]
    if rows % 128 or tokens % 16:
        both = jnp.concatenate([own, other], axis=0).T
        return jnp.take(both.reshape(-1, rows, 2 * tokens), order, axis=0)
    return pl.pallas_call(
        functools.partial(turn_kernel, rows),
        out_shape=pltpu.VMEM((count, rows, 2 * tokens), own.dtype),
        in_specs=[pl.BlockSpec(memory_space=pltpu.SMEM)] + [pl.BlockSpec(memory_space=pltpu.VMEM)] * 2,
        out_specs=pl.BlockSpec(memory_space=pltpu.VMEM),
        name="turn_cotangent",
    )(order, own, other)


def update_kernel(basis, step, out):
    product = lax.dot_general(
        basis[...], step[...], (((1,), (1,)), ((), ())), preferred_element_type=jnp.float32
    )
    out[...] = (16.0 * product).astype(out.dtype)


def update_of(basis, step):
    depth, rank = basis.shape
    columns, tile = step.shape[0], depth // 4
    basis = pltpu.with_memory_space_constraint(basis, pltpu.VMEM)
    return pl.pallas_call(
        update_kernel,
        out_shape=jax.ShapeDtypeStruct((depth, columns), jnp.bfloat16),
        grid=(4,),
        in_specs=[
            pl.BlockSpec((tile, rank), lambda i: (i, 0)),
            pl.BlockSpec((columns, rank), lambda i: (0, 0)),
        ],
        out_specs=pl.BlockSpec((tile, columns), lambda i: (i, 0)),
        name="update",
    )(basis, step)


def solution(mesh):
    dp, fsdp = mesh.shape["dp"], mesh.shape["fsdp"]
    pairs = dp // 2

    def swap(value, across_pairs=0, across_fsdp=(0, 0), across_core=0):
        mask = across_pairs * 2 + across_core
        steps = [
            (d * fsdp + f, (d ^ mask) * fsdp + (f ^ across_fsdp[d % 2]))
            for d in range(dp)
            for f in range(fsdp)
        ]
        return lax.ppermute(value, ("dp", "fsdp"), steps)

    def local(activations, cotangent, basis, first_moment, second_moment):
        tokens, depth, rank = activations.shape[0], basis.shape[0], basis.shape[1]
        half, rows = depth // 2, first_moment.shape[0]
        mine, here = lax.axis_index("dp"), lax.axis_index("fsdp")
        core, pair = mine % 2, mine // 2

        part, rest = halves_of(basis, core)
        begin = core * half
        parts, starts = [part], [here * depth + begin]
        if fsdp == 4:
            near = here ^ (1 + core)
            parts.append(swap(part, across_fsdp=(1, 2)))
            parts.append(swap(rest, across_fsdp=(1, 2)))
            parts.append(swap(parts[1], across_fsdp=(2, 1)))
            starts += [near * depth + begin, near * depth + half - begin, (here ^ 3) * depth + begin]
        else:
            for k in range(1, fsdp):
                parts.append(swap(part, across_fsdp=(k, k)))
                starts.append((here ^ k) * depth + begin)

        shared = pack(activations, swap(activations, across_core=1), starts, half)
        order = (
            ((jnp.arange(pairs) ^ pair) * 2 + core)[:, None] * fsdp + (jnp.arange(fsdp) ^ here)[None, :]
        )
        order = order.reshape(2, pairs // 2, fsdp).swapaxes(1, 2).reshape(-1)
        features = turn(cotangent, swap(cotangent, across_core=1), order, rows)
        features = features.reshape(2, fsdp, pairs // 2 * rows, 2 * tokens)
        shared, features = lax.optimization_barrier((shared, features))

        projected = 0.0
        for block, piece in zip(shared, parts):
            projected += dot(block, piece)
        other = swap(projected.astype(jnp.bfloat16), across_core=1)
        other = jnp.concatenate([other[tokens:], other[:tokens]], axis=0)
        projected = (projected + other.astype(jnp.float32)).astype(jnp.bfloat16)

        def term(side, k):
            return dot(features[side, k], projected).reshape(pairs // 2, rows, rank)

        order = sorted(range(1, fsdp), key=lambda k: -bin(k).count("1"))
        arrived = {
            side: [swap(term(side, k).astype(jnp.bfloat16), across_fsdp=(k, k)) for k in order] for side in (1, 0)
        }
        arrivals, plane = [], {}
        for side in (1, 0):
            plane[side] = term(side, 0)
            for value in arrived[side]:
                plane[side] += value.astype(jnp.float32)
            for k in range(side * (pairs // 2), (side + 1) * (pairs // 2)):
                if k:
                    value = plane[side][k - side * (pairs // 2)].astype(jnp.bfloat16)
                    arrivals.append(swap(value, across_pairs=k))
        grad = plane[0][0]
        for value in arrivals:
            grad += value.astype(jnp.float32)

        new_first = 0.9 * first_moment + 0.1 * grad
        new_second = 0.999 * second_moment + 0.001 * grad * grad
        bias_one = 1.0 - 0.9**ADAM_STEP
        bias_two = 1.0 - 0.999**ADAM_STEP
        step = (new_first / bias_one / (jnp.sqrt(new_second / bias_two) + 1e-08)).astype(jnp.bfloat16)
        update = update_of(basis, lax.all_gather(step, "fsdp", axis=0, tiled=True))
        return (update, new_first, new_second)

    in_specs = (
        P(("dp", "fsdp"), None),
        P(("dp", "fsdp"), None),
        P("fsdp", None),
        P(("dp", "fsdp"), None),
        P(("dp", "fsdp"), None),
    )
    out_specs = (P("fsdp", "dp"), P(("dp", "fsdp"), None), P(("dp", "fsdp"), None))
    return jax.shard_map(local, mesh=mesh, in_specs=in_specs, out_specs=out_specs, check_vma=False)
```

time: 97.7 us -> 66.1 us (0.68)
  waiting for transfers between devices: 37.5 us -> 14.6 us
  local copies, waits for them, and re-layouts: 18.3 us -> 3.1 us
  Pallas kernels: 0 us -> 10.5 us
  matrix products: 13 us -> 7.53 us
  starting transfers between devices: 13.3 us -> 17.8 us
  other arithmetic: 6.02 us -> 1.72 us
  blocking collectives: 7.97 us -> 9.6 us
    ppermute x12 -> x15, waiting for transfers between devices: 37.5 us -> 14.6 us  [swap(): return lax.ppermute(value, ('dp', 'fsdp'), steps)]
    pallas_call x0 -> x4, Pallas kernels: none -> 10.5 us  [the longest x1 3.57 us: update_of(): pl.pallas_call(update_kernel, out_shape=jax.ShapeDtypeStruct((depth, colu...]
    reshape x1 -> x0, local copies, waits for them, and re-layouts: 6.08 us -> none  [local(): features = features.T.reshape(pairs, 2, fsdp, rows, 2 * tokens)]
    dot_general x12, matrix products: 12.3 us -> 7.53 us  [dot(): return jnp.dot(a, b, preferred_element_type=jnp.float32)]
    gather x2 -> x0, local copies, waits for them, and re-layouts: 4.6 us -> none  [the longest x1 2.3 us: local(): features = jnp.take(features, jnp.arange(pairs) ^ pair, axis=0)]
    ppermute x12 -> x15, starting transfers between devices: 13.3 us -> 17.8 us  [swap(): return lax.ppermute(value, ('dp', 'fsdp'), steps)]
    transpose x1 -> x0, other arithmetic: 3.45 us -> none  [local(): features = features.T.reshape(pairs, 2, fsdp, rows, 2 * tokens)]
    unnamed x18 -> x14, local copies, waits for them, and re-layouts: 5.64 us -> 2.31 us
  transfers between devices with their start and end apart: 12 -> 15, of which waited for: 7 -> 7; matrix products, arithmetic and copies ran while one was open for 27% -> 11% of each run, Pallas kernels for 0% -> 11%
where the time goes in v2:
time: 66.1 us; the launch traced here: 65.7 us
  starting transfers between devices  17.8 us (27%)
  waiting for transfers between devices  14.6 us (22%)
  Pallas kernels  10.5 us (16%)
  blocking collectives  9.6 us (15%)
  matrix products  7.53 us (11%)
  local copies, waits for them, and re-layouts  3.1 us (5%)
  other arithmetic  1.72 us (3%)
  between operations  0.87 us (1%)
    ppermute x15, starting transfers between devices, swap(): return lax.ppermute(value, ('dp', 'fsdp'), steps)  17.8 us
    ppermute x15, waiting for transfers between devices, swap(): return lax.ppermute(value, ('dp', 'fsdp'), steps)  14.6 us
    all_gather x1, blocking collectives, local(): update = update_of(basis, lax.all_gather(step, 'fsdp', axis=0, tiled=True))  9.6 us
    dot_general x12, matrix products, dot(): return jnp.dot(a, b, preferred_element_type=jnp.float32)  7.53 us
    pallas_call x1, Pallas kernels, update_of(): pl.pallas_call(update_kernel, out_shape=jax.ShapeDtypeStruct((depth, colu...  3.57 us
    pallas_call x1, Pallas kernels, pack(): pl.pallas_call(functools.partial(pack_kernel, tokens), out_shape=[pltpu.V...  2.57 us
    pallas_call x1, Pallas kernels, turn(): pl.pallas_call(functools.partial(turn_kernel, rows), out_shape=pltpu.VMEM...  2.36 us
    unnamed x14, local copies, waits for them, and re-layouts  2.31 us
  transfers between devices with their start and end apart: 15, of which 7 were waited for; matrix products, arithmetic and copies ran while one was open for 11% of the time, Pallas kernels for 11%

profile of v2, /device:TPU:0, one launch (start us, length us, event | category | flops | bytes accessed | tf_op | source)
XLA Modules:
  0.0 65.7 jit_solution(10801727554547252971)
XLA Ops:
  0.6 0.5 collective-permute-start
  1.2 2.0 %halves.1 = (bf16[1024,256]{1,0:T(8,128)(2,1)S(1)}, bf16[1024,256]{1,0:T(8,128)(2,1)}) custom-call(s32[1]{0:T(128)} %bitcast.6.core, bf16[2048,256]{1,0:T(8,128)(2,1)} %basis.1), custom_call_target="tpu_custom_call" | custom-call | tf_op jit(solution)/shard_map/halves/pallas_call | solution.py:38
  3.3 3.0 %collective-permute-start.2 = (bf16[1024,256]{1,0:T(8,128)(2,1)S(1)}, bf16[1024,256]{1,0:T(8,128)(2,1)}, u32[]{:S(2)}, u32[]{:S(2)}) collective-permute-start(bf16[1024,256]{1,0:T(8,128)(2,1)S(1)} %get-tuple-element.20), channel_id=1, source_target_pairs={{0,1},{1,0},{2,3},{3,2},{4,6},{5,7},{6,4},{7,5},{8,9},{9,8},{10,11... | collective-permute-start | bytes 1572872 | tf_op jit(solution)/shard_map/ppermute | solution.py:129
  6.4 0.6 add.108.order
  7.0 0.7 pad_add_fusion.starts
  7.7 5.8 %collective-permute-done.2 = bf16[1024,256]{1,0:T(8,128)(2,1)} collective-permute-done((bf16[1024,256]{1,0:T(8,128)(2,1)S(1)}, bf16[1024,256]{1,0:T(8,128)(2,1)}, u32[]{:S(2)}, u32[]{:S(2)}) %collective-permute-start.2) | collective-permute-done | bytes 524320 | tf_op jit(solution)/shard_map/ppermute | solution.py:129
  13.5 2.0 %collective-permute-start.4 = (bf16[1024,256]{1,0:T(8,128)(2,1)}, bf16[1024,256]{1,0:T(8,128)(2,1)}, u32[]{:S(2)}, u32[]{:S(2)}) collective-permute-start(bf16[1024,256]{1,0:T(8,128)(2,1)} %collective-permute-done.2), channel_id=1, source_target_pairs={{0,2},{1,3},{2,0},{3,1},{4,5},{5,4},{6,7},{7,6},{8,10},{9,11},{10,... | collective-permute-start | bytes 1572872 | tf_op jit(solution)/shard_map/ppermute | solution.py:129
  15.6 1.1 %copy-done.4 = bf16[192,4096]{1,0:T(8,128)(2,1)} copy-done((bf16[192,4096]{1,0:T(8,128)(2,1)}, bf16[192,4096]{1,0:T(8,128)(2,1)S(1)}, u32[]{:S(2)}) %copy-start.4) | copy-done | bytes 1572888
  16.7 2.4 %turn_cotangent.1 = bf16[16,128,384]{2,1,0:T(8,128)(2,1)S(1)} custom-call(s32[16]{0:T(128)} %add.108.order, bf16[192,4096]{1,0:T(8,128)(2,1)} %own.3, bf16[192,4096]{1,0:T(8,128)(2,1)} %copy-done.4), custom_call_target="tpu_custom_call" | custom-call | tf_op jit(solution)/shard_map/turn_cotangent/pallas_call | solution.py:85
  19.1 1.1 %copy-done = bf16[16,128,384]{2,1,0:T(8,128)(2,1)} copy-done((bf16[16,128,384]{2,1,0:T(8,128)(2,1)}, bf16[16,128,384]{2,1,0:T(8,128)(2,1)S(1)}, u32[]{:S(2)}) %copy-start) | copy-done | bytes 1572888
  20.2 2.6 %pack_activations.1 = (bf16[384,1024]{1,0:T(8,128)(2,1)S(1)}, bf16[384,1024]{1,0:T(8,128)(2,1)S(1)}, bf16[384,1024]{1,0:T(8,128)(2,1)S(1)}, bf16[384,1024]{1,0:T(8,128)(2,1)S(1)}) custom-call(s32[4]{0:T(128)} %pad_add_fusion.starts, bf16[192,8192]{1,0:T(8,128)(2,1)} %own.2, bf16[192,8192]{1,0:T(8,128)(2,1)} %collective-permute-done.other), custom_call_target="tpu_custom_call" | custom-call | tf_op jit(solution)/shard_map/pack_activations/pallas_call | solution.py:64
  22.8 1.4 %fusion.10 = f32[384,256]{1,0:T(8,128)S(1)} fusion(bf16[384,1024]{1,0:T(8,128)(2,1)S(1)} %get-tuple-element.19, bf16[1024,256]{1,0:T(8,128)(2,1)} %copy-done.3), kind=kOutput, calls=%fused_computation.32 | convolution fusion | flops 201326592 | bytes 1703936 | tf_op jit(solution)/shard_map/dot_general | solution.py:15
  24.2 1.4 %convolution_add_fusion.2 = f32[384,256]{1,0:T(8,128)S(1)} fusion(f32[384,256]{1,0:T(8,128)S(1)} %fusion.10, bf16[384,1024]{1,0:T(8,128)(2,1)S(1)} %get-tuple-element.21, bf16[1024,256]{1,0:T(8,128)(2,1)} %collective-permute-done.2), kind=kOutput, calls=%fused_computation.2 | convolution fusion | flops 201424896 | bytes 2097152 | tf_op jit(solution)/shard_map/dot_general | solution.py:15
  25.7 1.4 %convolution_add_fusion.1 = f32[384,256]{1,0:T(8,128)S(1)} fusion(f32[384,256]{1,0:T(8,128)S(1)} %convolution_add_fusion.2, bf16[384,1024]{1,0:T(8,128)(2,1)S(1)} %get-tuple-element.22, bf16[1024,256]{1,0:T(8,128)(2,1)} %collective-permute-done.3), kind=kOutput, calls=%fused_computation.1 | convolution fusion | flops 201424896 | bytes 2097152 | tf_op jit(solution)/shard_map/dot_general | solution.py:15
  27.1 1.5 %fusion.9 = (bf16[384,256]{1,0:T(8,128)(2,1)S(1)}, f32[384,256]{1,0:T(8,128)S(1)}) fusion(f32[384,256]{1,0:T(8,128)S(1)} %convolution_add_fusion.1, bf16[384,1024]{1,0:T(8,128)(2,1)S(1)} %get-tuple-element.24, bf16[1024,256]{1,0:T(8,128)(2,1)} %collective-permute-done.4), kind=kOutput, calls=%fused_computation.31 | convolution fusion | flops 201523200 | bytes 2293760 | tf_op jit(solution)/shard_map/dot_general | solution.py:15
  28.9 1.2 %collective-permute-done.5 = bf16[384,256]{1,0:T(8,128)(2,1)S(1)} collective-permute-done((bf16[384,256]{1,0:T(8,128)(2,1)S(1)}, bf16[384,256]{1,0:T(8,128)(2,1)S(1)}, u32[]{:S(2)}, u32[]{:S(2)}) %collective-permute-start.5) | collective-permute-done | bytes 196640 | tf_op jit(solution)/shard_map/ppermute | solution.py:129
  30.5 1.5 %collective-permute-start.9 = (bf16[2,128,256]{2,1,0:T(8,128)(2,1)S(1)}, bf16[2,128,256]{2,1,0:T(8,128)(2,1)S(1)}, u32[]{:S(2)}, u32[]{:S(2)}) collective-permute-start(bf16[2,128,256]{2,1,0:T(8,128)(2,1)S(1)} %convolution_convert_fusion.2), channel_id=1, source_target_pairs={{0,3},{1,2},{2,1},{3,0},{4,7},{5,6},{6,5},{7,4},{8,11},{9,10},{10,... | collective-permute-start | bytes 393224 | tf_op jit(solution)/shard_map/ppermute | solution.py:129
  32.8 2.0 %collective-permute-start.11 = (bf16[2,128,256]{2,1,0:T(8,128)(2,1)S(1)}, bf16[2,128,256]{2,1,0:T(8,128)(2,1)S(1)}, u32[]{:S(2)}, u32[]{:S(2)}) collective-permute-start(bf16[2,128,256]{2,1,0:T(8,128)(2,1)S(1)} %convolution_convert_fusion), channel_id=1, source_target_pairs={{0,2},{1,3},{2,0},{3,1},{4,6},{5,7},{6,4},{7,5},{8,10},{9,11},{10,... | collective-permute-start | bytes 393224 | tf_op jit(solution)/shard_map/ppermute | solution.py:129
  34.8 0.2 convolution_convert_fusion.5
  35.0 1.5 %collective-permute-start.6 = (bf16[2,128,256]{2,1,0:T(8,128)(2,1)S(1)}, bf16[2,128,256]{2,1,0:T(8,128)(2,1)S(1)}, u32[]{:S(2)}, u32[]{:S(2)}) collective-permute-start(bf16[2,128,256]{2,1,0:T(8,128)(2,1)S(1)} %convolution_convert_fusion.5), channel_id=1, source_target_pairs={{0,3},{1,2},{2,1},{3,0},{4,7},{5,6},{6,5},{7,4},{8,11},{9,10},{10,... | collective-permute-start | bytes 393224 | tf_op jit(solution)/shard_map/ppermute | solution.py:129
  37.4 0.3 collective-permute-done.9
  37.8 1.7 %collective-permute-start.8 = (bf16[2,128,256]{2,1,0:T(8,128)(2,1)S(1)}, bf16[2,128,256]{2,1,0:T(8,128)(2,1)S(1)}, u32[]{:S(2)}, u32[]{:S(2)}) collective-permute-start(bf16[2,128,256]{2,1,0:T(8,128)(2,1)S(1)} %convolution_convert_fusion.3), channel_id=1, source_target_pairs={{0,2},{1,3},{2,0},{3,1},{4,6},{5,7},{6,4},{7,5},{8,10},{9,11},{10,... | collective-permute-start | bytes 393224 | tf_op jit(solution)/shard_map/ppermute | solution.py:129
  39.5 2.5 %collective-permute-done.11 = bf16[2,128,256]{2,1,0:T(8,128)(2,1)S(1)} collective-permute-done((bf16[2,128,256]{2,1,0:T(8,128)(2,1)S(1)}, bf16[2,128,256]{2,1,0:T(8,128)(2,1)S(1)}, u32[]{:S(2)}, u32[]{:S(2)}) %collective-permute-start.11) | collective-permute-done | bytes 131104 | tf_op jit(solution)/shard_map/ppermute | solution.py:129
  42.1 3.2 %collective-permute-start.12 = (bf16[128,256]{1,0:T(8,128)(2,1)S(1)}, bf16[128,256]{1,0:T(8,128)(2,1)S(1)}, u32[]{:S(2)}, u32[]{:S(2)}) collective-permute-start(bf16[128,256]{1,0:T(8,128)(2,1)S(1)} %get-tuple-element.38), channel_id=1, source_target_pairs={{0,16},{1,17},{2,18},{3,19},{4,20},{5,21},{6,22},{7,23},{8,24},{9,... | collective-permute-start | bytes 196616 | tf_op jit(solution)/shard_map/ppermute | solution.py:129
  45.3 1.3 %collective-permute-start.13 = (bf16[128,256]{1,0:T(8,128)(2,1)S(1)}, bf16[128,256]{1,0:T(8,128)(2,1)S(1)}, u32[]{:S(2)}, u32[]{:S(2)}) collective-permute-start(bf16[128,256]{1,0:T(8,128)(2,1)S(1)} %get-tuple-element.39), channel_id=1, source_target_pairs={{0,24},{1,25},{2,26},{3,27},{4,28},{5,29},{6,30},{7,31},{8,16},{9,... | collective-permute-start | bytes 196616 | tf_op jit(solution)/shard_map/ppermute | solution.py:129
  46.7 0.4 collective-permute-start.14
  47.1 1.0 %collective-permute-done.12 = bf16[128,256]{1,0:T(8,128)(2,1)S(1)} collective-permute-done((bf16[128,256]{1,0:T(8,128)(2,1)S(1)}, bf16[128,256]{1,0:T(8,128)(2,1)S(1)}, u32[]{:S(2)}, u32[]{:S(2)}) %collective-permute-start.12) | collective-permute-done | bytes 65568 | tf_op jit(solution)/shard_map/ppermute | solution.py:129
  48.1 3.3 %collective-permute-done.13 = bf16[128,256]{1,0:T(8,128)(2,1)S(1)} collective-permute-done((bf16[128,256]{1,0:T(8,128)(2,1)S(1)}, bf16[128,256]{1,0:T(8,128)(2,1)S(1)}, u32[]{:S(2)}, u32[]{:S(2)}) %collective-permute-start.13) | collective-permute-done | bytes 65568 | tf_op jit(solution)/shard_map/ppermute | solution.py:129
  51.4 0.3 collective-permute-done.14
  51.7 0.8 %divide_convert_fusion = (bf16[128,256]{1,0:T(8,128)(2,1)S(1)}, f32[128,256]{1,0:T(8,128)}, f32[128,256]{1,0:T(8,128)}) fusion(bf16[128,256]{1,0:T(8,128)(2,1)S(1)} %collective-permute-done.14, bf16[128,256]{1,0:T(8,128)(2,1)S(1)} %collective-permute-done.13, bf16[128,256]{1,0:T(8,128)(2,1)S(1)} %collective-permute-done.12, ...), kind=kLoop, calls=%fused_computation.20 | loop fusion | flops 589824 | bytes 917504 | tf_op jit(solution)/shard_map/convert_element_type | solution.py:191
  52.5 9.6 %all_gather.3.step = bf16[512,256]{1,0:T(8,128)(2,1)} all-gather(bf16[128,256]{1,0:T(8,128)(2,1)S(1)} %get-tuple-element.25), channel_id=1, replica_groups=mesh['dp'=8,'fsdp'=4] {'fsdp'}, dimensions={0}, use_global_device_ids=true | all-gather | bytes 327680 | tf_op jit(solution)/shard_map/all_gather | solution.py:192
  62.2 3.6 %update.1 = bf16[2048,512]{1,0:T(8,128)(2,1)} custom-call(bf16[2048,256]{1,0:T(8,128)(2,1)S(1)} %copy-done.2, bf16[512,256]{1,0:T(8,128)(2,1)} %all_gather.3.step), custom_call_target="tpu_custom_call" | custom-call | tf_op jit(solution)/shard_map/update/pallas_call | solution.py:105
  (42 shorter events, 2.7 us)
Async XLA Ops:
  0.6 19.6 %collective-permute-start = (bf16[192,8192]{1,0:T(8,128)(2,1)}, bf16[192,8192]{1,0:T(8,128)(2,1)}, u32[]{:S(2)}, u32[]{:S(2)}) collective-permute-start(bf16[192,8192]{1,0:T(8,128)(2,1)} %own.2), channel_id=1, source_target_pairs={{0,4},{1,5},{2,6},{3,7},{4,0},{5,1},{6,2},{7,3},{8,12},{9,13},{10,... | collective-permute-start | bytes 9437192 | tf_op jit(solution)/shard_map/ppermute | solution.py:129
  1.1 14.4 %collective-permute-start.1 = (bf16[192,4096]{1,0:T(8,128)(2,1)}, bf16[192,4096]{1,0:T(8,128)(2,1)S(1)}, u32[]{:S(2)}, u32[]{:S(2)}) collective-permute-start(bf16[192,4096]{1,0:T(8,128)(2,1)} %own.3), channel_id=1, source_target_pairs={{0,4},{1,5},{2,6},{3,7},{4,0},{5,1},{6,2},{7,3},{8,12},{9,13},{10,... | collective-permute-start | bytes 4718600 | tf_op jit(solution)/shard_map/ppermute | solution.py:129
  3.3 12.3 %copy-start.3 = (bf16[1024,256]{1,0:T(8,128)(2,1)}, bf16[1024,256]{1,0:T(8,128)(2,1)S(1)}, u32[]{:S(2)}) copy-start(bf16[1024,256]{1,0:T(8,128)(2,1)S(1)} %get-tuple-element.20) | copy-start | bytes 1572868
  3.3 10.2 %collective-permute-start.2 = (bf16[1024,256]{1,0:T(8,128)(2,1)S(1)}, bf16[1024,256]{1,0:T(8,128)(2,1)}, u32[]{:S(2)}, u32[]{:S(2)}) collective-permute-start(bf16[1024,256]{1,0:T(8,128)(2,1)S(1)} %get-tuple-element.20), channel_id=1, source_target_pairs={{0,1},{1,0},{2,3},{3,2},{4,6},{5,7},{6,4},{7,5},{8,9},{9,8},{10,11... | collective-permute-start | bytes 1572872 | tf_op jit(solution)/shard_map/ppermute | solution.py:129
  6.3 19.4 %collective-permute-start.3 = (bf16[1024,256]{1,0:T(8,128)(2,1)}, bf16[1024,256]{1,0:T(8,128)(2,1)}, u32[]{:S(2)}, u32[]{:S(2)}) collective-permute-start(bf16[1024,256]{1,0:T(8,128)(2,1)} %get-tuple-element.23), channel_id=1, source_target_pairs={{0,1},{1,0},{2,3},{3,2},{4,6},{5,7},{6,4},{7,5},{8,9},{9,8},{10,11... | collective-permute-start | bytes 1572872 | tf_op jit(solution)/shard_map/ppermute | solution.py:129
  13.5 13.6 %collective-permute-start.4 = (bf16[1024,256]{1,0:T(8,128)(2,1)}, bf16[1024,256]{1,0:T(8,128)(2,1)}, u32[]{:S(2)}, u32[]{:S(2)}) collective-permute-start(bf16[1024,256]{1,0:T(8,128)(2,1)} %collective-permute-done.2), channel_id=1, source_target_pairs={{0,2},{1,3},{2,0},{3,1},{4,5},{5,4},{6,7},{7,6},{8,10},{9,11},{10,... | collective-permute-start | bytes 1572872 | tf_op jit(solution)/shard_map/ppermute | solution.py:129
  15.6 1.1 %copy-start.4 = (bf16[192,4096]{1,0:T(8,128)(2,1)}, bf16[192,4096]{1,0:T(8,128)(2,1)S(1)}, u32[]{:S(2)}) copy-start(bf16[192,4096]{1,0:T(8,128)(2,1)S(1)} %collective-permute-done.1.other) | copy-start | bytes 4718596
  19.1 1.1 %copy-start = (bf16[16,128,384]{2,1,0:T(8,128)(2,1)}, bf16[16,128,384]{2,1,0:T(8,128)(2,1)S(1)}, u32[]{:S(2)}) copy-start(bf16[16,128,384]{2,1,0:T(8,128)(2,1)S(1)} %turn_cotangent.1) | copy-start | bytes 4718596
  27.1 1.6 %copy-start.1 = (bf16[16,128,384]{2,1,0:T(8,128)(2,1)S(1)}, bf16[16,128,384]{2,1,0:T(8,128)(2,1)}, u32[]{:S(2)}) copy-start(bf16[16,128,384]{2,1,0:T(8,128)(2,1)} %copy-done) | copy-start | bytes 4718596
  28.6 1.5 %collective-permute-start.5 = (bf16[384,256]{1,0:T(8,128)(2,1)S(1)}, bf16[384,256]{1,0:T(8,128)(2,1)S(1)}, u32[]{:S(2)}, u32[]{:S(2)}) collective-permute-start(bf16[384,256]{1,0:T(8,128)(2,1)S(1)} %get-tuple-element.40), channel_id=1, source_target_pairs={{0,4},{1,5},{2,6},{3,7},{4,0},{5,1},{6,2},{7,3},{8,12},{9,13},{10,... | collective-permute-start | bytes 589832 | tf_op jit(solution)/shard_map/ppermute | solution.py:129
  30.5 7.3 %collective-permute-start.9 = (bf16[2,128,256]{2,1,0:T(8,128)(2,1)S(1)}, bf16[2,128,256]{2,1,0:T(8,128)(2,1)S(1)}, u32[]{:S(2)}, u32[]{:S(2)}) collective-permute-start(bf16[2,128,256]{2,1,0:T(8,128)(2,1)S(1)} %convolution_convert_fusion.2), channel_id=1, source_target_pairs={{0,3},{1,2},{2,1},{3,0},{4,7},{5,6},{6,5},{7,4},{8,11},{9,10},{10,... | collective-permute-start | bytes 393224 | tf_op jit(solution)/shard_map/ppermute | solution.py:129
  32.4 7.1 %collective-permute-start.10 = (bf16[2,128,256]{2,1,0:T(8,128)(2,1)S(1)}, bf16[2,128,256]{2,1,0:T(8,128)(2,1)S(1)}, u32[]{:S(2)}, u32[]{:S(2)}) collective-permute-start(bf16[2,128,256]{2,1,0:T(8,128)(2,1)S(1)} %convolution_convert_fusion.1), channel_id=1, source_target_pairs={{0,1},{1,0},{2,3},{3,2},{4,5},{5,4},{6,7},{7,6},{8,9},{9,8},{10,11... | collective-permute-start | bytes 393224 | tf_op jit(solution)/shard_map/ppermute | solution.py:129
  32.8 9.2 %collective-permute-start.11 = (bf16[2,128,256]{2,1,0:T(8,128)(2,1)S(1)}, bf16[2,128,256]{2,1,0:T(8,128)(2,1)S(1)}, u32[]{:S(2)}, u32[]{:S(2)}) collective-permute-start(bf16[2,128,256]{2,1,0:T(8,128)(2,1)S(1)} %convolution_convert_fusion), channel_id=1, source_target_pairs={{0,2},{1,3},{2,0},{3,1},{4,6},{5,7},{6,4},{7,5},{8,10},{9,11},{10,... | collective-permute-start | bytes 393224 | tf_op jit(solution)/shard_map/ppermute | solution.py:129
  35.0 11.6 %collective-permute-start.6 = (bf16[2,128,256]{2,1,0:T(8,128)(2,1)S(1)}, bf16[2,128,256]{2,1,0:T(8,128)(2,1)S(1)}, u32[]{:S(2)}, u32[]{:S(2)}) collective-permute-start(bf16[2,128,256]{2,1,0:T(8,128)(2,1)S(1)} %convolution_convert_fusion.5), channel_id=1, source_target_pairs={{0,3},{1,2},{2,1},{3,0},{4,7},{5,6},{6,5},{7,4},{8,11},{9,10},{10,... | collective-permute-start | bytes 393224 | tf_op jit(solution)/shard_map/ppermute | solution.py:129
  36.8 15.0 %copy-start.5 = (f32[128,256]{1,0:T(8,128)S(1)}, f32[128,256]{1,0:T(8,128)}, u32[]{:S(2)}) copy-start(f32[128,256]{1,0:T(8,128)} %param.8) | copy-start | bytes 393220
  36.8 15.0 %copy-start.6 = (f32[128,256]{1,0:T(8,128)S(1)}, f32[128,256]{1,0:T(8,128)}, u32[]{:S(2)}) copy-start(f32[128,256]{1,0:T(8,128)} %param.9) | copy-start | bytes 393220
  37.0 9.6 %collective-permute-start.7 = (bf16[2,128,256]{2,1,0:T(8,128)(2,1)S(1)}, bf16[2,128,256]{2,1,0:T(8,128)(2,1)S(1)}, u32[]{:S(2)}, u32[]{:S(2)}) collective-permute-start(bf16[2,128,256]{2,1,0:T(8,128)(2,1)S(1)} %convolution_convert_fusion.4), channel_id=1, source_target_pairs={{0,1},{1,0},{2,3},{3,2},{4,5},{5,4},{6,7},{7,6},{8,9},{9,8},{10,11... | collective-permute-start | bytes 393224 | tf_op jit(solution)/shard_map/ppermute | solution.py:129
  37.4 24.7 %copy-start.2 = (bf16[2048,256]{1,0:T(8,128)(2,1)S(1)}, bf16[2048,256]{1,0:T(8,128)(2,1)}, u32[]{:S(2)}) copy-start(bf16[2048,256]{1,0:T(8,128)(2,1)} %basis.1) | copy-start | bytes 3145732
  37.8 8.9 %collective-permute-start.8 = (bf16[2,128,256]{2,1,0:T(8,128)(2,1)S(1)}, bf16[2,128,256]{2,1,0:T(8,128)(2,1)S(1)}, u32[]{:S(2)}, u32[]{:S(2)}) collective-permute-start(bf16[2,128,256]{2,1,0:T(8,128)(2,1)S(1)} %convolution_convert_fusion.3), channel_id=1, source_target_pairs={{0,2},{1,3},{2,0},{3,1},{4,6},{5,7},{6,4},{7,5},{8,10},{9,11},{10,... | collective-permute-start | bytes 393224 | tf_op jit(solution)/shard_map/ppermute | solution.py:129
  42.1 6.0 %collective-permute-start.12 = (bf16[128,256]{1,0:T(8,128)(2,1)S(1)}, bf16[128,256]{1,0:T(8,128)(2,1)S(1)}, u32[]{:S(2)}, u32[]{:S(2)}) collective-permute-start(bf16[128,256]{1,0:T(8,128)(2,1)S(1)} %get-tuple-element.38), channel_id=1, source_target_pairs={{0,16},{1,17},{2,18},{3,19},{4,20},{5,21},{6,22},{7,23},{8,24},{9,... | collective-permute-start | bytes 196616 | tf_op jit(solution)/shard_map/ppermute | solution.py:129
  45.3 6.2 %collective-permute-start.13 = (bf16[128,256]{1,0:T(8,128)(2,1)S(1)}, bf16[128,256]{1,0:T(8,128)(2,1)S(1)}, u32[]{:S(2)}, u32[]{:S(2)}) collective-permute-start(bf16[128,256]{1,0:T(8,128)(2,1)S(1)} %get-tuple-element.39), channel_id=1, source_target_pairs={{0,24},{1,25},{2,26},{3,27},{4,28},{5,29},{6,30},{7,31},{8,16},{9,... | collective-permute-start | bytes 196616 | tf_op jit(solution)/shard_map/ppermute | solution.py:129
  46.7 5.0 %collective-permute-start.14 = (bf16[128,256]{1,0:T(8,128)(2,1)S(1)}, bf16[128,256]{1,0:T(8,128)(2,1)S(1)}, u32[]{:S(2)}, u32[]{:S(2)}) collective-permute-start(bf16[128,256]{1,0:T(8,128)(2,1)S(1)} %fusion.5), channel_id=1, source_target_pairs={{0,8},{1,9},{2,10},{3,11},{4,12},{5,13},{6,14},{7,15},{8,0},{9,1},... | collective-permute-start | bytes 196616 | tf_op jit(solution)/shard_map/ppermute | solution.py:129

commit v3 on v2

--- a/solution.py
+++ b/solution.py
@@ -9,6 +9,7 @@
 
 ADAM_STEP = 10
 ANY = pl.BlockSpec(memory_space=pl.ANY)
+SMALL = pltpu.CompilerParams(vmem_limit_bytes=8 * 2**20)
 
 
 def dot(a, b):
@@ -38,10 +39,11 @@
     return pl.pallas_call(
         halves_kernel,
         out_shape=[pltpu.VMEM((half, rank), basis.dtype)] * 2,
-        in_specs=[pl.BlockSpec(memory_space=pltpu.SMEM), ANY],
+        in_specs=[pl.BlockSpec(memory_space=pltpu.SMEM), pl.BlockSpec(memory_space=pltpu.HBM)],
         out_specs=[pl.BlockSpec(memory_space=pltpu.VMEM)] * 2,
         scratch_shapes=[pltpu.SemaphoreType.DMA((2,))],
         name="halves",
+        compiler_params=SMALL,
     )(core.reshape(1), basis)
 
 
@@ -68,6 +70,7 @@
         out_specs=[pl.BlockSpec(memory_space=pltpu.VMEM)] * count,
         scratch_shapes=[pltpu.SemaphoreType.DMA((2 * count,))],
         name="pack_activations",
+        compiler_params=SMALL,
     )(jnp.stack(starts), own, other)
 
 
@@ -88,31 +91,47 @@
         in_specs=[pl.BlockSpec(memory_space=pltpu.SMEM)] + [pl.BlockSpec(memory_space=pltpu.VMEM)] * 2,
         out_specs=pl.BlockSpec(memory_space=pltpu.VMEM),
         name="turn_cotangent",
+        compiler_params=SMALL,
     )(order, own, other)
 
 
-def update_kernel(basis, step, out):
-    product = lax.dot_general(
-        basis[...], step[...], (((1,), (1,)), ((), ())), preferred_element_type=jnp.float32
-    )
-    out[...] = (16.0 * product).astype(out.dtype)
-
-
-def update_of(basis, step):
-    depth, rank = basis.shape
-    columns, tile = step.shape[0], depth // 4
-    basis = pltpu.with_memory_space_constraint(basis, pltpu.VMEM)
-    return pl.pallas_call(
-        update_kernel,
-        out_shape=jax.ShapeDtypeStruct((depth, columns), jnp.bfloat16),
-        grid=(4,),
-        in_specs=[
-            pl.BlockSpec((tile, rank), lambda i: (i, 0)),
-            pl.BlockSpec((columns, rank), lambda i: (0, 0)),
+def update_kernel(tiles, here, basis, *refs):
+    steps, (out, held, sem) = refs[:-3], refs[-3:]
+    depth, rows = basis.shape[0], steps[0].shape[0]
+    tile, copies = depth // tiles, []
+    for mask, step in enumerate(steps):
+        columns = pl.ds(pl.multiple_of((here[0] ^ mask) * rows, rows), rows)
+        turned = step[...].T
+        for index in range(tiles):
+            part = pl.ds(index * tile, tile)
+            held[mask, part, :] = (16.0 * dot(basis[part, :], turned)).astype(out.dtype)
+            copies.append(
+                pltpu.make_async_copy(held.at[mask, part, :], out.at[part, columns], sem.at[mask * tiles + index])
+            )
+            copies[-1].start()
+    for copy in copies:
+        copy.wait()
+
+
+def update_of(basis, steps, here):
+    depth, (rows, rank) = basis.shape[0], steps[0].shape
+    if rows % 128:
+        step = jnp.take(jnp.stack(steps), jnp.arange(len(steps)) ^ here, axis=0).reshape(-1, rank)
+        return (16.0 * dot(basis, step.T)).astype(jnp.bfloat16)
+    tiles = 4
+    inputs = [pltpu.with_memory_space_constraint(value, pltpu.VMEM) for value in [basis] + steps]
+    return pl.pallas_call(
+        functools.partial(update_kernel, tiles),
+        out_shape=jax.ShapeDtypeStruct((depth, len(steps) * rows), jnp.bfloat16),
+        in_specs=[pl.BlockSpec(memory_space=pltpu.SMEM)] + [pl.BlockSpec(memory_space=pltpu.VMEM)] * len(inputs),
+        out_specs=ANY,
+        scratch_shapes=[
+            pltpu.VMEM((len(steps), depth, rows), jnp.bfloat16),
+            pltpu.SemaphoreType.DMA((len(steps) * tiles,)),
         ],
-        out_specs=pl.BlockSpec((tile, columns), lambda i: (i, 0)),
         name="update",
-    )(basis, step)
+        compiler_params=SMALL,
+    )(here.reshape(1), *inputs)
 
 
 def solution(mesh):
@@ -136,50 +155,52 @@
 
         part, rest = halves_of(basis, core)
         begin = core * half
-        parts, starts = [part], [here * depth + begin]
+        parts = [part]
         if fsdp == 4:
             near = here ^ (1 + core)
-            parts.append(swap(part, across_fsdp=(1, 2)))
-            parts.append(swap(rest, across_fsdp=(1, 2)))
+            parts += [swap(part, across_fsdp=(1, 2)), swap(rest, across_fsdp=(1, 2))]
+            starts = [here * depth + begin, near * depth + begin, near * depth + half - begin, (here ^ 3) * depth + begin]
+        else:
+            parts += [swap(part, across_fsdp=(k, k)) for k in range(1, fsdp)]
+            starts = [(here ^ k) * depth + begin for k in range(fsdp)]
+
+        shared = list(pack(activations, swap(activations, across_core=1), starts, half))
+        if fsdp == 4:
+            parts[1], shared[1] = lax.optimization_barrier((parts[1], shared[1]))
             parts.append(swap(parts[1], across_fsdp=(2, 1)))
-            starts += [near * depth + begin, near * depth + half - begin, (here ^ 3) * depth + begin]
-        else:
-            for k in range(1, fsdp):
-                parts.append(swap(part, across_fsdp=(k, k)))
-                starts.append((here ^ k) * depth + begin)
-
-        shared = pack(activations, swap(activations, across_core=1), starts, half)
-        order = (
+
+        owners = (
             ((jnp.arange(pairs) ^ pair) * 2 + core)[:, None] * fsdp + (jnp.arange(fsdp) ^ here)[None, :]
         )
-        order = order.reshape(2, pairs // 2, fsdp).swapaxes(1, 2).reshape(-1)
-        features = turn(cotangent, swap(cotangent, across_core=1), order, rows)
+        owners = owners.reshape(2, pairs // 2, fsdp).swapaxes(1, 2).reshape(-1)
+        features = turn(cotangent, swap(cotangent, across_core=1), owners, rows)
         features = features.reshape(2, fsdp, pairs // 2 * rows, 2 * tokens)
-        shared, features = lax.optimization_barrier((shared, features))
+        shared[0], features = lax.optimization_barrier((shared[0], features))
 
         projected = 0.0
         for block, piece in zip(shared, parts):
-            projected += dot(block, piece)
+            projected = lax.optimization_barrier(projected + dot(block, piece))
         other = swap(projected.astype(jnp.bfloat16), across_core=1)
         other = jnp.concatenate([other[tokens:], other[:tokens]], axis=0)
         projected = (projected + other.astype(jnp.float32)).astype(jnp.bfloat16)
 
-        def term(side, k):
-            return dot(features[side, k], projected).reshape(pairs // 2, rows, rank)
+        def term(side, k, value):
+            return dot(features[side, k].reshape(-1, 2 * tokens), value).reshape(pairs // 2, rows, rank)
 
         order = sorted(range(1, fsdp), key=lambda k: -bin(k).count("1"))
-        arrived = {
-            side: [swap(term(side, k).astype(jnp.bfloat16), across_fsdp=(k, k)) for k in order] for side in (1, 0)
-        }
-        arrivals, plane = [], {}
+        arrivals, arrived, plane, value = [], {}, {}, projected
         for side in (1, 0):
-            plane[side] = term(side, 0)
-            for value in arrived[side]:
-                plane[side] += value.astype(jnp.float32)
+            terms = [term(side, k, value).astype(jnp.bfloat16) for k in order]
+            arrived[side] = [swap(v, across_fsdp=(k, k)) for k, v in zip(order, terms)]
+            value, arrived[side][0] = lax.optimization_barrier((value, arrived[side][0]))
+        for side in (1, 0):
+            plane[side] = term(side, 0, projected)
+            for other in arrived[side]:
+                plane[side] += other.astype(jnp.float32)
             for k in range(side * (pairs // 2), (side + 1) * (pairs // 2)):
                 if k:
-                    value = plane[side][k - side * (pairs // 2)].astype(jnp.bfloat16)
-                    arrivals.append(swap(value, across_pairs=k))
+                    block = plane[side][k - side * (pairs // 2)].astype(jnp.bfloat16)
+                    arrivals.append(swap(block, across_pairs=k))
         grad = plane[0][0]
         for value in arrivals:
             grad += value.astype(jnp.float32)
@@ -189,7 +210,8 @@
         bias_one = 1.0 - 0.9**ADAM_STEP
         bias_two = 1.0 - 0.999**ADAM_STEP
         step = (new_first / bias_one / (jnp.sqrt(new_second / bias_two) + 1e-08)).astype(jnp.bfloat16)
-        update = update_of(basis, lax.all_gather(step, "fsdp", axis=0, tiled=True))
+        steps = {k: swap(step, across_fsdp=(k, k)) for k in order}
+        update = update_of(basis, [step] + [steps[k] for k in range(1, fsdp)], here)
         return (update, new_first, new_second)
 
     in_specs = (

time: 66.1 us -> 60.2 us (0.911)
  blocking collectives: 9.6 us -> 0 us
  starting transfers between devices: 17.8 us -> 23.2 us
  waiting for transfers between devices: 14.6 us -> 19.3 us
  Pallas kernels: 10.5 us -> 5.96 us
  matrix products: 7.53 us -> 6.4 us
    all_gather x1 -> x0, blocking collectives: 9.6 us -> none  [local(): update = update_of(basis, lax.all_gather(step, 'fsdp', axis=0, tiled=True))]
    ppermute x15 -> x18, starting transfers between devices: 17.8 us -> 23.2 us  [swap(): return lax.ppermute(value, ('dp', 'fsdp'), steps)]
    ppermute x15 -> x18, waiting for transfers between devices: 14.6 us -> 19.3 us  [swap(): return lax.ppermute(value, ('dp', 'fsdp'), steps)]
    pallas_call x1, Pallas kernels: 2.57 us -> 0.91 us  [pack(): pl.pallas_call(functools.partial(pack_kernel, tokens), out_shape=[pltpu.V...]
    pallas_call x1, Pallas kernels: 3.57 us -> 2.09 us  [update_of(): pl.pallas_call(functools.partial(update_kernel, tiles), out_shape=jax.Sha...]
    dot_general x12, matrix products: 7.53 us -> 6.4 us  [dot(): return jnp.dot(a, b, preferred_element_type=jnp.float32)]
    pallas_call x1, Pallas kernels: 2.02 us -> 1.07 us  [halves_of(): pl.pallas_call(halves_kernel, out_shape=[pltpu.VMEM((half, rank), basis.d...]
    unnamed x14 -> x12, local copies, waits for them, and re-layouts: 2.31 us -> 2.65 us
  transfers between devices with their start and end apart: 15 -> 18, of which waited for: 7 -> 11; matrix products, arithmetic and copies ran while one was open for 11% -> 11% of each run, Pallas kernels for 11% -> 6%
where the time goes in v3:
time: 60.2 us; the launch traced here: 59.9 us
  starting transfers between devices  23.2 us (39%)
  waiting for transfers between devices  19.3 us (32%)
  matrix products  6.4 us (11%)
  Pallas kernels  5.96 us (10%)
  local copies, waits for them, and re-layouts  2.93 us (5%)
  other arithmetic  1.26 us (2%)
  between operations  0.86 us (1%)
    ppermute x18, starting transfers between devices, swap(): return lax.ppermute(value, ('dp', 'fsdp'), steps)  23.2 us
    ppermute x18, waiting for transfers between devices, swap(): return lax.ppermute(value, ('dp', 'fsdp'), steps)  19.3 us
    dot_general x12, matrix products, dot(): return jnp.dot(a, b, preferred_element_type=jnp.float32)  6.4 us
    unnamed x12, local copies, waits for them, and re-layouts  2.65 us
    pallas_call x1, Pallas kernels, update_of(): pl.pallas_call(functools.partial(update_kernel, tiles), out_shape=jax.Sha...  2.09 us
    pallas_call x1, Pallas kernels, turn(): pl.pallas_call(functools.partial(turn_kernel, rows), out_shape=pltpu.VMEM...  1.88 us
  transfers between devices with their start and end apart: 18, of which 11 were waited for; matrix products, arithmetic and copies ran while one was open for 11% of the time, Pallas kernels for 6%

profile of v3, /device:TPU:0, one launch (start us, length us, event | category | flops | bytes accessed | tf_op | source)
XLA Modules:
  0.0 59.9 jit_solution(2930243191261176665)
XLA Ops:
  1.2 1.2 %copy-done = bf16[2048,256]{1,0:T(8,128)(2,1)S(1)} copy-done((bf16[2048,256]{1,0:T(8,128)(2,1)S(1)}, bf16[2048,256]{1,0:T(8,128)(2,1)}, u32[]{:S(2)}) %copy-start) | copy-done | bytes 1048600
  2.5 1.1 %halves.1 = (bf16[1024,256]{1,0:T(8,128)(2,1)}, bf16[1024,256]{1,0:T(8,128)(2,1)}) custom-call(s32[1]{0:T(128)} %bitcast.7.core, bf16[2048,256]{1,0:T(8,128)(2,1)S(1)} %copy-done), custom_call_target="tpu_custom_call" | custom-call | tf_op jit(solution)/shard_map/halves/pallas_call | solution.py:39
  3.5 3.0 %collective-permute-start.2 = (bf16[1024,256]{1,0:T(8,128)(2,1)}, bf16[1024,256]{1,0:T(8,128)(2,1)}, u32[]{:S(2)}, u32[]{:S(2)}) collective-permute-start(bf16[1024,256]{1,0:T(8,128)(2,1)} %get-tuple-element.19), channel_id=1, source_target_pairs={{0,1},{1,0},{2,3},{3,2},{4,6},{5,7},{6,4},{7,5},{8,9},{9,8},{10,11... | collective-permute-start | bytes 1572872 | tf_op jit(solution)/shard_map/ppermute | solution.py:148
  6.8 2.1 %collective-permute-done.1.other = bf16[192,4096]{1,0:T(8,128)(2,1)} collective-permute-done((bf16[192,4096]{1,0:T(8,128)(2,1)}, bf16[192,4096]{1,0:T(8,128)(2,1)}, u32[]{:S(2)}, u32[]{:S(2)}) %collective-permute-start.1) | collective-permute-done | bytes 1572896 | tf_op jit(solution)/shard_map/ppermute | solution.py:148
  8.9 1.4 %copy-done.3 = bf16[192,4096]{1,0:T(8,128)(2,1)S(1)} copy-done((bf16[192,4096]{1,0:T(8,128)(2,1)S(1)}, bf16[192,4096]{1,0:T(8,128)(2,1)}, u32[]{:S(2)}) %copy-start.3) | copy-done | bytes 1572888
  10.4 1.9 %turn_cotangent.1 = bf16[16,128,384]{2,1,0:T(8,128)(2,1)S(1)} custom-call(s32[16]{0:T(128)S(1)} %add.108.order, bf16[192,4096]{1,0:T(8,128)(2,1)S(1)} %copy-done.3, bf16[192,4096]{1,0:T(8,128)(2,1)} %collective-permute-done.1.other), custom_call_target="tpu_custom_call" | custom-call | tf_op jit(solution)/shard_map/turn_cotangent/pallas_call | solution.py:88
  12.3 0.9 %pack_activations.1 = (bf16[384,1024]{1,0:T(8,128)(2,1)S(1)}, bf16[384,1024]{1,0:T(8,128)(2,1)S(1)}, bf16[384,1024]{1,0:T(8,128)(2,1)S(1)}, bf16[384,1024]{1,0:T(8,128)(2,1)S(1)}) custom-call(s32[4]{0:T(128)S(1)} %pad_add_fusion.starts, bf16[192,8192]{1,0:T(8,128)(2,1)S(1)} %copy-done.2, bf16[192,8192]{1,0:T(8,128)(2,1)S(1)} %collective-permute-done.other), custom_call_target="tpu_custom_call" | custom-call | tf_op jit(solution)/shard_map/pack_activations/pallas_call | solution.py:66
  13.2 1.4 %fusion.18 = f32[384,256]{1,0:T(8,128)S(1)} fusion(bf16[384,1024]{1,0:T(8,128)(2,1)S(1)} %get-tuple-element.18, bf16[1024,256]{1,0:T(8,128)(2,1)} %get-tuple-element.19), kind=kOutput, calls=%fused_computation.39 | convolution fusion | flops 201326592 | bytes 1703936 | tf_op jit(solution)/shard_map/dot_general | solution.py:16
  14.6 2.7 %collective-permute-start.4 = (bf16[1024,256]{1,0:T(8,128)(2,1)}, bf16[1024,256]{1,0:T(8,128)(2,1)S(1)}, u32[]{:S(2)}, u32[]{:S(2)}) collective-permute-start(bf16[1024,256]{1,0:T(8,128)(2,1)} %collective-permute-done.2), channel_id=1, source_target_pairs={{0,2},{1,3},{2,0},{3,1},{4,5},{5,4},{6,7},{7,6},{8,10},{9,11},{10,... | collective-permute-start | bytes 1572872 | tf_op jit(solution)/shard_map/ppermute | solution.py:148
  17.3 1.4 %convolution_add_fusion.1 = f32[384,256]{1,0:T(8,128)S(1)} fusion(f32[384,256]{1,0:T(8,128)S(1)} %fusion.18, bf16[384,1024]{1,0:T(8,128)(2,1)S(1)} %get-tuple-element.21, bf16[1024,256]{1,0:T(8,128)(2,1)} %collective-permute-done.2), kind=kOutput, calls=%fused_computation.1 | convolution fusion | flops 201424896 | bytes 2097152 | tf_op jit(solution)/shard_map/dot_general | solution.py:16
  18.7 1.6 %collective-permute-done.3 = bf16[1024,256]{1,0:T(8,128)(2,1)} collective-permute-done((bf16[1024,256]{1,0:T(8,128)(2,1)}, bf16[1024,256]{1,0:T(8,128)(2,1)}, u32[]{:S(2)}, u32[]{:S(2)}) %collective-permute-start.3) | collective-permute-done | bytes 524320 | tf_op jit(solution)/shard_map/ppermute | solution.py:148
  20.4 1.4 %convolution_add_fusion = f32[384,256]{1,0:T(8,128)S(1)} fusion(f32[384,256]{1,0:T(8,128)S(1)} %convolution_add_fusion.1, bf16[384,1024]{1,0:T(8,128)(2,1)S(1)} %get-tuple-element.23, bf16[1024,256]{1,0:T(8,128)(2,1)} %collective-permute-done.3), kind=kOutput, calls=%fused_computation | convolution fusion | flops 201424896 | bytes 2097152 | tf_op jit(solution)/shard_map/dot_general | solution.py:16
  21.8 2.9 %collective-permute-done.4 = bf16[1024,256]{1,0:T(8,128)(2,1)S(1)} collective-permute-done((bf16[1024,256]{1,0:T(8,128)(2,1)}, bf16[1024,256]{1,0:T(8,128)(2,1)S(1)}, u32[]{:S(2)}, u32[]{:S(2)}) %collective-permute-start.4) | collective-permute-done | bytes 524320 | tf_op jit(solution)/shard_map/ppermute | solution.py:148
  25.6 1.0 %collective-permute-done.5 = bf16[384,256]{1,0:T(8,128)(2,1)S(1)} collective-permute-done((bf16[384,256]{1,0:T(8,128)(2,1)S(1)}, bf16[384,256]{1,0:T(8,128)(2,1)S(1)}, u32[]{:S(2)}, u32[]{:S(2)}) %collective-permute-start.5) | collective-permute-done | bytes 196640 | tf_op jit(solution)/shard_map/ppermute | solution.py:148
  26.9 3.0 %collective-permute-start.6 = (bf16[2,128,256]{2,1,0:T(8,128)(2,1)S(1)}, bf16[2,128,256]{2,1,0:T(8,128)(2,1)S(1)}, u32[]{:S(2)}, u32[]{:S(2)}) collective-permute-start(bf16[2,128,256]{2,1,0:T(8,128)(2,1)S(1)} %convolution_convert_fusion.5), channel_id=1, source_target_pairs={{0,3},{1,2},{2,1},{3,0},{4,7},{5,6},{6,5},{7,4},{8,11},{9,10},{10,... | collective-permute-start | bytes 393224 | tf_op jit(solution)/shard_map/ppermute | solution.py:148
  30.4 0.6 collective-permute-start.11
  31.6 2.5 %collective-permute-done.6 = bf16[2,128,256]{2,1,0:T(8,128)(2,1)S(1)} collective-permute-done((bf16[2,128,256]{2,1,0:T(8,128)(2,1)S(1)}, bf16[2,128,256]{2,1,0:T(8,128)(2,1)S(1)}, u32[]{:S(2)}, u32[]{:S(2)}) %collective-permute-start.6) | collective-permute-done | bytes 131104 | tf_op jit(solution)/shard_map/ppermute | solution.py:148
  34.2 2.2 %collective-permute-start.9 = (bf16[2,128,256]{2,1,0:T(8,128)(2,1)S(1)}, bf16[2,128,256]{2,1,0:T(8,128)(2,1)S(1)}, u32[]{:S(2)}, u32[]{:S(2)}) collective-permute-start(bf16[2,128,256]{2,1,0:T(8,128)(2,1)S(1)} %convolution_convert_fusion.2), channel_id=1, source_target_pairs={{0,2},{1,3},{2,0},{3,1},{4,6},{5,7},{6,4},{7,5},{8,10},{9,11},{10,... | collective-permute-start | bytes 393224 | tf_op jit(solution)/shard_map/ppermute | solution.py:148
  36.7 1.7 %collective-permute-start.8 = (bf16[2,128,256]{2,1,0:T(8,128)(2,1)S(1)}, bf16[2,128,256]{2,1,0:T(8,128)(2,1)S(1)}, u32[]{:S(2)}, u32[]{:S(2)}) collective-permute-start(bf16[2,128,256]{2,1,0:T(8,128)(2,1)S(1)} %convolution_convert_fusion.3), channel_id=1, source_target_pairs={{0,1},{1,0},{2,3},{3,2},{4,5},{5,4},{6,7},{7,6},{8,9},{9,8},{10,11... | collective-permute-start | bytes 393224 | tf_op jit(solution)/shard_map/ppermute | solution.py:148
  38.8 3.7 %collective-permute-start.13 = (bf16[128,256]{1,0:T(8,128)(2,1)S(1)}, bf16[128,256]{1,0:T(8,128)(2,1)S(1)}, u32[]{:S(2)}, u32[]{:S(2)}) collective-permute-start(bf16[128,256]{1,0:T(8,128)(2,1)S(1)} %get-tuple-element.43), channel_id=1, source_target_pairs={{0,24},{1,25},{2,26},{3,27},{4,28},{5,29},{6,30},{7,31},{8,16},{9,... | collective-permute-start | bytes 196616 | tf_op jit(solution)/shard_map/ppermute | solution.py:148
  42.5 2.1 %collective-permute-done.7 = bf16[2,128,256]{2,1,0:T(8,128)(2,1)S(1)} collective-permute-done((bf16[2,128,256]{2,1,0:T(8,128)(2,1)S(1)}, bf16[2,128,256]{2,1,0:T(8,128)(2,1)S(1)}, u32[]{:S(2)}, u32[]{:S(2)}) %collective-permute-start.7) | collective-permute-done | bytes 131104 | tf_op jit(solution)/shard_map/ppermute | solution.py:148
  44.6 1.6 %collective-permute-start.14 = (bf16[128,256]{1,0:T(8,128)(2,1)S(1)}, bf16[128,256]{1,0:T(8,128)(2,1)S(1)}, u32[]{:S(2)}, u32[]{:S(2)}) collective-permute-start(bf16[128,256]{1,0:T(8,128)(2,1)S(1)} %fusion.14), channel_id=1, source_target_pairs={{0,8},{1,9},{2,10},{3,11},{4,12},{5,13},{6,14},{7,15},{8,0},{9,1},... | collective-permute-start | bytes 196616 | tf_op jit(solution)/shard_map/ppermute | solution.py:148
  46.3 1.4 %collective-permute-done.12 = bf16[128,256]{1,0:T(8,128)(2,1)S(1)} collective-permute-done((bf16[128,256]{1,0:T(8,128)(2,1)S(1)}, bf16[128,256]{1,0:T(8,128)(2,1)S(1)}, u32[]{:S(2)}, u32[]{:S(2)}) %collective-permute-start.12) | collective-permute-done | bytes 65568 | tf_op jit(solution)/shard_map/ppermute | solution.py:148
  47.6 1.3 %collective-permute-done.14 = bf16[128,256]{1,0:T(8,128)(2,1)S(1)} collective-permute-done((bf16[128,256]{1,0:T(8,128)(2,1)S(1)}, bf16[128,256]{1,0:T(8,128)(2,1)S(1)}, u32[]{:S(2)}, u32[]{:S(2)}) %collective-permute-start.14) | collective-permute-done | bytes 65568 | tf_op jit(solution)/shard_map/ppermute | solution.py:148
  49.0 0.8 %divide_convert_fusion = (bf16[128,256]{1,0:T(8,128)(2,1)S(1)}, f32[128,256]{1,0:T(8,128)}, f32[128,256]{1,0:T(8,128)}) fusion(bf16[128,256]{1,0:T(8,128)(2,1)S(1)} %collective-permute-done.14, bf16[128,256]{1,0:T(8,128)(2,1)S(1)} %collective-permute-done.13, bf16[128,256]{1,0:T(8,128)(2,1)S(1)} %collective-permute-done.12, ...), kind=kLoop, calls=%fused_computation.28 | loop fusion | flops 589824 | bytes 917504 | tf_op jit(solution)/shard_map/convert_element_type | solution.py:212
  49.8 1.2 %collective-permute-start.15 = (bf16[128,256]{1,0:T(8,128)(2,1)S(1)}, bf16[128,256]{1,0:T(8,128)(2,1)S(1)}, u32[]{:S(2)}, u32[]{:S(2)}) collective-permute-start(bf16[128,256]{1,0:T(8,128)(2,1)S(1)} %get-tuple-element.29.refs_0_), channel_id=1, source_target_pairs={{0,1},{1,0},{2,3},{3,2},{4,5},{5,4},{6,7},{7,6},{8,9},{9,8},{10,11... | collective-permute-start | bytes 196616 | tf_op jit(solution)/shard_map/ppermute | solution.py:148
  51.0 1.6 %collective-permute-start.16 = (bf16[128,256]{1,0:T(8,128)(2,1)S(1)}, bf16[128,256]{1,0:T(8,128)(2,1)S(1)}, u32[]{:S(2)}, u32[]{:S(2)}) collective-permute-start(bf16[128,256]{1,0:T(8,128)(2,1)S(1)} %get-tuple-element.29.refs_0_), channel_id=1, source_target_pairs={{0,2},{1,3},{2,0},{3,1},{4,6},{5,7},{6,4},{7,5},{8,10},{9,11},{10,... | collective-permute-start | bytes 196616 | tf_op jit(solution)/shard_map/ppermute | solution.py:148
  52.6 0.6 %collective-permute-start.17 = (bf16[128,256]{1,0:T(8,128)(2,1)S(1)}, bf16[128,256]{1,0:T(8,128)(2,1)S(1)}, u32[]{:S(2)}, u32[]{:S(2)}) collective-permute-start(bf16[128,256]{1,0:T(8,128)(2,1)S(1)} %get-tuple-element.29.refs_0_), channel_id=1, source_target_pairs={{0,3},{1,2},{2,1},{3,0},{4,7},{5,6},{6,5},{7,4},{8,11},{9,10},{10,... | collective-permute-start | bytes 196616 | tf_op jit(solution)/shard_map/ppermute | solution.py:148
  53.3 0.8 %collective-permute-done.15.refs_1_ = bf16[128,256]{1,0:T(8,128)(2,1)S(1)} collective-permute-done((bf16[128,256]{1,0:T(8,128)(2,1)S(1)}, bf16[128,256]{1,0:T(8,128)(2,1)S(1)}, u32[]{:S(2)}, u32[]{:S(2)}) %collective-permute-start.15) | collective-permute-done | bytes 65568 | tf_op jit(solution)/shard_map/ppermute | solution.py:148
  54.1 1.2 %collective-permute-done.16.refs_2_ = bf16[128,256]{1,0:T(8,128)(2,1)S(1)} collective-permute-done((bf16[128,256]{1,0:T(8,128)(2,1)S(1)}, bf16[128,256]{1,0:T(8,128)(2,1)S(1)}, u32[]{:S(2)}, u32[]{:S(2)}) %collective-permute-start.16) | collective-permute-done | bytes 65568 | tf_op jit(solution)/shard_map/ppermute | solution.py:148
  55.3 2.5 %collective-permute-done.17.refs_3_ = bf16[128,256]{1,0:T(8,128)(2,1)S(1)} collective-permute-done((bf16[128,256]{1,0:T(8,128)(2,1)S(1)}, bf16[128,256]{1,0:T(8,128)(2,1)S(1)}, u32[]{:S(2)}, u32[]{:S(2)}) %collective-permute-start.17) | collective-permute-done | bytes 65568 | tf_op jit(solution)/shard_map/ppermute | solution.py:148
  57.8 2.1 %update.1 = bf16[2048,512]{1,0:T(8,128)(2,1)} custom-call(s32[1]{0:T(128)} %bitcast.here, bf16[2048,256]{1,0:T(8,128)(2,1)S(1)} %copy-done.1, bf16[128,256]{1,0:T(8,128)(2,1)S(1)} %get-tuple-element.29.refs_0_, bf16[128,256]{1,0:T(8,128)(2,1)S(1)} %collective-permute-done.15.refs_1_, bf16[128,256]{1,0:T(8,128)(2,1)S(1)} %collective-permute-done.16.refs_2_, ...), custom_call_target="tpu_custom_call" | custom-call | tf_op jit(solution)/shard_map/update/pallas_call | solution.py:123
  (47 shorter events, 4.1 us)
Async XLA Ops:
  0.6 11.6 %collective-permute-start = (bf16[192,8192]{1,0:T(8,128)(2,1)}, bf16[192,8192]{1,0:T(8,128)(2,1)S(1)}, u32[]{:S(2)}, u32[]{:S(2)}) collective-permute-start(bf16[192,8192]{1,0:T(8,128)(2,1)} %own.2), channel_id=1, source_target_pairs={{0,4},{1,5},{2,6},{3,7},{4,0},{5,1},{6,2},{7,3},{8,12},{9,13},{10,... | collective-permute-start | bytes 9437192 | tf_op jit(solution)/shard_map/ppermute | solution.py:148
  1.1 7.8 %collective-permute-start.1 = (bf16[192,4096]{1,0:T(8,128)(2,1)}, bf16[192,4096]{1,0:T(8,128)(2,1)}, u32[]{:S(2)}, u32[]{:S(2)}) collective-permute-start(bf16[192,4096]{1,0:T(8,128)(2,1)} %own.3), channel_id=1, source_target_pairs={{0,4},{1,5},{2,6},{3,7},{4,0},{5,1},{6,2},{7,3},{8,12},{9,13},{10,... | collective-permute-start | bytes 4718600 | tf_op jit(solution)/shard_map/ppermute | solution.py:148
  1.2 1.2 %copy-start = (bf16[2048,256]{1,0:T(8,128)(2,1)S(1)}, bf16[2048,256]{1,0:T(8,128)(2,1)}, u32[]{:S(2)}) copy-start(bf16[2048,256]{1,0:T(8,128)(2,1)} %basis.1) | copy-start | bytes 3145732
  3.5 11.1 %collective-permute-start.2 = (bf16[1024,256]{1,0:T(8,128)(2,1)}, bf16[1024,256]{1,0:T(8,128)(2,1)}, u32[]{:S(2)}, u32[]{:S(2)}) collective-permute-start(bf16[1024,256]{1,0:T(8,128)(2,1)} %get-tuple-element.19), channel_id=1, source_target_pairs={{0,1},{1,0},{2,3},{3,2},{4,6},{5,7},{6,4},{7,5},{8,9},{9,8},{10,11... | collective-permute-start | bytes 1572872 | tf_op jit(solution)/shard_map/ppermute | solution.py:148
  6.5 13.8 %collective-permute-start.3 = (bf16[1024,256]{1,0:T(8,128)(2,1)}, bf16[1024,256]{1,0:T(8,128)(2,1)}, u32[]{:S(2)}, u32[]{:S(2)}) collective-permute-start(bf16[1024,256]{1,0:T(8,128)(2,1)} %get-tuple-element.24), channel_id=1, source_target_pairs={{0,1},{1,0},{2,3},{3,2},{4,6},{5,7},{6,4},{7,5},{8,9},{9,8},{10,11... | collective-permute-start | bytes 1572872 | tf_op jit(solution)/shard_map/ppermute | solution.py:148
  6.8 5.4 %copy-start.2 = (bf16[192,8192]{1,0:T(8,128)(2,1)S(1)}, bf16[192,8192]{1,0:T(8,128)(2,1)}, u32[]{:S(2)}) copy-start(bf16[192,8192]{1,0:T(8,128)(2,1)} %own.2) | copy-start | bytes 9437188
  8.9 1.4 %copy-start.3 = (bf16[192,4096]{1,0:T(8,128)(2,1)S(1)}, bf16[192,4096]{1,0:T(8,128)(2,1)}, u32[]{:S(2)}) copy-start(bf16[192,4096]{1,0:T(8,128)(2,1)} %own.3) | copy-start | bytes 4718596
  14.6 10.0 %collective-permute-start.4 = (bf16[1024,256]{1,0:T(8,128)(2,1)}, bf16[1024,256]{1,0:T(8,128)(2,1)S(1)}, u32[]{:S(2)}, u32[]{:S(2)}) collective-permute-start(bf16[1024,256]{1,0:T(8,128)(2,1)} %collective-permute-done.2), channel_id=1, source_target_pairs={{0,2},{1,3},{2,0},{3,1},{4,5},{5,4},{6,7},{7,6},{8,10},{9,11},{10,... | collective-permute-start | bytes 1572872 | tf_op jit(solution)/shard_map/ppermute | solution.py:148
  25.1 1.5 %collective-permute-start.5 = (bf16[384,256]{1,0:T(8,128)(2,1)S(1)}, bf16[384,256]{1,0:T(8,128)(2,1)S(1)}, u32[]{:S(2)}, u32[]{:S(2)}) collective-permute-start(bf16[384,256]{1,0:T(8,128)(2,1)S(1)} %convert_element_type.69), channel_id=1, source_target_pairs={{0,4},{1,5},{2,6},{3,7},{4,0},{5,1},{6,2},{7,3},{8,12},{9,13},{10,... | collective-permute-start | bytes 589832 | tf_op jit(solution)/shard_map/ppermute | solution.py:148
  26.9 7.1 %collective-permute-start.6 = (bf16[2,128,256]{2,1,0:T(8,128)(2,1)S(1)}, bf16[2,128,256]{2,1,0:T(8,128)(2,1)S(1)}, u32[]{:S(2)}, u32[]{:S(2)}) collective-permute-start(bf16[2,128,256]{2,1,0:T(8,128)(2,1)S(1)} %convolution_convert_fusion.5), channel_id=1, source_target_pairs={{0,3},{1,2},{2,1},{3,0},{4,7},{5,6},{6,5},{7,4},{8,11},{9,10},{10,... | collective-permute-start | bytes 393224 | tf_op jit(solution)/shard_map/ppermute | solution.py:148
  30.4 8.3 %collective-permute-start.11 = (bf16[2,128,256]{2,1,0:T(8,128)(2,1)S(1)}, bf16[2,128,256]{2,1,0:T(8,128)(2,1)S(1)}, u32[]{:S(2)}, u32[]{:S(2)}) collective-permute-start(bf16[2,128,256]{2,1,0:T(8,128)(2,1)S(1)} %convolution_convert_fusion), channel_id=1, source_target_pairs={{0,2},{1,3},{2,0},{3,1},{4,6},{5,7},{6,4},{7,5},{8,10},{9,11},{10,... | collective-permute-start | bytes 393224 | tf_op jit(solution)/shard_map/ppermute | solution.py:148
  31.2 7.5 %collective-permute-start.10 = (bf16[2,128,256]{2,1,0:T(8,128)(2,1)S(1)}, bf16[2,128,256]{2,1,0:T(8,128)(2,1)S(1)}, u32[]{:S(2)}, u32[]{:S(2)}) collective-permute-start(bf16[2,128,256]{2,1,0:T(8,128)(2,1)S(1)} %convolution_convert_fusion.1), channel_id=1, source_target_pairs={{0,1},{1,0},{2,3},{3,2},{4,5},{5,4},{6,7},{7,6},{8,9},{9,8},{10,11... | collective-permute-start | bytes 393224 | tf_op jit(solution)/shard_map/ppermute | solution.py:148
  34.2 10.3 %collective-permute-start.9 = (bf16[2,128,256]{2,1,0:T(8,128)(2,1)S(1)}, bf16[2,128,256]{2,1,0:T(8,128)(2,1)S(1)}, u32[]{:S(2)}, u32[]{:S(2)}) collective-permute-start(bf16[2,128,256]{2,1,0:T(8,128)(2,1)S(1)} %convolution_convert_fusion.2), channel_id=1, source_target_pairs={{0,2},{1,3},{2,0},{3,1},{4,6},{5,7},{6,4},{7,5},{8,10},{9,11},{10,... | collective-permute-start | bytes 393224 | tf_op jit(solution)/shard_map/ppermute | solution.py:148
  36.4 12.5 %copy-start.4 = (f32[128,256]{1,0:T(8,128)S(1)}, f32[128,256]{1,0:T(8,128)}, u32[]{:S(2)}) copy-start(f32[128,256]{1,0:T(8,128)} %param.8) | copy-start | bytes 393220
  36.4 12.5 %copy-start.5 = (f32[128,256]{1,0:T(8,128)S(1)}, f32[128,256]{1,0:T(8,128)}, u32[]{:S(2)}) copy-start(f32[128,256]{1,0:T(8,128)} %param.9) | copy-start | bytes 393220
  36.7 7.9 %collective-permute-start.8 = (bf16[2,128,256]{2,1,0:T(8,128)(2,1)S(1)}, bf16[2,128,256]{2,1,0:T(8,128)(2,1)S(1)}, u32[]{:S(2)}, u32[]{:S(2)}) collective-permute-start(bf16[2,128,256]{2,1,0:T(8,128)(2,1)S(1)} %convolution_convert_fusion.3), channel_id=1, source_target_pairs={{0,1},{1,0},{2,3},{3,2},{4,5},{5,4},{6,7},{7,6},{8,9},{9,8},{10,11... | collective-permute-start | bytes 393224 | tf_op jit(solution)/shard_map/ppermute | solution.py:148
  38.6 19.2 %copy-start.1 = (bf16[2048,256]{1,0:T(8,128)(2,1)S(1)}, bf16[2048,256]{1,0:T(8,128)(2,1)}, u32[]{:S(2)}) copy-start(bf16[2048,256]{1,0:T(8,128)(2,1)} %basis.1) | copy-start | bytes 3145732
  38.6 5.9 %collective-permute-start.7 = (bf16[2,128,256]{2,1,0:T(8,128)(2,1)S(1)}, bf16[2,128,256]{2,1,0:T(8,128)(2,1)S(1)}, u32[]{:S(2)}, u32[]{:S(2)}) collective-permute-start(bf16[2,128,256]{2,1,0:T(8,128)(2,1)S(1)} %convolution_convert_fusion.4), channel_id=1, source_target_pairs={{0,3},{1,2},{2,1},{3,0},{4,7},{5,6},{6,5},{7,4},{8,11},{9,10},{10,... | collective-permute-start | bytes 393224 | tf_op jit(solution)/shard_map/ppermute | solution.py:148
  38.8 7.5 %collective-permute-start.13 = (bf16[128,256]{1,0:T(8,128)(2,1)S(1)}, bf16[128,256]{1,0:T(8,128)(2,1)S(1)}, u32[]{:S(2)}, u32[]{:S(2)}) collective-permute-start(bf16[128,256]{1,0:T(8,128)(2,1)S(1)} %get-tuple-element.43), channel_id=1, source_target_pairs={{0,24},{1,25},{2,26},{3,27},{4,28},{5,29},{6,30},{7,31},{8,16},{9,... | collective-permute-start | bytes 196616 | tf_op jit(solution)/shard_map/ppermute | solution.py:148
  42.5 5.2 %collective-permute-start.12 = (bf16[128,256]{1,0:T(8,128)(2,1)S(1)}, bf16[128,256]{1,0:T(8,128)(2,1)S(1)}, u32[]{:S(2)}, u32[]{:S(2)}) collective-permute-start(bf16[128,256]{1,0:T(8,128)(2,1)S(1)} %get-tuple-element.42), channel_id=1, source_target_pairs={{0,16},{1,17},{2,18},{3,19},{4,20},{5,21},{6,22},{7,23},{8,24},{9,... | collective-permute-start | bytes 196616 | tf_op jit(solution)/shard_map/ppermute | solution.py:148
  44.6 4.3 %collective-permute-start.14 = (bf16[128,256]{1,0:T(8,128)(2,1)S(1)}, bf16[128,256]{1,0:T(8,128)(2,1)S(1)}, u32[]{:S(2)}, u32[]{:S(2)}) collective-permute-start(bf16[128,256]{1,0:T(8,128)(2,1)S(1)} %fusion.14), channel_id=1, source_target_pairs={{0,8},{1,9},{2,10},{3,11},{4,12},{5,13},{6,14},{7,15},{8,0},{9,1},... | collective-permute-start | bytes 196616 | tf_op jit(solution)/shard_map/ppermute | solution.py:148
  49.8 4.3 %collective-permute-start.15 = (bf16[128,256]{1,0:T(8,128)(2,1)S(1)}, bf16[128,256]{1,0:T(8,128)(2,1)S(1)}, u32[]{:S(2)}, u32[]{:S(2)}) collective-permute-start(bf16[128,256]{1,0:T(8,128)(2,1)S(1)} %get-tuple-element.29.refs_0_), channel_id=1, source_target_pairs={{0,1},{1,0},{2,3},{3,2},{4,5},{5,4},{6,7},{7,6},{8,9},{9,8},{10,11... | collective-permute-start | bytes 196616 | tf_op jit(solution)/shard_map/ppermute | solution.py:148
  51.0 4.3 %collective-permute-start.16 = (bf16[128,256]{1,0:T(8,128)(2,1)S(1)}, bf16[128,256]{1,0:T(8,128)(2,1)S(1)}, u32[]{:S(2)}, u32[]{:S(2)}) collective-permute-start(bf16[128,256]{1,0:T(8,128)(2,1)S(1)} %get-tuple-element.29.refs_0_), channel_id=1, source_target_pairs={{0,2},{1,3},{2,0},{3,1},{4,6},{5,7},{6,4},{7,5},{8,10},{9,11},{10,... | collective-permute-start | bytes 196616 | tf_op jit(solution)/shard_map/ppermute | solution.py:148
  52.6 5.2 %collective-permute-start.17 = (bf16[128,256]{1,0:T(8,128)(2,1)S(1)}, bf16[128,256]{1,0:T(8,128)(2,1)S(1)}, u32[]{:S(2)}, u32[]{:S(2)}) collective-permute-start(bf16[128,256]{1,0:T(8,128)(2,1)S(1)} %get-tuple-element.29.refs_0_), channel_id=1, source_target_pairs={{0,3},{1,2},{2,1},{3,0},{4,7},{5,6},{6,5},{7,4},{8,11},{9,10},{10,... | collective-permute-start | bytes 196616 | tf_op jit(solution)/shard_map/ppermute | solution.py:148

commit v4 on v3

--- a/solution.py
+++ b/solution.py
@@ -21,30 +21,6 @@
         copy.start()
     for copy in copies:
         copy.wait()
-
-
-def halves_kernel(core, source, first, second, sem):
-    half = first.shape[0]
-    begins = (core[0] * half, (1 - core[0]) * half)
-    copy_all(
-        [
-            pltpu.make_async_copy(source.at[pl.ds(pl.multiple_of(begin, 16), half), :], out, sem.at[i])
-            for i, (begin, out) in enumerate(zip(begins, (first, second)))
-        ]
-    )
-
-
-def halves_of(basis, core):
-    half, rank = basis.shape[0] // 2, basis.shape[1]
-    return pl.pallas_call(
-        halves_kernel,
-        out_shape=[pltpu.VMEM((half, rank), basis.dtype)] * 2,
-        in_specs=[pl.BlockSpec(memory_space=pltpu.SMEM), pl.BlockSpec(memory_space=pltpu.HBM)],
-        out_specs=[pl.BlockSpec(memory_space=pltpu.VMEM)] * 2,
-        scratch_shapes=[pltpu.SemaphoreType.DMA((2,))],
-        name="halves",
-        compiler_params=SMALL,
-    )(core.reshape(1), basis)
 
 
 def pack_kernel(tokens, starts, own, other, *refs):
@@ -95,43 +71,47 @@
     )(order, own, other)
 
 
-def update_kernel(tiles, here, basis, *refs):
-    steps, (out, held, sem) = refs[:-3], refs[-3:]
-    depth, rows = basis.shape[0], steps[0].shape[0]
-    tile, copies = depth // tiles, []
-    for mask, step in enumerate(steps):
-        columns = pl.ds(pl.multiple_of((here[0] ^ mask) * rows, rows), rows)
-        turned = step[...].T
+def update_kernel(tiles, masks, place, first, second, *refs):
+    steps, (out, step, held, sem) = refs[:-4], refs[-4:]
+    half, rows = first.shape[0], steps[0].shape[0]
+    for mask, block in zip(masks, steps):
+        step[pl.ds(pl.multiple_of((place[0] ^ mask) * rows, rows), rows), :] = block[...]
+    turned, tile, copies = step[...].T, half // tiles, []
+    for side, basis in enumerate((first, second)):
         for index in range(tiles):
             part = pl.ds(index * tile, tile)
-            held[mask, part, :] = (16.0 * dot(basis[part, :], turned)).astype(out.dtype)
+            held[side, part, :] = (16.0 * dot(basis[part, :], turned)).astype(out.dtype)
+            begin = pl.multiple_of((place[1] ^ side) * half + index * tile, tile)
             copies.append(
-                pltpu.make_async_copy(held.at[mask, part, :], out.at[part, columns], sem.at[mask * tiles + index])
+                pltpu.make_async_copy(held.at[side, part, :], out.at[pl.ds(begin, tile), :], sem.at[len(copies)])
             )
             copies[-1].start()
     for copy in copies:
         copy.wait()
 
 
-def update_of(basis, steps, here):
-    depth, (rows, rank) = basis.shape[0], steps[0].shape
+def update_of(first, second, steps, masks, here, core):
+    half, (rows, rank) = first.shape[0], steps[0].shape
     if rows % 128:
-        step = jnp.take(jnp.stack(steps), jnp.arange(len(steps)) ^ here, axis=0).reshape(-1, rank)
+        step = jnp.zeros((len(steps), rows, rank), jnp.bfloat16)
+        step = step.at[jnp.array(masks) ^ here].set(jnp.stack(steps)).reshape(-1, rank)
+        basis = jnp.where(core == 0, jnp.concatenate([first, second]), jnp.concatenate([second, first]))
         return (16.0 * dot(basis, step.T)).astype(jnp.bfloat16)
     tiles = 4
-    inputs = [pltpu.with_memory_space_constraint(value, pltpu.VMEM) for value in [basis] + steps]
+    inputs = [pltpu.with_memory_space_constraint(value, pltpu.VMEM) for value in [first, second] + steps]
     return pl.pallas_call(
-        functools.partial(update_kernel, tiles),
-        out_shape=jax.ShapeDtypeStruct((depth, len(steps) * rows), jnp.bfloat16),
+        functools.partial(update_kernel, tiles, masks),
+        out_shape=jax.ShapeDtypeStruct((2 * half, len(steps) * rows), jnp.bfloat16),
         in_specs=[pl.BlockSpec(memory_space=pltpu.SMEM)] + [pl.BlockSpec(memory_space=pltpu.VMEM)] * len(inputs),
         out_specs=ANY,
         scratch_shapes=[
-            pltpu.VMEM((len(steps), depth, rows), jnp.bfloat16),
-            pltpu.SemaphoreType.DMA((len(steps) * tiles,)),
+            pltpu.VMEM((len(steps) * rows, rank), jnp.bfloat16),
+            pltpu.VMEM((2, half, len(steps) * rows), jnp.bfloat16),
+            pltpu.SemaphoreType.DMA((2 * tiles,)),
         ],
         name="update",
         compiler_params=SMALL,
-    )(here.reshape(1), *inputs)
+    )(jnp.stack([here, core]), *inputs)
 
 
 def solution(mesh):
@@ -153,8 +133,8 @@
         mine, here = lax.axis_index("dp"), lax.axis_index("fsdp")
         core, pair = mine % 2, mine // 2
 
-        part, rest = halves_of(basis, core)
         begin = core * half
+        part, rest = (lax.dynamic_slice(basis, (at, 0), (half, rank)) for at in (begin, half - begin))
         parts = [part]
         if fsdp == 4:
             near = here ^ (1 + core)
@@ -187,20 +167,19 @@
         def term(side, k, value):
             return dot(features[side, k].reshape(-1, 2 * tokens), value).reshape(pairs // 2, rows, rank)
 
-        order = sorted(range(1, fsdp), key=lambda k: -bin(k).count("1"))
+        masks, middle = range(fsdp - 1, 0, -1), pairs // 2
         arrivals, arrived, plane, value = [], {}, {}, projected
         for side in (1, 0):
-            terms = [term(side, k, value).astype(jnp.bfloat16) for k in order]
-            arrived[side] = [swap(v, across_fsdp=(k, k)) for k, v in zip(order, terms)]
-            value, arrived[side][0] = lax.optimization_barrier((value, arrived[side][0]))
+            terms = {k: term(side, k, value).astype(jnp.bfloat16) for k in masks}
+            arrived[side] = {k: swap(v, across_fsdp=(k, k)) for k, v in terms.items()}
+            value, arrived[side][1] = lax.optimization_barrier((value, arrived[side][1]))
         for side in (1, 0):
             plane[side] = term(side, 0, projected)
-            for other in arrived[side]:
-                plane[side] += other.astype(jnp.float32)
-            for k in range(side * (pairs // 2), (side + 1) * (pairs // 2)):
-                if k:
-                    block = plane[side][k - side * (pairs // 2)].astype(jnp.bfloat16)
-                    arrivals.append(swap(block, across_pairs=k))
+            for k in masks:
+                plane[side] += arrived[side][k].astype(jnp.float32)
+        for k in [middle] + [k for k in range(1, pairs) if k != middle]:
+            block = plane[k // middle][k % middle].astype(jnp.bfloat16)
+            arrivals.append(swap(block, across_pairs=k))
         grad = plane[0][0]
         for value in arrivals:
             grad += value.astype(jnp.float32)
@@ -210,8 +189,8 @@
         bias_one = 1.0 - 0.9**ADAM_STEP
         bias_two = 1.0 - 0.999**ADAM_STEP
         step = (new_first / bias_one / (jnp.sqrt(new_second / bias_two) + 1e-08)).astype(jnp.bfloat16)
-        steps = {k: swap(step, across_fsdp=(k, k)) for k in order}
-        update = update_of(basis, [step] + [steps[k] for k in range(1, fsdp)], here)
+        steps = {k: swap(step, across_fsdp=(k, k)) for k in range(1, fsdp)}
+        update = update_of(part, rest, [step] + [steps[k] for k in masks], [0, *masks], here, core)
         return (update, new_first, new_second)
 
     in_specs = (

time: 60.2 us -> 56.9 us (0.945)
  matrix products: 6.4 us -> 4.29 us
  local copies, waits for them, and re-layouts: 2.93 us -> 1.56 us
    unnamed x12 -> x8, local copies, waits for them, and re-layouts: 2.65 us -> 0.02 us
    dot_general x12, matrix products: 6.4 us -> 4.29 us  [dot(): return jnp.dot(a, b, preferred_element_type=jnp.float32)]
    dynamic_slice x0 -> x1, local copies, waits for them, and re-layouts: none -> 1.27 us  [local(): lax.dynamic_slice(basis, (at, 0), (half, rank))]
    pallas_call x1, Pallas kernels: 0.91 us -> 2.03 us  [pack(): pl.pallas_call(functools.partial(pack_kernel, tokens), out_shape=[pltpu.V...]
    pallas_call x2 -> x1, Pallas kernels: 3.17 us -> 2.2 us  [update_of(): pl.pallas_call(functools.partial(update_kernel, tiles, masks), out_shape=...]
  transfers between devices with their start and end apart: 18 -> 18, of which waited for: 11 -> 12; matrix products, arithmetic and copies ran while one was open for 11% -> 10% of each run, Pallas kernels for 6% -> 7%
where the time goes in v4:
time: 56.9 us; the launch traced here: 56.7 us
  starting transfers between devices  23.3 us (41%)
  waiting for transfers between devices  19.3 us (34%)
  Pallas kernels  6.12 us (11%)
  matrix products  4.29 us (8%)
  local copies, waits for them, and re-layouts  1.56 us (3%)
  other arithmetic  1.29 us (2%)
  between operations  0.84 us (1%)
    ppermute x18, starting transfers between devices, swap(): return lax.ppermute(value, ('dp', 'fsdp'), steps)  23.3 us
    ppermute x18, waiting for transfers between devices, swap(): return lax.ppermute(value, ('dp', 'fsdp'), steps)  19.3 us
    dot_general x12, matrix products, dot(): return jnp.dot(a, b, preferred_element_type=jnp.float32)  4.29 us
    pallas_call x1, Pallas kernels, update_of(): pl.pallas_call(functools.partial(update_kernel, tiles, masks), out_shape=...  2.2 us
    pallas_call x1, Pallas kernels, pack(): pl.pallas_call(functools.partial(pack_kernel, tokens), out_shape=[pltpu.V...  2.03 us
    pallas_call x1, Pallas kernels, turn(): pl.pallas_call(functools.partial(turn_kernel, rows), out_shape=pltpu.VMEM...  1.88 us
    dynamic_slice x1, local copies, waits for them, and re-layouts, local(): lax.dynamic_slice(basis, (at, 0), (half, rank))  1.27 us
  transfers between devices with their start and end apart: 18, of which 12 were waited for; matrix products, arithmetic and copies ran while one was open for 10% of the time, Pallas kernels for 7%

profile of v4, /device:TPU:0, one launch (start us, length us, event | category | flops | bytes accessed | tf_op | source)
XLA Modules:
  0.0 56.7 jit_solution(1996222694833099915)
XLA Ops:
  0.6 0.5 collective-permute-start
  1.2 1.3 %constant_dynamic-slice_fusion = (bf16[1024,256]{1,0:T(8,128)(2,1)S(1)}, bf16[1024,256]{1,0:T(8,128)(2,1)S(1)}) fusion(bf16[2048,256]{1,0:T(8,128)(2,1)} %param.7, s32[]{:T(128)S(6)} %select_n.19, s32[]{:T(128)S(6)} %select_n.18), kind=kLoop, calls=%fused_computation.38 | loop fusion | bytes 2097160 | tf_op jit(solution)/shard_map/dynamic_slice | solution.py:137
  2.5 3.0 %collective-permute-start.2 = (bf16[1024,256]{1,0:T(8,128)(2,1)S(1)}, bf16[1024,256]{1,0:T(8,128)(2,1)S(1)}, u32[]{:S(2)}, u32[]{:S(2)}) collective-permute-start(bf16[1024,256]{1,0:T(8,128)(2,1)S(1)} %get-tuple-element.37.first), channel_id=1, source_target_pairs={{0,1},{1,0},{2,3},{3,2},{4,6},{5,7},{6,4},{7,5},{8,9},{9,8},{10,11... | collective-permute-start | bytes 1572872 | tf_op jit(solution)/shard_map/ppermute | solution.py:128
  5.8 3.2 %collective-permute-done.1.other = bf16[192,4096]{1,0:T(8,128)(2,1)} collective-permute-done((bf16[192,4096]{1,0:T(8,128)(2,1)}, bf16[192,4096]{1,0:T(8,128)(2,1)}, u32[]{:S(2)}, u32[]{:S(2)}) %collective-permute-start.1) | collective-permute-done | bytes 1572896 | tf_op jit(solution)/shard_map/ppermute | solution.py:128
  9.0 1.9 %turn_cotangent.1 = bf16[16,128,384]{2,1,0:T(8,128)(2,1)S(1)} custom-call(s32[16]{0:T(128)S(1)} %add.117.order, bf16[192,4096]{1,0:T(8,128)(2,1)S(1)} %copy-done.1, bf16[192,4096]{1,0:T(8,128)(2,1)} %collective-permute-done.1.other), custom_call_target="tpu_custom_call" | custom-call | tf_op jit(solution)/shard_map/turn_cotangent/pallas_call | solution.py:64
  10.9 2.0 %pack_activations.1 = (bf16[384,1024]{1,0:T(8,128)(2,1)S(1)}, bf16[384,1024]{1,0:T(8,128)(2,1)S(1)}, bf16[384,1024]{1,0:T(8,128)(2,1)S(1)}, bf16[384,1024]{1,0:T(8,128)(2,1)S(1)}) custom-call(s32[4]{0:T(128)S(1)} %pad_add_fusion.1.starts, bf16[192,8192]{1,0:T(8,128)(2,1)S(1)} %copy-done, bf16[192,8192]{1,0:T(8,128)(2,1)} %collective-permute-done.other), custom_call_target="tpu_custom_call" | custom-call | tf_op jit(solution)/shard_map/pack_activations/pallas_call | solution.py:42
  13.0 0.4 fusion.18
  13.4 3.0 %collective-permute-start.4 = (bf16[1024,256]{1,0:T(8,128)(2,1)S(1)}, bf16[1024,256]{1,0:T(8,128)(2,1)S(1)}, u32[]{:S(2)}, u32[]{:S(2)}) collective-permute-start(bf16[1024,256]{1,0:T(8,128)(2,1)S(1)} %collective-permute-done.2), channel_id=1, source_target_pairs={{0,2},{1,3},{2,0},{3,1},{4,5},{5,4},{6,7},{7,6},{8,10},{9,11},{10,... | collective-permute-start | bytes 1572872 | tf_op jit(solution)/shard_map/ppermute | solution.py:128
  16.7 2.6 %collective-permute-done.3 = bf16[1024,256]{1,0:T(8,128)(2,1)} collective-permute-done((bf16[1024,256]{1,0:T(8,128)(2,1)S(1)}, bf16[1024,256]{1,0:T(8,128)(2,1)}, u32[]{:S(2)}, u32[]{:S(2)}) %collective-permute-start.3) | collective-permute-done | bytes 524320 | tf_op jit(solution)/shard_map/ppermute | solution.py:128
  19.3 1.4 %convolution_add_fusion = f32[384,256]{1,0:T(8,128)S(1)} fusion(f32[384,256]{1,0:T(8,128)S(1)} %convolution_add_fusion.1, bf16[384,1024]{1,0:T(8,128)(2,1)S(1)} %get-tuple-element.20, bf16[1024,256]{1,0:T(8,128)(2,1)} %collective-permute-done.3), kind=kOutput, calls=%fused_computation | convolution fusion | flops 201424896 | bytes 2097152 | tf_op jit(solution)/shard_map/dot_general | solution.py:16
  20.7 2.8 %collective-permute-done.4 = bf16[1024,256]{1,0:T(8,128)(2,1)S(1)} collective-permute-done((bf16[1024,256]{1,0:T(8,128)(2,1)S(1)}, bf16[1024,256]{1,0:T(8,128)(2,1)S(1)}, u32[]{:S(2)}, u32[]{:S(2)}) %collective-permute-start.4) | collective-permute-done | bytes 524320 | tf_op jit(solution)/shard_map/ppermute | solution.py:128
  23.5 0.4 fusion.19
  24.4 1.1 %collective-permute-done.5 = bf16[384,256]{1,0:T(8,128)(2,1)S(1)} collective-permute-done((bf16[384,256]{1,0:T(8,128)(2,1)S(1)}, bf16[384,256]{1,0:T(8,128)(2,1)S(1)}, u32[]{:S(2)}, u32[]{:S(2)}) %collective-permute-start.5) | collective-permute-done | bytes 196640 | tf_op jit(solution)/shard_map/ppermute | solution.py:128
  25.8 2.1 %collective-permute-start.6 = (bf16[2,128,256]{2,1,0:T(8,128)(2,1)S(1)}, bf16[2,128,256]{2,1,0:T(8,128)(2,1)S(1)}, u32[]{:S(2)}, u32[]{:S(2)}) collective-permute-start(bf16[2,128,256]{2,1,0:T(8,128)(2,1)S(1)} %convolution_convert_fusion.5), channel_id=1, source_target_pairs={{0,1},{1,0},{2,3},{3,2},{4,5},{5,4},{6,7},{7,6},{8,9},{9,8},{10,11... | collective-permute-start | bytes 393224 | tf_op jit(solution)/shard_map/ppermute | solution.py:128
  28.1 1.6 %collective-permute-start.11 = (bf16[2,128,256]{2,1,0:T(8,128)(2,1)S(1)}, bf16[2,128,256]{2,1,0:T(8,128)(2,1)S(1)}, u32[]{:S(2)}, u32[]{:S(2)}) collective-permute-start(bf16[2,128,256]{2,1,0:T(8,128)(2,1)S(1)} %convolution_convert_fusion), channel_id=1, source_target_pairs={{0,2},{1,3},{2,0},{3,1},{4,6},{5,7},{6,4},{7,5},{8,10},{9,11},{10,... | collective-permute-start | bytes 393224 | tf_op jit(solution)/shard_map/ppermute | solution.py:128
  30.4 1.3 %collective-permute-done.6 = bf16[2,128,256]{2,1,0:T(8,128)(2,1)S(1)} collective-permute-done((bf16[2,128,256]{2,1,0:T(8,128)(2,1)S(1)}, bf16[2,128,256]{2,1,0:T(8,128)(2,1)S(1)}, u32[]{:S(2)}, u32[]{:S(2)}) %collective-permute-start.6) | collective-permute-done | bytes 131104 | tf_op jit(solution)/shard_map/ppermute | solution.py:128
  32.0 2.5 %collective-permute-start.9 = (bf16[2,128,256]{2,1,0:T(8,128)(2,1)S(1)}, bf16[2,128,256]{2,1,0:T(8,128)(2,1)S(1)}, u32[]{:S(2)}, u32[]{:S(2)}) collective-permute-start(bf16[2,128,256]{2,1,0:T(8,128)(2,1)S(1)} %convolution_convert_fusion.2), channel_id=1, source_target_pairs={{0,1},{1,0},{2,3},{3,2},{4,5},{5,4},{6,7},{7,6},{8,9},{9,8},{10,11... | collective-permute-start | bytes 393224 | tf_op jit(solution)/shard_map/ppermute | solution.py:128
  34.7 1.4 %collective-permute-start.8 = (bf16[2,128,256]{2,1,0:T(8,128)(2,1)S(1)}, bf16[2,128,256]{2,1,0:T(8,128)(2,1)S(1)}, u32[]{:S(2)}, u32[]{:S(2)}) collective-permute-start(bf16[2,128,256]{2,1,0:T(8,128)(2,1)S(1)} %convolution_convert_fusion.3), channel_id=1, source_target_pairs={{0,2},{1,3},{2,0},{3,1},{4,6},{5,7},{6,4},{7,5},{8,10},{9,11},{10,... | collective-permute-start | bytes 393224 | tf_op jit(solution)/shard_map/ppermute | solution.py:128
  36.6 0.6 %collective-permute-done.10 = bf16[2,128,256]{2,1,0:T(8,128)(2,1)S(1)} collective-permute-done((bf16[2,128,256]{2,1,0:T(8,128)(2,1)S(1)}, bf16[2,128,256]{2,1,0:T(8,128)(2,1)S(1)}, u32[]{:S(2)}, u32[]{:S(2)}) %collective-permute-start.10) | collective-permute-done | bytes 131104 | tf_op jit(solution)/shard_map/ppermute | solution.py:128
  37.3 3.7 %collective-permute-start.14 = (bf16[128,256]{1,0:T(8,128)(2,1)S(1)}, bf16[128,256]{1,0:T(8,128)(2,1)S(1)}, u32[]{:S(2)}, u32[]{:S(2)}) collective-permute-start(bf16[128,256]{1,0:T(8,128)(2,1)S(1)} %get-tuple-element.41), channel_id=1, source_target_pairs={{0,24},{1,25},{2,26},{3,27},{4,28},{5,29},{6,30},{7,31},{8,16},{9,... | collective-permute-start | bytes 196616 | tf_op jit(solution)/shard_map/ppermute | solution.py:128
  40.9 1.6 %collective-permute-done.8 = bf16[2,128,256]{2,1,0:T(8,128)(2,1)S(1)} collective-permute-done((bf16[2,128,256]{2,1,0:T(8,128)(2,1)S(1)}, bf16[2,128,256]{2,1,0:T(8,128)(2,1)S(1)}, u32[]{:S(2)}, u32[]{:S(2)}) %collective-permute-start.8) | collective-permute-done | bytes 131104 | tf_op jit(solution)/shard_map/ppermute | solution.py:128
  42.6 1.5 %collective-permute-start.13 = (bf16[128,256]{1,0:T(8,128)(2,1)S(1)}, bf16[128,256]{1,0:T(8,128)(2,1)S(1)}, u32[]{:S(2)}, u32[]{:S(2)}) collective-permute-start(bf16[128,256]{1,0:T(8,128)(2,1)S(1)} %fusion.14), channel_id=1, source_target_pairs={{0,8},{1,9},{2,10},{3,11},{4,12},{5,13},{6,14},{7,15},{8,0},{9,1},... | collective-permute-start | bytes 196616 | tf_op jit(solution)/shard_map/ppermute | solution.py:128
  44.1 2.0 %collective-permute-done.12 = bf16[128,256]{1,0:T(8,128)(2,1)S(1)} collective-permute-done((bf16[128,256]{1,0:T(8,128)(2,1)S(1)}, bf16[128,256]{1,0:T(8,128)(2,1)S(1)}, u32[]{:S(2)}, u32[]{:S(2)}) %collective-permute-start.12) | collective-permute-done | bytes 65568 | tf_op jit(solution)/shard_map/ppermute | solution.py:128
  46.1 0.8 %collective-permute-done.13 = bf16[128,256]{1,0:T(8,128)(2,1)S(1)} collective-permute-done((bf16[128,256]{1,0:T(8,128)(2,1)S(1)}, bf16[128,256]{1,0:T(8,128)(2,1)S(1)}, u32[]{:S(2)}, u32[]{:S(2)}) %collective-permute-start.13) | collective-permute-done | bytes 65568 | tf_op jit(solution)/shard_map/ppermute | solution.py:128
  46.9 0.8 %divide_convert_fusion = (bf16[128,256]{1,0:T(8,128)(2,1)S(1)}, f32[128,256]{1,0:T(8,128)}, f32[128,256]{1,0:T(8,128)}) fusion(bf16[128,256]{1,0:T(8,128)(2,1)S(1)} %collective-permute-done.14, bf16[128,256]{1,0:T(8,128)(2,1)S(1)} %collective-permute-done.13, bf16[128,256]{1,0:T(8,128)(2,1)S(1)} %collective-permute-done.12, ...), kind=kLoop, calls=%fused_computation.28 | loop fusion | flops 589824 | bytes 917504 | tf_op jit(solution)/shard_map/convert_element_type | solution.py:191
  47.7 1.6 %collective-permute-start.15 = (bf16[128,256]{1,0:T(8,128)(2,1)S(1)}, bf16[128,256]{1,0:T(8,128)(2,1)S(1)}, u32[]{:S(2)}, u32[]{:S(2)}) collective-permute-start(bf16[128,256]{1,0:T(8,128)(2,1)S(1)} %get-tuple-element.25.refs_0_), channel_id=1, source_target_pairs={{0,3},{1,2},{2,1},{3,0},{4,7},{5,6},{6,5},{7,4},{8,11},{9,10},{10,... | collective-permute-start | bytes 196616 | tf_op jit(solution)/shard_map/ppermute | solution.py:128
  49.3 0.9 %collective-permute-start.16 = (bf16[128,256]{1,0:T(8,128)(2,1)S(1)}, bf16[128,256]{1,0:T(8,128)(2,1)S(1)}, u32[]{:S(2)}, u32[]{:S(2)}) collective-permute-start(bf16[128,256]{1,0:T(8,128)(2,1)S(1)} %get-tuple-element.25.refs_0_), channel_id=1, source_target_pairs={{0,2},{1,3},{2,0},{3,1},{4,6},{5,7},{6,4},{7,5},{8,10},{9,11},{10,... | collective-permute-start | bytes 196616 | tf_op jit(solution)/shard_map/ppermute | solution.py:128
  50.2 1.0 %collective-permute-start.17 = (bf16[128,256]{1,0:T(8,128)(2,1)S(1)}, bf16[128,256]{1,0:T(8,128)(2,1)S(1)}, u32[]{:S(2)}, u32[]{:S(2)}) collective-permute-start(bf16[128,256]{1,0:T(8,128)(2,1)S(1)} %get-tuple-element.25.refs_0_), channel_id=1, source_target_pairs={{0,1},{1,0},{2,3},{3,2},{4,5},{5,4},{6,7},{7,6},{8,9},{9,8},{10,11... | collective-permute-start | bytes 196616 | tf_op jit(solution)/shard_map/ppermute | solution.py:128
  51.3 1.6 %collective-permute-done.15.refs_1_ = bf16[128,256]{1,0:T(8,128)(2,1)S(1)} collective-permute-done((bf16[128,256]{1,0:T(8,128)(2,1)S(1)}, bf16[128,256]{1,0:T(8,128)(2,1)S(1)}, u32[]{:S(2)}, u32[]{:S(2)}) %collective-permute-start.15) | collective-permute-done | bytes 65568 | tf_op jit(solution)/shard_map/ppermute | solution.py:128
  52.9 0.7 %collective-permute-done.16.refs_2_ = bf16[128,256]{1,0:T(8,128)(2,1)S(1)} collective-permute-done((bf16[128,256]{1,0:T(8,128)(2,1)S(1)}, bf16[128,256]{1,0:T(8,128)(2,1)S(1)}, u32[]{:S(2)}, u32[]{:S(2)}) %collective-permute-start.16) | collective-permute-done | bytes 65568 | tf_op jit(solution)/shard_map/ppermute | solution.py:128
  53.6 0.9 %collective-permute-done.17.refs_3_ = bf16[128,256]{1,0:T(8,128)(2,1)S(1)} collective-permute-done((bf16[128,256]{1,0:T(8,128)(2,1)S(1)}, bf16[128,256]{1,0:T(8,128)(2,1)S(1)}, u32[]{:S(2)}, u32[]{:S(2)}) %collective-permute-start.17) | collective-permute-done | bytes 65568 | tf_op jit(solution)/shard_map/ppermute | solution.py:128
  54.5 2.2 %update.1 = bf16[2048,512]{1,0:T(8,128)(2,1)} custom-call(s32[2]{0:T(128)S(1)} %pad_add_fusion.place, bf16[1024,256]{1,0:T(8,128)(2,1)S(1)} %get-tuple-element.37.first, bf16[1024,256]{1,0:T(8,128)(2,1)S(1)} %get-tuple-element.36.second, bf16[128,256]{1,0:T(8,128)(2,1)S(1)} %get-tuple-element.25.refs_0_, ...), custom_call_target="tpu_custom_call" | custom-call | tf_op jit(solution)/shard_map/update/pallas_call | solution.py:102
  (44 shorter events, 3.7 us)
Async XLA Ops:
  0.6 8.4 %copy-start.1 = (bf16[192,4096]{1,0:T(8,128)(2,1)S(1)}, bf16[192,4096]{1,0:T(8,128)(2,1)}, u32[]{:S(2)}) copy-start(bf16[192,4096]{1,0:T(8,128)(2,1)} %own.3) | copy-start | bytes 4718596
  0.6 10.3 %collective-permute-start = (bf16[192,8192]{1,0:T(8,128)(2,1)}, bf16[192,8192]{1,0:T(8,128)(2,1)}, u32[]{:S(2)}, u32[]{:S(2)}) collective-permute-start(bf16[192,8192]{1,0:T(8,128)(2,1)} %own.2), channel_id=1, source_target_pairs={{0,4},{1,5},{2,6},{3,7},{4,0},{5,1},{6,2},{7,3},{8,12},{9,13},{10,... | collective-permute-start | bytes 9437192 | tf_op jit(solution)/shard_map/ppermute | solution.py:128
  1.2 7.9 %collective-permute-start.1 = (bf16[192,4096]{1,0:T(8,128)(2,1)}, bf16[192,4096]{1,0:T(8,128)(2,1)}, u32[]{:S(2)}, u32[]{:S(2)}) collective-permute-start(bf16[192,4096]{1,0:T(8,128)(2,1)} %own.3), channel_id=1, source_target_pairs={{0,4},{1,5},{2,6},{3,7},{4,0},{5,1},{6,2},{7,3},{8,12},{9,13},{10,... | collective-permute-start | bytes 4718600 | tf_op jit(solution)/shard_map/ppermute | solution.py:128
  2.5 10.9 %collective-permute-start.2 = (bf16[1024,256]{1,0:T(8,128)(2,1)S(1)}, bf16[1024,256]{1,0:T(8,128)(2,1)S(1)}, u32[]{:S(2)}, u32[]{:S(2)}) collective-permute-start(bf16[1024,256]{1,0:T(8,128)(2,1)S(1)} %get-tuple-element.37.first), channel_id=1, source_target_pairs={{0,1},{1,0},{2,3},{3,2},{4,6},{5,7},{6,4},{7,5},{8,9},{9,8},{10,11... | collective-permute-start | bytes 1572872 | tf_op jit(solution)/shard_map/ppermute | solution.py:128
  5.5 13.8 %collective-permute-start.3 = (bf16[1024,256]{1,0:T(8,128)(2,1)S(1)}, bf16[1024,256]{1,0:T(8,128)(2,1)}, u32[]{:S(2)}, u32[]{:S(2)}) collective-permute-start(bf16[1024,256]{1,0:T(8,128)(2,1)S(1)} %get-tuple-element.36.second), channel_id=1, source_target_pairs={{0,1},{1,0},{2,3},{3,2},{4,6},{5,7},{6,4},{7,5},{8,9},{9,8},{10,11... | collective-permute-start | bytes 1572872 | tf_op jit(solution)/shard_map/ppermute | solution.py:128
  5.8 5.1 %copy-start = (bf16[192,8192]{1,0:T(8,128)(2,1)S(1)}, bf16[192,8192]{1,0:T(8,128)(2,1)}, u32[]{:S(2)}) copy-start(bf16[192,8192]{1,0:T(8,128)(2,1)} %own.2) | copy-start | bytes 9437188
  13.4 10.1 %collective-permute-start.4 = (bf16[1024,256]{1,0:T(8,128)(2,1)S(1)}, bf16[1024,256]{1,0:T(8,128)(2,1)S(1)}, u32[]{:S(2)}, u32[]{:S(2)}) collective-permute-start(bf16[1024,256]{1,0:T(8,128)(2,1)S(1)} %collective-permute-done.2), channel_id=1, source_target_pairs={{0,2},{1,3},{2,0},{3,1},{4,5},{5,4},{6,7},{7,6},{8,10},{9,11},{10,... | collective-permute-start | bytes 1572872 | tf_op jit(solution)/shard_map/ppermute | solution.py:128
  24.0 1.5 %collective-permute-start.5 = (bf16[384,256]{1,0:T(8,128)(2,1)S(1)}, bf16[384,256]{1,0:T(8,128)(2,1)S(1)}, u32[]{:S(2)}, u32[]{:S(2)}) collective-permute-start(bf16[384,256]{1,0:T(8,128)(2,1)S(1)} %convert_element_type.69), channel_id=1, source_target_pairs={{0,4},{1,5},{2,6},{3,7},{4,0},{5,1},{6,2},{7,3},{8,12},{9,13},{10,... | collective-permute-start | bytes 589832 | tf_op jit(solution)/shard_map/ppermute | solution.py:128
  25.8 6.0 %collective-permute-start.6 = (bf16[2,128,256]{2,1,0:T(8,128)(2,1)S(1)}, bf16[2,128,256]{2,1,0:T(8,128)(2,1)S(1)}, u32[]{:S(2)}, u32[]{:S(2)}) collective-permute-start(bf16[2,128,256]{2,1,0:T(8,128)(2,1)S(1)} %convolution_convert_fusion.5), channel_id=1, source_target_pairs={{0,1},{1,0},{2,3},{3,2},{4,5},{5,4},{6,7},{7,6},{8,9},{9,8},{10,11... | collective-permute-start | bytes 393224 | tf_op jit(solution)/shard_map/ppermute | solution.py:128
  28.1 8.5 %collective-permute-start.11 = (bf16[2,128,256]{2,1,0:T(8,128)(2,1)S(1)}, bf16[2,128,256]{2,1,0:T(8,128)(2,1)S(1)}, u32[]{:S(2)}, u32[]{:S(2)}) collective-permute-start(bf16[2,128,256]{2,1,0:T(8,128)(2,1)S(1)} %convolution_convert_fusion), channel_id=1, source_target_pairs={{0,2},{1,3},{2,0},{3,1},{4,6},{5,7},{6,4},{7,5},{8,10},{9,11},{10,... | collective-permute-start | bytes 393224 | tf_op jit(solution)/shard_map/ppermute | solution.py:128
  30.1 7.1 %collective-permute-start.10 = (bf16[2,128,256]{2,1,0:T(8,128)(2,1)S(1)}, bf16[2,128,256]{2,1,0:T(8,128)(2,1)S(1)}, u32[]{:S(2)}, u32[]{:S(2)}) collective-permute-start(bf16[2,128,256]{2,1,0:T(8,128)(2,1)S(1)} %convolution_convert_fusion.1), channel_id=1, source_target_pairs={{0,3},{1,2},{2,1},{3,0},{4,7},{5,6},{6,5},{7,4},{8,11},{9,10},{10,... | collective-permute-start | bytes 393224 | tf_op jit(solution)/shard_map/ppermute | solution.py:128
  32.0 9.0 %collective-permute-start.9 = (bf16[2,128,256]{2,1,0:T(8,128)(2,1)S(1)}, bf16[2,128,256]{2,1,0:T(8,128)(2,1)S(1)}, u32[]{:S(2)}, u32[]{:S(2)}) collective-permute-start(bf16[2,128,256]{2,1,0:T(8,128)(2,1)S(1)} %convolution_convert_fusion.2), channel_id=1, source_target_pairs={{0,1},{1,0},{2,3},{3,2},{4,5},{5,4},{6,7},{7,6},{8,9},{9,8},{10,11... | collective-permute-start | bytes 393224 | tf_op jit(solution)/shard_map/ppermute | solution.py:128
  34.5 12.5 %copy-start.2 = (f32[128,256]{1,0:T(8,128)S(1)}, f32[128,256]{1,0:T(8,128)}, u32[]{:S(2)}) copy-start(f32[128,256]{1,0:T(8,128)} %param.8) | copy-start | bytes 393220
  34.5 12.5 %copy-start.3 = (f32[128,256]{1,0:T(8,128)S(1)}, f32[128,256]{1,0:T(8,128)}, u32[]{:S(2)}) copy-start(f32[128,256]{1,0:T(8,128)} %param.9) | copy-start | bytes 393220
  34.7 7.8 %collective-permute-start.8 = (bf16[2,128,256]{2,1,0:T(8,128)(2,1)S(1)}, bf16[2,128,256]{2,1,0:T(8,128)(2,1)S(1)}, u32[]{:S(2)}, u32[]{:S(2)}) collective-permute-start(bf16[2,128,256]{2,1,0:T(8,128)(2,1)S(1)} %convolution_convert_fusion.3), channel_id=1, source_target_pairs={{0,2},{1,3},{2,0},{3,1},{4,6},{5,7},{6,4},{7,5},{8,10},{9,11},{10,... | collective-permute-start | bytes 393224 | tf_op jit(solution)/shard_map/ppermute | solution.py:128
  36.3 6.2 %collective-permute-start.7 = (bf16[2,128,256]{2,1,0:T(8,128)(2,1)S(1)}, bf16[2,128,256]{2,1,0:T(8,128)(2,1)S(1)}, u32[]{:S(2)}, u32[]{:S(2)}) collective-permute-start(bf16[2,128,256]{2,1,0:T(8,128)(2,1)S(1)} %convolution_convert_fusion.4), channel_id=1, source_target_pairs={{0,3},{1,2},{2,1},{3,0},{4,7},{5,6},{6,5},{7,4},{8,11},{9,10},{10,... | collective-permute-start | bytes 393224 | tf_op jit(solution)/shard_map/ppermute | solution.py:128
  37.3 6.8 %collective-permute-start.14 = (bf16[128,256]{1,0:T(8,128)(2,1)S(1)}, bf16[128,256]{1,0:T(8,128)(2,1)S(1)}, u32[]{:S(2)}, u32[]{:S(2)}) collective-permute-start(bf16[128,256]{1,0:T(8,128)(2,1)S(1)} %get-tuple-element.41), channel_id=1, source_target_pairs={{0,24},{1,25},{2,26},{3,27},{4,28},{5,29},{6,30},{7,31},{8,16},{9,... | collective-permute-start | bytes 196616 | tf_op jit(solution)/shard_map/ppermute | solution.py:128
  40.9 5.2 %collective-permute-start.12 = (bf16[128,256]{1,0:T(8,128)(2,1)S(1)}, bf16[128,256]{1,0:T(8,128)(2,1)S(1)}, u32[]{:S(2)}, u32[]{:S(2)}) collective-permute-start(bf16[128,256]{1,0:T(8,128)(2,1)S(1)} %get-tuple-element.40), channel_id=1, source_target_pairs={{0,16},{1,17},{2,18},{3,19},{4,20},{5,21},{6,22},{7,23},{8,24},{9,... | collective-permute-start | bytes 196616 | tf_op jit(solution)/shard_map/ppermute | solution.py:128
  42.6 4.3 %collective-permute-start.13 = (bf16[128,256]{1,0:T(8,128)(2,1)S(1)}, bf16[128,256]{1,0:T(8,128)(2,1)S(1)}, u32[]{:S(2)}, u32[]{:S(2)}) collective-permute-start(bf16[128,256]{1,0:T(8,128)(2,1)S(1)} %fusion.14), channel_id=1, source_target_pairs={{0,8},{1,9},{2,10},{3,11},{4,12},{5,13},{6,14},{7,15},{8,0},{9,1},... | collective-permute-start | bytes 196616 | tf_op jit(solution)/shard_map/ppermute | solution.py:128
  47.7 5.2 %collective-permute-start.15 = (bf16[128,256]{1,0:T(8,128)(2,1)S(1)}, bf16[128,256]{1,0:T(8,128)(2,1)S(1)}, u32[]{:S(2)}, u32[]{:S(2)}) collective-permute-start(bf16[128,256]{1,0:T(8,128)(2,1)S(1)} %get-tuple-element.25.refs_0_), channel_id=1, source_target_pairs={{0,3},{1,2},{2,1},{3,0},{4,7},{5,6},{6,5},{7,4},{8,11},{9,10},{10,... | collective-permute-start | bytes 196616 | tf_op jit(solution)/shard_map/ppermute | solution.py:128
  49.3 4.3 %collective-permute-start.16 = (bf16[128,256]{1,0:T(8,128)(2,1)S(1)}, bf16[128,256]{1,0:T(8,128)(2,1)S(1)}, u32[]{:S(2)}, u32[]{:S(2)}) collective-permute-start(bf16[128,256]{1,0:T(8,128)(2,1)S(1)} %get-tuple-element.25.refs_0_), channel_id=1, source_target_pairs={{0,2},{1,3},{2,0},{3,1},{4,6},{5,7},{6,4},{7,5},{8,10},{9,11},{10,... | collective-permute-start | bytes 196616 | tf_op jit(solution)/shard_map/ppermute | solution.py:128
  50.2 4.3 %collective-permute-start.17 = (bf16[128,256]{1,0:T(8,128)(2,1)S(1)}, bf16[128,256]{1,0:T(8,128)(2,1)S(1)}, u32[]{:S(2)}, u32[]{:S(2)}) collective-permute-start(bf16[128,256]{1,0:T(8,128)(2,1)S(1)} %get-tuple-element.25.refs_0_), channel_id=1, source_target_pairs={{0,1},{1,0},{2,3},{3,2},{4,5},{5,4},{6,7},{7,6},{8,9},{9,8},{10,11... | collective-permute-start | bytes 196616 | tf_op jit(solution)/shard_map/ppermute | solution.py:128

commit v5 on v4

--- a/solution.py
+++ b/solution.py
@@ -134,7 +134,9 @@
         core, pair = mine % 2, mine // 2
 
         begin = core * half
-        part, rest = (lax.dynamic_slice(basis, (at, 0), (half, rank)) for at in (begin, half - begin))
+        part = lax.dynamic_slice(basis, (begin, 0), (half, rank))
+        part, later = lax.optimization_barrier((part, basis))
+        rest = lax.dynamic_slice(later, (half - begin, 0), (half, rank))
         parts = [part]
         if fsdp == 4:
             near = here ^ (1 + core)
@@ -153,7 +155,8 @@
             ((jnp.arange(pairs) ^ pair) * 2 + core)[:, None] * fsdp + (jnp.arange(fsdp) ^ here)[None, :]
         )
         owners = owners.reshape(2, pairs // 2, fsdp).swapaxes(1, 2).reshape(-1)
-        features = turn(cotangent, swap(cotangent, across_core=1), owners, rows)
+        other, parts[1] = lax.optimization_barrier((swap(cotangent, across_core=1), parts[1]))
+        features = turn(cotangent, other, owners, rows)
         features = features.reshape(2, fsdp, pairs // 2 * rows, 2 * tokens)
         shared[0], features = lax.optimization_barrier((shared[0], features))
 
@@ -167,13 +170,13 @@
         def term(side, k, value):
             return dot(features[side, k].reshape(-1, 2 * tokens), value).reshape(pairs // 2, rows, rank)
 
-        masks, middle = range(fsdp - 1, 0, -1), pairs // 2
+        masks, middle = range(1, fsdp), pairs // 2
         arrivals, arrived, plane, value = [], {}, {}, projected
         for side in (1, 0):
             terms = {k: term(side, k, value).astype(jnp.bfloat16) for k in masks}
             arrived[side] = {k: swap(v, across_fsdp=(k, k)) for k, v in terms.items()}
             value, arrived[side][1] = lax.optimization_barrier((value, arrived[side][1]))
-        for side in (1, 0):
+        for side in (0, 1):
             plane[side] = term(side, 0, projected)
             for k in masks:
                 plane[side] += arrived[side][k].astype(jnp.float32)
@@ -184,13 +187,17 @@
         for value in arrivals:
             grad += value.astype(jnp.float32)
 
-        new_first = 0.9 * first_moment + 0.1 * grad
-        new_second = 0.999 * second_moment + 0.001 * grad * grad
+        def moments(grad):
+            return 0.9 * first_moment + 0.1 * grad, 0.999 * second_moment + 0.001 * grad * grad
+
         bias_one = 1.0 - 0.9**ADAM_STEP
         bias_two = 1.0 - 0.999**ADAM_STEP
+        new_first, new_second = moments(grad)
         step = (new_first / bias_one / (jnp.sqrt(new_second / bias_two) + 1e-08)).astype(jnp.bfloat16)
-        steps = {k: swap(step, across_fsdp=(k, k)) for k in range(1, fsdp)}
-        update = update_of(part, rest, [step] + [steps[k] for k in masks], [0, *masks], here, core)
+        step, kept = lax.optimization_barrier((step, grad))
+        new_first, new_second = moments(kept)
+        steps = {k: swap(step, across_fsdp=(k, k)) for k in masks}
+        update = update_of(part, rest, [step] + [steps[k] for k in masks[::-1]], [0, *masks[::-1]], here, core)
         return (update, new_first, new_second)
 
     in_specs = (

time: 56.9 us -> 55.7 us (0.979)
  waiting for transfers between devices: 19.3 us -> 17.7 us
  local copies, waits for them, and re-layouts: 1.56 us -> 2.87 us
  matrix products: 4.29 us -> 3.25 us
    unnamed x8 -> x10, local copies, waits for them, and re-layouts: 0.02 us -> 2.52 us
    ppermute x18, waiting for transfers between devices: 19.3 us -> 17.7 us  [swap(): return lax.ppermute(value, ('dp', 'fsdp'), steps)]
    dynamic_slice x1 -> x2, local copies, waits for them, and re-layouts: 1.27 us -> 0.07 us  [the longest x1 0.03 us: local(): part = lax.dynamic_slice(basis, (begin, 0), (half, rank))]
    dot_general x12, matrix products: 4.29 us -> 3.25 us  [dot(): return jnp.dot(a, b, preferred_element_type=jnp.float32)]
    add x0 -> x1, other arithmetic: none -> 0.74 us  [moments(): 0.999 * second_moment + 0.001 * grad * grad]
    convert_element_type x1, other arithmetic: 0.8 us -> 0.12 us  [local(): (new_first / bias_one / (jnp.sqrt(new_second / bias_two) + 1e-08)).astype...]
  transfers between devices with their start and end apart: 18 -> 18, of which waited for: 12 -> 13; matrix products, arithmetic and copies ran while one was open for 10% -> 7% of each run, Pallas kernels for 7% -> 7%
where the time goes in v5:
time: 55.7 us; the launch traced here: 55.5 us
  starting transfers between devices  23.4 us (42%)
  waiting for transfers between devices  17.7 us (32%)
  Pallas kernels  6.12 us (11%)
  matrix products  3.25 us (6%)
  local copies, waits for them, and re-layouts  2.87 us (5%)
  other arithmetic  1.35 us (2%)
  between operations  0.86 us (2%)
    ppermute x18, starting transfers between devices, swap(): return lax.ppermute(value, ('dp', 'fsdp'), steps)  23.4 us
    ppermute x18, waiting for transfers between devices, swap(): return lax.ppermute(value, ('dp', 'fsdp'), steps)  17.7 us
    dot_general x12, matrix products, dot(): return jnp.dot(a, b, preferred_element_type=jnp.float32)  3.25 us
    unnamed x10, local copies, waits for them, and re-layouts  2.52 us
    pallas_call x1, Pallas kernels, update_of(): pl.pallas_call(functools.partial(update_kernel, tiles, masks), out_shape=...  2.2 us
    pallas_call x1, Pallas kernels, pack(): pl.pallas_call(functools.partial(pack_kernel, tokens), out_shape=[pltpu.V...  2.03 us
    pallas_call x1, Pallas kernels, turn(): pl.pallas_call(functools.partial(turn_kernel, rows), out_shape=pltpu.VMEM...  1.88 us
  transfers between devices with their start and end apart: 18, of which 13 were waited for; matrix products, arithmetic and copies ran while one was open for 7% of the time, Pallas kernels for 7%

profile of v5, /device:TPU:0, one launch (start us, length us, event | category | flops | bytes accessed | tf_op | source)
XLA Modules:
  0.0 55.5 jit_solution(12466053482855668018)
XLA Ops:
  0.6 0.5 collective-permute-start
  1.2 0.6 %copy-done = bf16[2048,256]{1,0:T(8,128)(2,1)S(1)} copy-done((bf16[2048,256]{1,0:T(8,128)(2,1)S(1)}, bf16[2048,256]{1,0:T(8,128)(2,1)}, u32[]{:S(2)}) %copy-start) | copy-done | bytes 1048600
  1.9 3.0 %collective-permute-start.2 = (bf16[1024,256]{1,0:T(8,128)(2,1)S(1)}, bf16[1024,256]{1,0:T(8,128)(2,1)S(1)}, u32[]{:S(2)}, u32[]{:S(2)}) collective-permute-start(bf16[1024,256]{1,0:T(8,128)(2,1)S(1)} %constant_dynamic-slice_fusion.1.first), channel_id=1, source_target_pairs={{0,1},{1,0},{2,3},{3,2},{4,6},{5,7},{6,4},{7,5},{8,9},{9,8},{10,11... | collective-permute-start | bytes 1572872 | tf_op jit(solution)/shard_map/ppermute | solution.py:128
  5.3 1.5 %collective-permute-done.other = bf16[192,8192]{1,0:T(8,128)(2,1)} collective-permute-done((bf16[192,8192]{1,0:T(8,128)(2,1)}, bf16[192,8192]{1,0:T(8,128)(2,1)}, u32[]{:S(2)}, u32[]{:S(2)}) %collective-permute-start) | collective-permute-done | bytes 3145760 | tf_op jit(solution)/shard_map/ppermute | solution.py:128
  6.8 1.9 %copy-done.1 = bf16[192,8192]{1,0:T(8,128)(2,1)S(1)} copy-done((bf16[192,8192]{1,0:T(8,128)(2,1)S(1)}, bf16[192,8192]{1,0:T(8,128)(2,1)}, u32[]{:S(2)}) %copy-start.1) | copy-done | bytes 3145752
  8.7 2.0 %pack_activations.1 = (bf16[384,1024]{1,0:T(8,128)(2,1)S(1)}, bf16[384,1024]{1,0:T(8,128)(2,1)S(1)}, bf16[384,1024]{1,0:T(8,128)(2,1)S(1)}, bf16[384,1024]{1,0:T(8,128)(2,1)S(1)}) custom-call(s32[4]{0:T(128)S(1)} %pad_add_fusion.1.starts, bf16[192,8192]{1,0:T(8,128)(2,1)S(1)} %copy-done.1, bf16[192,8192]{1,0:T(8,128)(2,1)} %collective-permute-done.other), custom_call_target="tpu_custom_call" | custom-call | tf_op jit(solution)/shard_map/pack_activations/pallas_call | solution.py:42
  10.7 1.3 %collective-permute-done.2 = bf16[1024,256]{1,0:T(8,128)(2,1)S(1)} collective-permute-done((bf16[1024,256]{1,0:T(8,128)(2,1)S(1)}, bf16[1024,256]{1,0:T(8,128)(2,1)S(1)}, u32[]{:S(2)}, u32[]{:S(2)}) %collective-permute-start.2) | collective-permute-done | bytes 524320 | tf_op jit(solution)/shard_map/ppermute | solution.py:128
  12.1 2.0 %collective-permute-start.4 = (bf16[1024,256]{1,0:T(8,128)(2,1)S(1)}, bf16[1024,256]{1,0:T(8,128)(2,1)S(1)}, u32[]{:S(2)}, u32[]{:S(2)}) collective-permute-start(bf16[1024,256]{1,0:T(8,128)(2,1)S(1)} %collective-permute-done.2), channel_id=1, source_target_pairs={{0,2},{1,3},{2,0},{3,1},{4,5},{5,4},{6,7},{7,6},{8,10},{9,11},{10,... | collective-permute-start | bytes 1572872 | tf_op jit(solution)/shard_map/ppermute | solution.py:128
  14.1 1.9 %turn_cotangent.1 = bf16[16,128,384]{2,1,0:T(8,128)(2,1)S(1)} custom-call(s32[16]{0:T(128)S(1)} %add.123.order, bf16[192,4096]{1,0:T(8,128)(2,1)S(1)} %copy-done.2, bf16[192,4096]{1,0:T(8,128)(2,1)} %collective-permute-done.1.other), custom_call_target="tpu_custom_call" | custom-call | tf_op jit(solution)/shard_map/turn_cotangent/pallas_call | solution.py:64
  16.8 3.9 %collective-permute-done.3 = bf16[1024,256]{1,0:T(8,128)(2,1)S(1)} collective-permute-done((bf16[1024,256]{1,0:T(8,128)(2,1)S(1)}, bf16[1024,256]{1,0:T(8,128)(2,1)S(1)}, u32[]{:S(2)}, u32[]{:S(2)}) %collective-permute-start.3) | collective-permute-done | bytes 524320 | tf_op jit(solution)/shard_map/ppermute | solution.py:128
  21.0 1.4 %collective-permute-done.4 = bf16[1024,256]{1,0:T(8,128)(2,1)S(1)} collective-permute-done((bf16[1024,256]{1,0:T(8,128)(2,1)S(1)}, bf16[1024,256]{1,0:T(8,128)(2,1)S(1)}, u32[]{:S(2)}, u32[]{:S(2)}) %collective-permute-start.4) | collective-permute-done | bytes 524320 | tf_op jit(solution)/shard_map/ppermute | solution.py:128
  23.0 0.7 %collective-permute-start.5 = (bf16[384,256]{1,0:T(8,128)(2,1)S(1)}, bf16[384,256]{1,0:T(8,128)(2,1)S(1)}, u32[]{:S(2)}, u32[]{:S(2)}) collective-permute-start(bf16[384,256]{1,0:T(8,128)(2,1)S(1)} %convert_element_type.69), channel_id=1, source_target_pairs={{0,4},{1,5},{2,6},{3,7},{4,0},{5,1},{6,2},{7,3},{8,12},{9,13},{10,... | collective-permute-start | bytes 589832 | tf_op jit(solution)/shard_map/ppermute | solution.py:128
  23.8 0.9 %collective-permute-done.5 = bf16[384,256]{1,0:T(8,128)(2,1)S(1)} collective-permute-done((bf16[384,256]{1,0:T(8,128)(2,1)S(1)}, bf16[384,256]{1,0:T(8,128)(2,1)S(1)}, u32[]{:S(2)}, u32[]{:S(2)}) %collective-permute-start.5) | collective-permute-done | bytes 196640 | tf_op jit(solution)/shard_map/ppermute | solution.py:128
  25.0 2.1 %collective-permute-start.6 = (bf16[2,128,256]{2,1,0:T(8,128)(2,1)S(1)}, bf16[2,128,256]{2,1,0:T(8,128)(2,1)S(1)}, u32[]{:S(2)}, u32[]{:S(2)}) collective-permute-start(bf16[2,128,256]{2,1,0:T(8,128)(2,1)S(1)} %convolution_convert_fusion.5), channel_id=1, source_target_pairs={{0,1},{1,0},{2,3},{3,2},{4,5},{5,4},{6,7},{7,6},{8,9},{9,8},{10,11... | collective-permute-start | bytes 393224 | tf_op jit(solution)/shard_map/ppermute | solution.py:128
  27.6 1.6 %collective-permute-start.10 = (bf16[2,128,256]{2,1,0:T(8,128)(2,1)S(1)}, bf16[2,128,256]{2,1,0:T(8,128)(2,1)S(1)}, u32[]{:S(2)}, u32[]{:S(2)}) collective-permute-start(bf16[2,128,256]{2,1,0:T(8,128)(2,1)S(1)} %convolution_convert_fusion.1), channel_id=1, source_target_pairs={{0,2},{1,3},{2,0},{3,1},{4,6},{5,7},{6,4},{7,5},{8,10},{9,11},{10,... | collective-permute-start | bytes 393224 | tf_op jit(solution)/shard_map/ppermute | solution.py:128
  29.7 1.4 %collective-permute-done.6 = bf16[2,128,256]{2,1,0:T(8,128)(2,1)S(1)} collective-permute-done((bf16[2,128,256]{2,1,0:T(8,128)(2,1)S(1)}, bf16[2,128,256]{2,1,0:T(8,128)(2,1)S(1)}, u32[]{:S(2)}, u32[]{:S(2)}) %collective-permute-start.6) | collective-permute-done | bytes 131104 | tf_op jit(solution)/shard_map/ppermute | solution.py:128
  31.4 2.4 %collective-permute-start.7 = (bf16[2,128,256]{2,1,0:T(8,128)(2,1)S(1)}, bf16[2,128,256]{2,1,0:T(8,128)(2,1)S(1)}, u32[]{:S(2)}, u32[]{:S(2)}) collective-permute-start(bf16[2,128,256]{2,1,0:T(8,128)(2,1)S(1)} %convolution_convert_fusion.4), channel_id=1, source_target_pairs={{0,1},{1,0},{2,3},{3,2},{4,5},{5,4},{6,7},{7,6},{8,9},{9,8},{10,11... | collective-permute-start | bytes 393224 | tf_op jit(solution)/shard_map/ppermute | solution.py:128
  34.0 1.6 %collective-permute-start.8 = (bf16[2,128,256]{2,1,0:T(8,128)(2,1)S(1)}, bf16[2,128,256]{2,1,0:T(8,128)(2,1)S(1)}, u32[]{:S(2)}, u32[]{:S(2)}) collective-permute-start(bf16[2,128,256]{2,1,0:T(8,128)(2,1)S(1)} %convolution_convert_fusion.3), channel_id=1, source_target_pairs={{0,2},{1,3},{2,0},{3,1},{4,6},{5,7},{6,4},{7,5},{8,10},{9,11},{10,... | collective-permute-start | bytes 393224 | tf_op jit(solution)/shard_map/ppermute | solution.py:128
  35.9 0.6 %collective-permute-done.11 = bf16[2,128,256]{2,1,0:T(8,128)(2,1)S(1)} collective-permute-done((bf16[2,128,256]{2,1,0:T(8,128)(2,1)S(1)}, bf16[2,128,256]{2,1,0:T(8,128)(2,1)S(1)}, u32[]{:S(2)}, u32[]{:S(2)}) %collective-permute-start.11) | collective-permute-done | bytes 131104 | tf_op jit(solution)/shard_map/ppermute | solution.py:128
  36.5 2.6 %collective-permute-start.12 = (bf16[128,256]{1,0:T(8,128)(2,1)S(1)}, bf16[128,256]{1,0:T(8,128)(2,1)S(1)}, u32[]{:S(2)}, u32[]{:S(2)}) collective-permute-start(bf16[128,256]{1,0:T(8,128)(2,1)S(1)} %get-tuple-element.51), channel_id=1, source_target_pairs={{0,16},{1,17},{2,18},{3,19},{4,20},{5,21},{6,22},{7,23},{8,24},{9,... | collective-permute-start | bytes 196616 | tf_op jit(solution)/shard_map/ppermute | solution.py:128
  39.2 1.4 %collective-permute-start.14 = (bf16[128,256]{1,0:T(8,128)(2,1)S(1)}, bf16[128,256]{1,0:T(8,128)(2,1)S(1)}, u32[]{:S(2)}, u32[]{:S(2)}) collective-permute-start(bf16[128,256]{1,0:T(8,128)(2,1)S(1)} %get-tuple-element.52), channel_id=1, source_target_pairs={{0,24},{1,25},{2,26},{3,27},{4,28},{5,29},{6,30},{7,31},{8,16},{9,... | collective-permute-start | bytes 196616 | tf_op jit(solution)/shard_map/ppermute | solution.py:128
  40.5 1.3 %collective-permute-done.8 = bf16[2,128,256]{2,1,0:T(8,128)(2,1)S(1)} collective-permute-done((bf16[2,128,256]{2,1,0:T(8,128)(2,1)S(1)}, bf16[2,128,256]{2,1,0:T(8,128)(2,1)S(1)}, u32[]{:S(2)}, u32[]{:S(2)}) %collective-permute-start.8) | collective-permute-done | bytes 131104 | tf_op jit(solution)/shard_map/ppermute | solution.py:128
  41.9 1.6 %collective-permute-start.13 = (bf16[128,256]{1,0:T(8,128)(2,1)S(1)}, bf16[128,256]{1,0:T(8,128)(2,1)S(1)}, u32[]{:S(2)}, u32[]{:S(2)}) collective-permute-start(bf16[128,256]{1,0:T(8,128)(2,1)S(1)} %fusion.20), channel_id=1, source_target_pairs={{0,8},{1,9},{2,10},{3,11},{4,12},{5,13},{6,14},{7,15},{8,0},{9,1},... | collective-permute-start | bytes 196616 | tf_op jit(solution)/shard_map/ppermute | solution.py:128
  43.5 2.4 %collective-permute-done.14 = bf16[128,256]{1,0:T(8,128)(2,1)S(1)} collective-permute-done((bf16[128,256]{1,0:T(8,128)(2,1)S(1)}, bf16[128,256]{1,0:T(8,128)(2,1)S(1)}, u32[]{:S(2)}, u32[]{:S(2)}) %collective-permute-start.14) | collective-permute-done | bytes 65568 | tf_op jit(solution)/shard_map/ppermute | solution.py:128
  46.6 1.8 %collective-permute-start.15 = (bf16[128,256]{1,0:T(8,128)(2,1)S(1)}, bf16[128,256]{1,0:T(8,128)(2,1)S(1)}, u32[]{:S(2)}, u32[]{:S(2)}) collective-permute-start(bf16[128,256]{1,0:T(8,128)(2,1)S(1)} %get-tuple-element.35.refs_0_), channel_id=1, source_target_pairs={{0,3},{1,2},{2,1},{3,0},{4,7},{5,6},{6,5},{7,4},{8,11},{9,10},{10,... | collective-permute-start | bytes 196616 | tf_op jit(solution)/shard_map/ppermute | solution.py:128
  48.4 0.7 %collective-permute-start.16 = (bf16[128,256]{1,0:T(8,128)(2,1)S(1)}, bf16[128,256]{1,0:T(8,128)(2,1)S(1)}, u32[]{:S(2)}, u32[]{:S(2)}) collective-permute-start(bf16[128,256]{1,0:T(8,128)(2,1)S(1)} %get-tuple-element.35.refs_0_), channel_id=1, source_target_pairs={{0,2},{1,3},{2,0},{3,1},{4,6},{5,7},{6,4},{7,5},{8,10},{9,11},{10,... | collective-permute-start | bytes 196616 | tf_op jit(solution)/shard_map/ppermute | solution.py:128
  49.0 1.1 %collective-permute-start.17 = (bf16[128,256]{1,0:T(8,128)(2,1)S(1)}, bf16[128,256]{1,0:T(8,128)(2,1)S(1)}, u32[]{:S(2)}, u32[]{:S(2)}) collective-permute-start(bf16[128,256]{1,0:T(8,128)(2,1)S(1)} %get-tuple-element.35.refs_0_), channel_id=1, source_target_pairs={{0,1},{1,0},{2,3},{3,2},{4,5},{5,4},{6,7},{7,6},{8,9},{9,8},{10,11... | collective-permute-start | bytes 196616 | tf_op jit(solution)/shard_map/ppermute | solution.py:128
  50.1 0.7 %fusion.15 = (f32[128,256]{1,0:T(8,128)}, f32[128,256]{1,0:T(8,128)}) fusion(f32[128,256]{1,0:T(8,128)S(1)} %get-tuple-element.36, f32[128,256]{1,0:T(8,128)S(1)} %copy-done.3, f32[128,256]{1,0:T(8,128)S(1)} %copy-done.4), kind=kLoop, calls=%fused_computation.28 | loop fusion | flops 229376 | bytes 655360 | tf_op jit(solution)/shard_map/add | solution.py:191
  50.9 0.9 %collective-permute-done.15.refs_1_ = bf16[128,256]{1,0:T(8,128)(2,1)S(1)} collective-permute-done((bf16[128,256]{1,0:T(8,128)(2,1)S(1)}, bf16[128,256]{1,0:T(8,128)(2,1)S(1)}, u32[]{:S(2)}, u32[]{:S(2)}) %collective-permute-start.15) | collective-permute-done | bytes 65568 | tf_op jit(solution)/shard_map/ppermute | solution.py:128
  51.8 0.8 %collective-permute-done.16.refs_2_ = bf16[128,256]{1,0:T(8,128)(2,1)S(1)} collective-permute-done((bf16[128,256]{1,0:T(8,128)(2,1)S(1)}, bf16[128,256]{1,0:T(8,128)(2,1)S(1)}, u32[]{:S(2)}, u32[]{:S(2)}) %collective-permute-start.16) | collective-permute-done | bytes 65568 | tf_op jit(solution)/shard_map/ppermute | solution.py:128
  52.6 0.7 %collective-permute-done.17.refs_3_ = bf16[128,256]{1,0:T(8,128)(2,1)S(1)} collective-permute-done((bf16[128,256]{1,0:T(8,128)(2,1)S(1)}, bf16[128,256]{1,0:T(8,128)(2,1)S(1)}, u32[]{:S(2)}, u32[]{:S(2)}) %collective-permute-start.17) | collective-permute-done | bytes 65568 | tf_op jit(solution)/shard_map/ppermute | solution.py:128
  53.3 2.2 %update.1 = bf16[2048,512]{1,0:T(8,128)(2,1)} custom-call(s32[2]{0:T(128)S(1)} %pad_add_fusion.place, bf16[1024,256]{1,0:T(8,128)(2,1)S(1)} %constant_dynamic-slice_fusion.1.first, bf16[1024,256]{1,0:T(8,128)(2,1)S(1)} %constant_dynamic-slice_fusion.second, bf16[128,256]{1,0:T(8,128)(2,1)S(1)} %get-tuple-element.35.refs_0_, ...), custom_call_target="tpu_custom_call" | custom-call | tf_op jit(solution)/shard_map/update/pallas_call | solution.py:102
  (48 shorter events, 5.1 us)
Async XLA Ops:
  0.6 1.2 %copy-start = (bf16[2048,256]{1,0:T(8,128)(2,1)S(1)}, bf16[2048,256]{1,0:T(8,128)(2,1)}, u32[]{:S(2)}) copy-start(bf16[2048,256]{1,0:T(8,128)(2,1)} %param.7) | copy-start | bytes 3145732
  0.6 6.1 %collective-permute-start = (bf16[192,8192]{1,0:T(8,128)(2,1)}, bf16[192,8192]{1,0:T(8,128)(2,1)}, u32[]{:S(2)}, u32[]{:S(2)}) collective-permute-start(bf16[192,8192]{1,0:T(8,128)(2,1)} %own.2), channel_id=1, source_target_pairs={{0,4},{1,5},{2,6},{3,7},{4,0},{5,1},{6,2},{7,3},{8,12},{9,13},{10,... | collective-permute-start | bytes 9437192 | tf_op jit(solution)/shard_map/ppermute | solution.py:128
  1.2 13.0 %collective-permute-start.1 = (bf16[192,4096]{1,0:T(8,128)(2,1)}, bf16[192,4096]{1,0:T(8,128)(2,1)}, u32[]{:S(2)}, u32[]{:S(2)}) collective-permute-start(bf16[192,4096]{1,0:T(8,128)(2,1)} %own.3), channel_id=1, source_target_pairs={{0,4},{1,5},{2,6},{3,7},{4,0},{5,1},{6,2},{7,3},{8,12},{9,13},{10,... | collective-permute-start | bytes 4718600 | tf_op jit(solution)/shard_map/ppermute | solution.py:128
  1.9 10.2 %collective-permute-start.2 = (bf16[1024,256]{1,0:T(8,128)(2,1)S(1)}, bf16[1024,256]{1,0:T(8,128)(2,1)S(1)}, u32[]{:S(2)}, u32[]{:S(2)}) collective-permute-start(bf16[1024,256]{1,0:T(8,128)(2,1)S(1)} %constant_dynamic-slice_fusion.1.first), channel_id=1, source_target_pairs={{0,1},{1,0},{2,3},{3,2},{4,6},{5,7},{6,4},{7,5},{8,9},{9,8},{10,11... | collective-permute-start | bytes 1572872 | tf_op jit(solution)/shard_map/ppermute | solution.py:128
  4.9 15.7 %collective-permute-start.3 = (bf16[1024,256]{1,0:T(8,128)(2,1)S(1)}, bf16[1024,256]{1,0:T(8,128)(2,1)S(1)}, u32[]{:S(2)}, u32[]{:S(2)}) collective-permute-start(bf16[1024,256]{1,0:T(8,128)(2,1)S(1)} %constant_dynamic-slice_fusion.second), channel_id=1, source_target_pairs={{0,1},{1,0},{2,3},{3,2},{4,6},{5,7},{6,4},{7,5},{8,9},{9,8},{10,11... | collective-permute-start | bytes 1572872 | tf_op jit(solution)/shard_map/ppermute | solution.py:128
  6.8 1.9 %copy-start.1 = (bf16[192,8192]{1,0:T(8,128)(2,1)S(1)}, bf16[192,8192]{1,0:T(8,128)(2,1)}, u32[]{:S(2)}) copy-start(bf16[192,8192]{1,0:T(8,128)(2,1)} %own.2) | copy-start | bytes 9437188
  8.7 5.4 %copy-start.2 = (bf16[192,4096]{1,0:T(8,128)(2,1)S(1)}, bf16[192,4096]{1,0:T(8,128)(2,1)}, u32[]{:S(2)}) copy-start(bf16[192,4096]{1,0:T(8,128)(2,1)} %own.3) | copy-start | bytes 4718596
  12.1 10.4 %collective-permute-start.4 = (bf16[1024,256]{1,0:T(8,128)(2,1)S(1)}, bf16[1024,256]{1,0:T(8,128)(2,1)S(1)}, u32[]{:S(2)}, u32[]{:S(2)}) collective-permute-start(bf16[1024,256]{1,0:T(8,128)(2,1)S(1)} %collective-permute-done.2), channel_id=1, source_target_pairs={{0,2},{1,3},{2,0},{3,1},{4,5},{5,4},{6,7},{7,6},{8,10},{9,11},{10,... | collective-permute-start | bytes 1572872 | tf_op jit(solution)/shard_map/ppermute | solution.py:128
  23.0 1.8 %collective-permute-start.5 = (bf16[384,256]{1,0:T(8,128)(2,1)S(1)}, bf16[384,256]{1,0:T(8,128)(2,1)S(1)}, u32[]{:S(2)}, u32[]{:S(2)}) collective-permute-start(bf16[384,256]{1,0:T(8,128)(2,1)S(1)} %convert_element_type.69), channel_id=1, source_target_pairs={{0,4},{1,5},{2,6},{3,7},{4,0},{5,1},{6,2},{7,3},{8,12},{9,13},{10,... | collective-permute-start | bytes 589832 | tf_op jit(solution)/shard_map/ppermute | solution.py:128
  25.0 6.1 %collective-permute-start.6 = (bf16[2,128,256]{2,1,0:T(8,128)(2,1)S(1)}, bf16[2,128,256]{2,1,0:T(8,128)(2,1)S(1)}, u32[]{:S(2)}, u32[]{:S(2)}) collective-permute-start(bf16[2,128,256]{2,1,0:T(8,128)(2,1)S(1)} %convolution_convert_fusion.5), channel_id=1, source_target_pairs={{0,1},{1,0},{2,3},{3,2},{4,5},{5,4},{6,7},{7,6},{8,9},{9,8},{10,11... | collective-permute-start | bytes 393224 | tf_op jit(solution)/shard_map/ppermute | solution.py:128
  27.6 8.3 %collective-permute-start.10 = (bf16[2,128,256]{2,1,0:T(8,128)(2,1)S(1)}, bf16[2,128,256]{2,1,0:T(8,128)(2,1)S(1)}, u32[]{:S(2)}, u32[]{:S(2)}) collective-permute-start(bf16[2,128,256]{2,1,0:T(8,128)(2,1)S(1)} %convolution_convert_fusion.1), channel_id=1, source_target_pairs={{0,2},{1,3},{2,0},{3,1},{4,6},{5,7},{6,4},{7,5},{8,10},{9,11},{10,... | collective-permute-start | bytes 393224 | tf_op jit(solution)/shard_map/ppermute | solution.py:128
  29.4 7.1 %collective-permute-start.11 = (bf16[2,128,256]{2,1,0:T(8,128)(2,1)S(1)}, bf16[2,128,256]{2,1,0:T(8,128)(2,1)S(1)}, u32[]{:S(2)}, u32[]{:S(2)}) collective-permute-start(bf16[2,128,256]{2,1,0:T(8,128)(2,1)S(1)} %convolution_convert_fusion), channel_id=1, source_target_pairs={{0,3},{1,2},{2,1},{3,0},{4,7},{5,6},{6,5},{7,4},{8,11},{9,10},{10,... | collective-permute-start | bytes 393224 | tf_op jit(solution)/shard_map/ppermute | solution.py:128
  31.4 9.2 %collective-permute-start.7 = (bf16[2,128,256]{2,1,0:T(8,128)(2,1)S(1)}, bf16[2,128,256]{2,1,0:T(8,128)(2,1)S(1)}, u32[]{:S(2)}, u32[]{:S(2)}) collective-permute-start(bf16[2,128,256]{2,1,0:T(8,128)(2,1)S(1)} %convolution_convert_fusion.4), channel_id=1, source_target_pairs={{0,1},{1,0},{2,3},{3,2},{4,5},{5,4},{6,7},{7,6},{8,9},{9,8},{10,11... | collective-permute-start | bytes 393224 | tf_op jit(solution)/shard_map/ppermute | solution.py:128
  33.7 12.7 %copy-start.3 = (f32[128,256]{1,0:T(8,128)S(1)}, f32[128,256]{1,0:T(8,128)}, u32[]{:S(2)}) copy-start(f32[128,256]{1,0:T(8,128)} %param.9) | copy-start | bytes 393220
  33.7 12.7 %copy-start.4 = (f32[128,256]{1,0:T(8,128)S(1)}, f32[128,256]{1,0:T(8,128)}, u32[]{:S(2)}) copy-start(f32[128,256]{1,0:T(8,128)} %param.8) | copy-start | bytes 393220
  34.0 7.8 %collective-permute-start.8 = (bf16[2,128,256]{2,1,0:T(8,128)(2,1)S(1)}, bf16[2,128,256]{2,1,0:T(8,128)(2,1)S(1)}, u32[]{:S(2)}, u32[]{:S(2)}) collective-permute-start(bf16[2,128,256]{2,1,0:T(8,128)(2,1)S(1)} %convolution_convert_fusion.3), channel_id=1, source_target_pairs={{0,2},{1,3},{2,0},{3,1},{4,6},{5,7},{6,4},{7,5},{8,10},{9,11},{10,... | collective-permute-start | bytes 393224 | tf_op jit(solution)/shard_map/ppermute | solution.py:128
  35.8 6.0 %collective-permute-start.9 = (bf16[2,128,256]{2,1,0:T(8,128)(2,1)S(1)}, bf16[2,128,256]{2,1,0:T(8,128)(2,1)S(1)}, u32[]{:S(2)}, u32[]{:S(2)}) collective-permute-start(bf16[2,128,256]{2,1,0:T(8,128)(2,1)S(1)} %convolution_convert_fusion.2), channel_id=1, source_target_pairs={{0,3},{1,2},{2,1},{3,0},{4,7},{5,6},{6,5},{7,4},{8,11},{9,10},{10,... | collective-permute-start | bytes 393224 | tf_op jit(solution)/shard_map/ppermute | solution.py:128
  36.5 7.0 %collective-permute-start.12 = (bf16[128,256]{1,0:T(8,128)(2,1)S(1)}, bf16[128,256]{1,0:T(8,128)(2,1)S(1)}, u32[]{:S(2)}, u32[]{:S(2)}) collective-permute-start(bf16[128,256]{1,0:T(8,128)(2,1)S(1)} %get-tuple-element.51), channel_id=1, source_target_pairs={{0,16},{1,17},{2,18},{3,19},{4,20},{5,21},{6,22},{7,23},{8,24},{9,... | collective-permute-start | bytes 196616 | tf_op jit(solution)/shard_map/ppermute | solution.py:128
  39.2 6.8 %collective-permute-start.14 = (bf16[128,256]{1,0:T(8,128)(2,1)S(1)}, bf16[128,256]{1,0:T(8,128)(2,1)S(1)}, u32[]{:S(2)}, u32[]{:S(2)}) collective-permute-start(bf16[128,256]{1,0:T(8,128)(2,1)S(1)} %get-tuple-element.52), channel_id=1, source_target_pairs={{0,24},{1,25},{2,26},{3,27},{4,28},{5,29},{6,30},{7,31},{8,16},{9,... | collective-permute-start | bytes 196616 | tf_op jit(solution)/shard_map/ppermute | solution.py:128
  41.9 4.5 %collective-permute-start.13 = (bf16[128,256]{1,0:T(8,128)(2,1)S(1)}, bf16[128,256]{1,0:T(8,128)(2,1)S(1)}, u32[]{:S(2)}, u32[]{:S(2)}) collective-permute-start(bf16[128,256]{1,0:T(8,128)(2,1)S(1)} %fusion.20), channel_id=1, source_target_pairs={{0,8},{1,9},{2,10},{3,11},{4,12},{5,13},{6,14},{7,15},{8,0},{9,1},... | collective-permute-start | bytes 196616 | tf_op jit(solution)/shard_map/ppermute | solution.py:128
  46.6 5.2 %collective-permute-start.15 = (bf16[128,256]{1,0:T(8,128)(2,1)S(1)}, bf16[128,256]{1,0:T(8,128)(2,1)S(1)}, u32[]{:S(2)}, u32[]{:S(2)}) collective-permute-start(bf16[128,256]{1,0:T(8,128)(2,1)S(1)} %get-tuple-element.35.refs_0_), channel_id=1, source_target_pairs={{0,3},{1,2},{2,1},{3,0},{4,7},{5,6},{6,5},{7,4},{8,11},{9,10},{10,... | collective-permute-start | bytes 196616 | tf_op jit(solution)/shard_map/ppermute | solution.py:128
  48.4 4.3 %collective-permute-start.16 = (bf16[128,256]{1,0:T(8,128)(2,1)S(1)}, bf16[128,256]{1,0:T(8,128)(2,1)S(1)}, u32[]{:S(2)}, u32[]{:S(2)}) collective-permute-start(bf16[128,256]{1,0:T(8,128)(2,1)S(1)} %get-tuple-element.35.refs_0_), channel_id=1, source_target_pairs={{0,2},{1,3},{2,0},{3,1},{4,6},{5,7},{6,4},{7,5},{8,10},{9,11},{10,... | collective-permute-start | bytes 196616 | tf_op jit(solution)/shard_map/ppermute | solution.py:128
  49.0 4.3 %collective-permute-start.17 = (bf16[128,256]{1,0:T(8,128)(2,1)S(1)}, bf16[128,256]{1,0:T(8,128)(2,1)S(1)}, u32[]{:S(2)}, u32[]{:S(2)}) collective-permute-start(bf16[128,256]{1,0:T(8,128)(2,1)S(1)} %get-tuple-element.35.refs_0_), channel_id=1, source_target_pairs={{0,1},{1,0},{2,3},{3,2},{4,5},{5,4},{6,7},{7,6},{8,9},{9,8},{10,11... | collective-permute-start | bytes 196616 | tf_op jit(solution)/shard_map/ppermute | solution.py:128

commit v6 on v5

--- a/solution.py
+++ b/solution.py
@@ -71,17 +71,18 @@
     )(order, own, other)
 
 
-def update_kernel(tiles, masks, place, first, second, *refs):
+def update_kernel(tiles, places, first, second, *refs):
     steps, (out, step, held, sem) = refs[:-4], refs[-4:]
+    core, owners = places()
     half, rows = first.shape[0], steps[0].shape[0]
-    for mask, block in zip(masks, steps):
-        step[pl.ds(pl.multiple_of((place[0] ^ mask) * rows, rows), rows), :] = block[...]
+    for index, block in enumerate(steps):
+        step[pl.ds(pl.multiple_of(owners[index] * rows, rows), rows), :] = block[...]
     turned, tile, copies = step[...].T, half // tiles, []
     for side, basis in enumerate((first, second)):
         for index in range(tiles):
             part = pl.ds(index * tile, tile)
             held[side, part, :] = (16.0 * dot(basis[part, :], turned)).astype(out.dtype)
-            begin = pl.multiple_of((place[1] ^ side) * half + index * tile, tile)
+            begin = pl.multiple_of((core ^ side) * half + index * tile, tile)
             copies.append(
                 pltpu.make_async_copy(held.at[side, part, :], out.at[pl.ds(begin, tile), :], sem.at[len(copies)])
             )
@@ -90,19 +91,20 @@
         copy.wait()
 
 
-def update_of(first, second, steps, masks, here, core):
+def update_of(first, second, steps, places):
     half, (rows, rank) = first.shape[0], steps[0].shape
     if rows % 128:
+        core, owners = places()
         step = jnp.zeros((len(steps), rows, rank), jnp.bfloat16)
-        step = step.at[jnp.array(masks) ^ here].set(jnp.stack(steps)).reshape(-1, rank)
+        step = step.at[jnp.stack(owners)].set(jnp.stack(steps)).reshape(-1, rank)
         basis = jnp.where(core == 0, jnp.concatenate([first, second]), jnp.concatenate([second, first]))
         return (16.0 * dot(basis, step.T)).astype(jnp.bfloat16)
     tiles = 4
     inputs = [pltpu.with_memory_space_constraint(value, pltpu.VMEM) for value in [first, second] + steps]
     return pl.pallas_call(
-        functools.partial(update_kernel, tiles, masks),
+        functools.partial(update_kernel, tiles, places),
         out_shape=jax.ShapeDtypeStruct((2 * half, len(steps) * rows), jnp.bfloat16),
-        in_specs=[pl.BlockSpec(memory_space=pltpu.SMEM)] + [pl.BlockSpec(memory_space=pltpu.VMEM)] * len(inputs),
+        in_specs=[pl.BlockSpec(memory_space=pltpu.VMEM)] * len(inputs),
         out_specs=ANY,
         scratch_shapes=[
             pltpu.VMEM((len(steps) * rows, rank), jnp.bfloat16),
@@ -111,7 +113,7 @@
         ],
         name="update",
         compiler_params=SMALL,
-    )(jnp.stack([here, core]), *inputs)
+    )(*inputs)
 
 
 def solution(mesh):
@@ -151,9 +153,16 @@
             parts[1], shared[1] = lax.optimization_barrier((parts[1], shared[1]))
             parts.append(swap(parts[1], across_fsdp=(2, 1)))
 
-        owners = (
-            ((jnp.arange(pairs) ^ pair) * 2 + core)[:, None] * fsdp + (jnp.arange(fsdp) ^ here)[None, :]
-        )
+        hops = {k: (k, k) for k in range(1, fsdp)}
+        if fsdp == 4:
+            hops[1], hops[2] = (1, 2), (2, 1)
+
+        def home(here, core, k):
+            first, second = hops.get(k, (0, 0))
+            return here ^ (first + core * (second - first))
+
+        homes = [home(here, core, k) for k in range(fsdp)]
+        owners = ((jnp.arange(pairs) ^ pair) * 2 + core)[:, None] * fsdp + jnp.stack(homes)[None, :]
         owners = owners.reshape(2, pairs // 2, fsdp).swapaxes(1, 2).reshape(-1)
         other, parts[1] = lax.optimization_barrier((swap(cotangent, across_core=1), parts[1]))
         features = turn(cotangent, other, owners, rows)
@@ -174,7 +183,7 @@
         arrivals, arrived, plane, value = [], {}, {}, projected
         for side in (1, 0):
             terms = {k: term(side, k, value).astype(jnp.bfloat16) for k in masks}
-            arrived[side] = {k: swap(v, across_fsdp=(k, k)) for k, v in terms.items()}
+            arrived[side] = {k: swap(v, across_fsdp=hops[k]) for k, v in terms.items()}
             value, arrived[side][1] = lax.optimization_barrier((value, arrived[side][1]))
         for side in (0, 1):
             plane[side] = term(side, 0, projected)
@@ -196,8 +205,14 @@
         step = (new_first / bias_one / (jnp.sqrt(new_second / bias_two) + 1e-08)).astype(jnp.bfloat16)
         step, kept = lax.optimization_barrier((step, grad))
         new_first, new_second = moments(kept)
-        steps = {k: swap(step, across_fsdp=(k, k)) for k in masks}
-        update = update_of(part, rest, [step] + [steps[k] for k in masks[::-1]], [0, *masks[::-1]], here, core)
+        steps = {k: swap(step, across_fsdp=hops[k]) for k in masks}
+        late = [0, *masks[::-1]]
+
+        def places():
+            here, core = lax.axis_index("fsdp"), lax.rem(lax.axis_index("dp"), 2)
+            return core, [home(here, core, k) for k in late]
+
+        update = update_of(part, rest, [step] + [steps[k] for k in late[1:]], places)
         return (update, new_first, new_second)
 
     in_specs = (

time: 55.7 us -> 55.2 us (level)
  waiting for transfers between devices: 17.7 us -> 16.5 us
  starting transfers between devices: 23.4 us -> 24.5 us
    ppermute x18, waiting for transfers between devices: 17.7 us -> 16.5 us  [swap(): return lax.ppermute(value, ('dp', 'fsdp'), steps)]
    ppermute x18, starting transfers between devices: 23.4 us -> 24.5 us  [swap(): return lax.ppermute(value, ('dp', 'fsdp'), steps)]
  transfers between devices with their start and end apart: 18 -> 18, of which waited for: 13 -> 14; matrix products, arithmetic and copies ran while one was open for 7% -> 7% of each run, Pallas kernels for 7% -> 7%
where the time goes in v6:
time: 55.2 us; the launch traced here: 54.9 us
  starting transfers between devices  24.5 us (44%)
  waiting for transfers between devices  16.5 us (30%)
  Pallas kernels  5.58 us (10%)
  matrix products  3.26 us (6%)
  local copies, waits for them, and re-layouts  2.87 us (5%)
  other arithmetic  1.35 us (2%)
  between operations  0.84 us (2%)
    ppermute x18, starting transfers between devices, swap(): return lax.ppermute(value, ('dp', 'fsdp'), steps)  24.5 us
    ppermute x18, waiting for transfers between devices, swap(): return lax.ppermute(value, ('dp', 'fsdp'), steps)  16.5 us
    dot_general x12, matrix products, dot(): return jnp.dot(a, b, preferred_element_type=jnp.float32)  3.26 us
    unnamed x10, local copies, waits for them, and re-layouts  2.52 us
    pallas_call x1, Pallas kernels, pack(): pl.pallas_call(functools.partial(pack_kernel, tokens), out_shape=[pltpu.V...  2.03 us
    pallas_call x1, Pallas kernels, turn(): pl.pallas_call(functools.partial(turn_kernel, rows), out_shape=pltpu.VMEM...  1.88 us
    pallas_call x1, Pallas kernels, update_of(): pl.pallas_call(functools.partial(update_kernel, tiles, places), out_shape...  1.66 us
  transfers between devices with their start and end apart: 18, of which 14 were waited for; matrix products, arithmetic and copies ran while one was open for 7% of the time, Pallas kernels for 7%

profile of v6, /device:TPU:0, one launch (start us, length us, event | category | flops | bytes accessed | tf_op | source)
XLA Modules:
  0.0 54.9 jit_solution(6035805870801105174)
XLA Ops:
  0.6 0.5 collective-permute-start
  1.2 0.6 %copy-done = bf16[2048,256]{1,0:T(8,128)(2,1)S(1)} copy-done((bf16[2048,256]{1,0:T(8,128)(2,1)S(1)}, bf16[2048,256]{1,0:T(8,128)(2,1)}, u32[]{:S(2)}) %copy-start) | copy-done | bytes 1048600
  1.9 3.0 %collective-permute-start.2 = (bf16[1024,256]{1,0:T(8,128)(2,1)S(1)}, bf16[1024,256]{1,0:T(8,128)(2,1)S(1)}, u32[]{:S(2)}, u32[]{:S(2)}) collective-permute-start(bf16[1024,256]{1,0:T(8,128)(2,1)S(1)} %constant_dynamic-slice_fusion.1.first), channel_id=1, source_target_pairs={{0,1},{1,0},{2,3},{3,2},{4,6},{5,7},{6,4},{7,5},{8,9},{9,8},{10,11... | collective-permute-start | bytes 1572872 | tf_op jit(solution)/shard_map/ppermute | solution.py:130
  5.4 1.4 %collective-permute-done.other = bf16[192,8192]{1,0:T(8,128)(2,1)} collective-permute-done((bf16[192,8192]{1,0:T(8,128)(2,1)}, bf16[192,8192]{1,0:T(8,128)(2,1)}, u32[]{:S(2)}, u32[]{:S(2)}) %collective-permute-start) | collective-permute-done | bytes 3145760 | tf_op jit(solution)/shard_map/ppermute | solution.py:130
  6.8 1.9 %copy-done.1 = bf16[192,8192]{1,0:T(8,128)(2,1)S(1)} copy-done((bf16[192,8192]{1,0:T(8,128)(2,1)S(1)}, bf16[192,8192]{1,0:T(8,128)(2,1)}, u32[]{:S(2)}) %copy-start.1) | copy-done | bytes 3145752
  8.7 2.0 %pack_activations.1 = (bf16[384,1024]{1,0:T(8,128)(2,1)S(1)}, bf16[384,1024]{1,0:T(8,128)(2,1)S(1)}, bf16[384,1024]{1,0:T(8,128)(2,1)S(1)}, bf16[384,1024]{1,0:T(8,128)(2,1)S(1)}) custom-call(s32[4]{0:T(128)S(1)} %pad_add_fusion.starts, bf16[192,8192]{1,0:T(8,128)(2,1)S(1)} %copy-done.1, bf16[192,8192]{1,0:T(8,128)(2,1)} %collective-permute-done.other), custom_call_target="tpu_custom_call" | custom-call | tf_op jit(solution)/shard_map/pack_activations/pallas_call | solution.py:42
  10.7 1.3 %collective-permute-done.2 = bf16[1024,256]{1,0:T(8,128)(2,1)S(1)} collective-permute-done((bf16[1024,256]{1,0:T(8,128)(2,1)S(1)}, bf16[1024,256]{1,0:T(8,128)(2,1)S(1)}, u32[]{:S(2)}, u32[]{:S(2)}) %collective-permute-start.2) | collective-permute-done | bytes 524320 | tf_op jit(solution)/shard_map/ppermute | solution.py:130
  12.1 2.0 %collective-permute-start.4 = (bf16[1024,256]{1,0:T(8,128)(2,1)S(1)}, bf16[1024,256]{1,0:T(8,128)(2,1)S(1)}, u32[]{:S(2)}, u32[]{:S(2)}) collective-permute-start(bf16[1024,256]{1,0:T(8,128)(2,1)S(1)} %collective-permute-done.2), channel_id=1, source_target_pairs={{0,2},{1,3},{2,0},{3,1},{4,5},{5,4},{6,7},{7,6},{8,10},{9,11},{10,... | collective-permute-start | bytes 1572872 | tf_op jit(solution)/shard_map/ppermute | solution.py:130
  14.1 1.9 %turn_cotangent.1 = bf16[16,128,384]{2,1,0:T(8,128)(2,1)S(1)} custom-call(s32[16]{0:T(128)S(1)} %add.132.order, bf16[192,4096]{1,0:T(8,128)(2,1)S(1)} %copy-done.2, bf16[192,4096]{1,0:T(8,128)(2,1)} %collective-permute-done.1.other), custom_call_target="tpu_custom_call" | custom-call | tf_op jit(solution)/shard_map/turn_cotangent/pallas_call | solution.py:64
  16.8 3.9 %collective-permute-done.3 = bf16[1024,256]{1,0:T(8,128)(2,1)S(1)} collective-permute-done((bf16[1024,256]{1,0:T(8,128)(2,1)S(1)}, bf16[1024,256]{1,0:T(8,128)(2,1)S(1)}, u32[]{:S(2)}, u32[]{:S(2)}) %collective-permute-start.3) | collective-permute-done | bytes 524320 | tf_op jit(solution)/shard_map/ppermute | solution.py:130
  21.0 1.4 %collective-permute-done.4 = bf16[1024,256]{1,0:T(8,128)(2,1)S(1)} collective-permute-done((bf16[1024,256]{1,0:T(8,128)(2,1)S(1)}, bf16[1024,256]{1,0:T(8,128)(2,1)S(1)}, u32[]{:S(2)}, u32[]{:S(2)}) %collective-permute-start.4) | collective-permute-done | bytes 524320 | tf_op jit(solution)/shard_map/ppermute | solution.py:130
  23.0 0.7 %collective-permute-start.5 = (bf16[384,256]{1,0:T(8,128)(2,1)S(1)}, bf16[384,256]{1,0:T(8,128)(2,1)S(1)}, u32[]{:S(2)}, u32[]{:S(2)}) collective-permute-start(bf16[384,256]{1,0:T(8,128)(2,1)S(1)} %convert_element_type.69), channel_id=1, source_target_pairs={{0,4},{1,5},{2,6},{3,7},{4,0},{5,1},{6,2},{7,3},{8,12},{9,13},{10,... | collective-permute-start | bytes 589832 | tf_op jit(solution)/shard_map/ppermute | solution.py:130
  23.8 0.9 %collective-permute-done.5 = bf16[384,256]{1,0:T(8,128)(2,1)S(1)} collective-permute-done((bf16[384,256]{1,0:T(8,128)(2,1)S(1)}, bf16[384,256]{1,0:T(8,128)(2,1)S(1)}, u32[]{:S(2)}, u32[]{:S(2)}) %collective-permute-start.5) | collective-permute-done | bytes 196640 | tf_op jit(solution)/shard_map/ppermute | solution.py:130
  25.0 2.1 %collective-permute-start.6 = (bf16[2,128,256]{2,1,0:T(8,128)(2,1)S(1)}, bf16[2,128,256]{2,1,0:T(8,128)(2,1)S(1)}, u32[]{:S(2)}, u32[]{:S(2)}) collective-permute-start(bf16[2,128,256]{2,1,0:T(8,128)(2,1)S(1)} %convolution_convert_fusion.5), channel_id=1, source_target_pairs={{0,1},{1,0},{2,3},{3,2},{4,6},{5,7},{6,4},{7,5},{8,9},{9,8},{10,11... | collective-permute-start | bytes 393224 | tf_op jit(solution)/shard_map/ppermute | solution.py:130
  27.6 1.6 %collective-permute-start.10 = (bf16[2,128,256]{2,1,0:T(8,128)(2,1)S(1)}, bf16[2,128,256]{2,1,0:T(8,128)(2,1)S(1)}, u32[]{:S(2)}, u32[]{:S(2)}) collective-permute-start(bf16[2,128,256]{2,1,0:T(8,128)(2,1)S(1)} %convolution_convert_fusion.1), channel_id=1, source_target_pairs={{0,2},{1,3},{2,0},{3,1},{4,5},{5,4},{6,7},{7,6},{8,10},{9,11},{10,... | collective-permute-start | bytes 393224 | tf_op jit(solution)/shard_map/ppermute | solution.py:130
  30.3 2.3 %collective-permute-start.7 = (bf16[2,128,256]{2,1,0:T(8,128)(2,1)S(1)}, bf16[2,128,256]{2,1,0:T(8,128)(2,1)S(1)}, u32[]{:S(2)}, u32[]{:S(2)}) collective-permute-start(bf16[2,128,256]{2,1,0:T(8,128)(2,1)S(1)} %convolution_convert_fusion.4), channel_id=1, source_target_pairs={{0,1},{1,0},{2,3},{3,2},{4,6},{5,7},{6,4},{7,5},{8,9},{9,8},{10,11... | collective-permute-start | bytes 393224 | tf_op jit(solution)/shard_map/ppermute | solution.py:130
  32.8 2.6 %collective-permute-start.8 = (bf16[2,128,256]{2,1,0:T(8,128)(2,1)S(1)}, bf16[2,128,256]{2,1,0:T(8,128)(2,1)S(1)}, u32[]{:S(2)}, u32[]{:S(2)}) collective-permute-start(bf16[2,128,256]{2,1,0:T(8,128)(2,1)S(1)} %convolution_convert_fusion.3), channel_id=1, source_target_pairs={{0,2},{1,3},{2,0},{3,1},{4,5},{5,4},{6,7},{7,6},{8,10},{9,11},{10,... | collective-permute-start | bytes 393224 | tf_op jit(solution)/shard_map/ppermute | solution.py:130
  35.9 1.0 %collective-permute-done.11 = bf16[2,128,256]{2,1,0:T(8,128)(2,1)S(1)} collective-permute-done((bf16[2,128,256]{2,1,0:T(8,128)(2,1)S(1)}, bf16[2,128,256]{2,1,0:T(8,128)(2,1)S(1)}, u32[]{:S(2)}, u32[]{:S(2)}) %collective-permute-start.11) | collective-permute-done | bytes 131104 | tf_op jit(solution)/shard_map/ppermute | solution.py:130
  36.9 2.6 %collective-permute-start.12 = (bf16[128,256]{1,0:T(8,128)(2,1)S(1)}, bf16[128,256]{1,0:T(8,128)(2,1)S(1)}, u32[]{:S(2)}, u32[]{:S(2)}) collective-permute-start(bf16[128,256]{1,0:T(8,128)(2,1)S(1)} %get-tuple-element.51), channel_id=1, source_target_pairs={{0,16},{1,17},{2,18},{3,19},{4,20},{5,21},{6,22},{7,23},{8,24},{9,... | collective-permute-start | bytes 196616 | tf_op jit(solution)/shard_map/ppermute | solution.py:130
  39.6 1.3 %collective-permute-start.14 = (bf16[128,256]{1,0:T(8,128)(2,1)S(1)}, bf16[128,256]{1,0:T(8,128)(2,1)S(1)}, u32[]{:S(2)}, u32[]{:S(2)}) collective-permute-start(bf16[128,256]{1,0:T(8,128)(2,1)S(1)} %get-tuple-element.52), channel_id=1, source_target_pairs={{0,24},{1,25},{2,26},{3,27},{4,28},{5,29},{6,30},{7,31},{8,16},{9,... | collective-permute-start | bytes 196616 | tf_op jit(solution)/shard_map/ppermute | solution.py:130
  40.9 0.7 %collective-permute-done.9 = bf16[2,128,256]{2,1,0:T(8,128)(2,1)S(1)} collective-permute-done((bf16[2,128,256]{2,1,0:T(8,128)(2,1)S(1)}, bf16[2,128,256]{2,1,0:T(8,128)(2,1)S(1)}, u32[]{:S(2)}, u32[]{:S(2)}) %collective-permute-start.9) | collective-permute-done | bytes 131104 | tf_op jit(solution)/shard_map/ppermute | solution.py:130
  41.7 1.6 %collective-permute-start.13 = (bf16[128,256]{1,0:T(8,128)(2,1)S(1)}, bf16[128,256]{1,0:T(8,128)(2,1)S(1)}, u32[]{:S(2)}, u32[]{:S(2)}) collective-permute-start(bf16[128,256]{1,0:T(8,128)(2,1)S(1)} %fusion.20), channel_id=1, source_target_pairs={{0,8},{1,9},{2,10},{3,11},{4,12},{5,13},{6,14},{7,15},{8,0},{9,1},... | collective-permute-start | bytes 196616 | tf_op jit(solution)/shard_map/ppermute | solution.py:130
  43.3 0.4 collective-permute-done.12
  43.8 2.3 %collective-permute-done.14 = bf16[128,256]{1,0:T(8,128)(2,1)S(1)} collective-permute-done((bf16[128,256]{1,0:T(8,128)(2,1)S(1)}, bf16[128,256]{1,0:T(8,128)(2,1)S(1)}, u32[]{:S(2)}, u32[]{:S(2)}) %collective-permute-start.14) | collective-permute-done | bytes 65568 | tf_op jit(solution)/shard_map/ppermute | solution.py:130
  46.7 1.8 %collective-permute-start.15 = (bf16[128,256]{1,0:T(8,128)(2,1)S(1)}, bf16[128,256]{1,0:T(8,128)(2,1)S(1)}, u32[]{:S(2)}, u32[]{:S(2)}) collective-permute-start(bf16[128,256]{1,0:T(8,128)(2,1)S(1)} %get-tuple-element.35.refs_0_), channel_id=1, source_target_pairs={{0,3},{1,2},{2,1},{3,0},{4,7},{5,6},{6,5},{7,4},{8,11},{9,10},{10,... | collective-permute-start | bytes 196616 | tf_op jit(solution)/shard_map/ppermute | solution.py:130
  48.4 0.6 %collective-permute-start.16 = (bf16[128,256]{1,0:T(8,128)(2,1)S(1)}, bf16[128,256]{1,0:T(8,128)(2,1)S(1)}, u32[]{:S(2)}, u32[]{:S(2)}) collective-permute-start(bf16[128,256]{1,0:T(8,128)(2,1)S(1)} %get-tuple-element.35.refs_0_), channel_id=1, source_target_pairs={{0,2},{1,3},{2,0},{3,1},{4,5},{5,4},{6,7},{7,6},{8,10},{9,11},{10,... | collective-permute-start | bytes 196616 | tf_op jit(solution)/shard_map/ppermute | solution.py:130
  49.0 1.2 %collective-permute-start.17 = (bf16[128,256]{1,0:T(8,128)(2,1)S(1)}, bf16[128,256]{1,0:T(8,128)(2,1)S(1)}, u32[]{:S(2)}, u32[]{:S(2)}) collective-permute-start(bf16[128,256]{1,0:T(8,128)(2,1)S(1)} %get-tuple-element.35.refs_0_), channel_id=1, source_target_pairs={{0,1},{1,0},{2,3},{3,2},{4,6},{5,7},{6,4},{7,5},{8,9},{9,8},{10,11... | collective-permute-start | bytes 196616 | tf_op jit(solution)/shard_map/ppermute | solution.py:130
  50.2 0.7 %fusion.15 = (f32[128,256]{1,0:T(8,128)}, f32[128,256]{1,0:T(8,128)}) fusion(f32[128,256]{1,0:T(8,128)S(1)} %get-tuple-element.36, f32[128,256]{1,0:T(8,128)S(1)} %copy-done.3, f32[128,256]{1,0:T(8,128)S(1)} %copy-done.4), kind=kLoop, calls=%fused_computation.28 | loop fusion | flops 229376 | bytes 655360 | tf_op jit(solution)/shard_map/add | solution.py:200
  51.0 0.9 %collective-permute-done.15.refs_1_ = bf16[128,256]{1,0:T(8,128)(2,1)S(1)} collective-permute-done((bf16[128,256]{1,0:T(8,128)(2,1)S(1)}, bf16[128,256]{1,0:T(8,128)(2,1)S(1)}, u32[]{:S(2)}, u32[]{:S(2)}) %collective-permute-start.15) | collective-permute-done | bytes 65568 | tf_op jit(solution)/shard_map/ppermute | solution.py:130
  51.9 0.8 %collective-permute-done.16.refs_2_ = bf16[128,256]{1,0:T(8,128)(2,1)S(1)} collective-permute-done((bf16[128,256]{1,0:T(8,128)(2,1)S(1)}, bf16[128,256]{1,0:T(8,128)(2,1)S(1)}, u32[]{:S(2)}, u32[]{:S(2)}) %collective-permute-start.16) | collective-permute-done | bytes 65568 | tf_op jit(solution)/shard_map/ppermute | solution.py:130
  52.7 0.6 %collective-permute-done.17.refs_3_ = bf16[128,256]{1,0:T(8,128)(2,1)S(1)} collective-permute-done((bf16[128,256]{1,0:T(8,128)(2,1)S(1)}, bf16[128,256]{1,0:T(8,128)(2,1)S(1)}, u32[]{:S(2)}, u32[]{:S(2)}) %collective-permute-start.17) | collective-permute-done | bytes 65568 | tf_op jit(solution)/shard_map/ppermute | solution.py:130
  53.3 1.7 %update.1 = bf16[2048,512]{1,0:T(8,128)(2,1)} custom-call(bf16[1024,256]{1,0:T(8,128)(2,1)S(1)} %constant_dynamic-slice_fusion.1.first, bf16[1024,256]{1,0:T(8,128)(2,1)S(1)} %constant_dynamic-slice_fusion.second, bf16[128,256]{1,0:T(8,128)(2,1)S(1)} %get-tuple-element.35.refs_0_, bf16[128,256]{1,0:T(8,128)(2,1)S(1)} %collective-permute-done.15.refs_1_, ...), custom_call_target="tpu_custom_call" | custom-call | tf_op jit(solution)/shard_map/update/pallas_call | solution.py:104
  (47 shorter events, 5.5 us)
Async XLA Ops:
  0.6 1.2 %copy-start = (bf16[2048,256]{1,0:T(8,128)(2,1)S(1)}, bf16[2048,256]{1,0:T(8,128)(2,1)}, u32[]{:S(2)}) copy-start(bf16[2048,256]{1,0:T(8,128)(2,1)} %param.7) | copy-start | bytes 3145732
  0.6 6.1 %collective-permute-start = (bf16[192,8192]{1,0:T(8,128)(2,1)}, bf16[192,8192]{1,0:T(8,128)(2,1)}, u32[]{:S(2)}, u32[]{:S(2)}) collective-permute-start(bf16[192,8192]{1,0:T(8,128)(2,1)} %own.2), channel_id=1, source_target_pairs={{0,4},{1,5},{2,6},{3,7},{4,0},{5,1},{6,2},{7,3},{8,12},{9,13},{10,... | collective-permute-start | bytes 9437192 | tf_op jit(solution)/shard_map/ppermute | solution.py:130
  1.2 13.0 %collective-permute-start.1 = (bf16[192,4096]{1,0:T(8,128)(2,1)}, bf16[192,4096]{1,0:T(8,128)(2,1)}, u32[]{:S(2)}, u32[]{:S(2)}) collective-permute-start(bf16[192,4096]{1,0:T(8,128)(2,1)} %own.3), channel_id=1, source_target_pairs={{0,4},{1,5},{2,6},{3,7},{4,0},{5,1},{6,2},{7,3},{8,12},{9,13},{10,... | collective-permute-start | bytes 4718600 | tf_op jit(solution)/shard_map/ppermute | solution.py:130
  1.9 10.2 %collective-permute-start.2 = (bf16[1024,256]{1,0:T(8,128)(2,1)S(1)}, bf16[1024,256]{1,0:T(8,128)(2,1)S(1)}, u32[]{:S(2)}, u32[]{:S(2)}) collective-permute-start(bf16[1024,256]{1,0:T(8,128)(2,1)S(1)} %constant_dynamic-slice_fusion.1.first), channel_id=1, source_target_pairs={{0,1},{1,0},{2,3},{3,2},{4,6},{5,7},{6,4},{7,5},{8,9},{9,8},{10,11... | collective-permute-start | bytes 1572872 | tf_op jit(solution)/shard_map/ppermute | solution.py:130
  4.9 15.7 %collective-permute-start.3 = (bf16[1024,256]{1,0:T(8,128)(2,1)S(1)}, bf16[1024,256]{1,0:T(8,128)(2,1)S(1)}, u32[]{:S(2)}, u32[]{:S(2)}) collective-permute-start(bf16[1024,256]{1,0:T(8,128)(2,1)S(1)} %constant_dynamic-slice_fusion.second), channel_id=1, source_target_pairs={{0,1},{1,0},{2,3},{3,2},{4,6},{5,7},{6,4},{7,5},{8,9},{9,8},{10,11... | collective-permute-start | bytes 1572872 | tf_op jit(solution)/shard_map/ppermute | solution.py:130
  6.8 1.9 %copy-start.1 = (bf16[192,8192]{1,0:T(8,128)(2,1)S(1)}, bf16[192,8192]{1,0:T(8,128)(2,1)}, u32[]{:S(2)}) copy-start(bf16[192,8192]{1,0:T(8,128)(2,1)} %own.2) | copy-start | bytes 9437188
  8.7 5.4 %copy-start.2 = (bf16[192,4096]{1,0:T(8,128)(2,1)S(1)}, bf16[192,4096]{1,0:T(8,128)(2,1)}, u32[]{:S(2)}) copy-start(bf16[192,4096]{1,0:T(8,128)(2,1)} %own.3) | copy-start | bytes 4718596
  12.1 10.4 %collective-permute-start.4 = (bf16[1024,256]{1,0:T(8,128)(2,1)S(1)}, bf16[1024,256]{1,0:T(8,128)(2,1)S(1)}, u32[]{:S(2)}, u32[]{:S(2)}) collective-permute-start(bf16[1024,256]{1,0:T(8,128)(2,1)S(1)} %collective-permute-done.2), channel_id=1, source_target_pairs={{0,2},{1,3},{2,0},{3,1},{4,5},{5,4},{6,7},{7,6},{8,10},{9,11},{10,... | collective-permute-start | bytes 1572872 | tf_op jit(solution)/shard_map/ppermute | solution.py:130
  23.0 1.8 %collective-permute-start.5 = (bf16[384,256]{1,0:T(8,128)(2,1)S(1)}, bf16[384,256]{1,0:T(8,128)(2,1)S(1)}, u32[]{:S(2)}, u32[]{:S(2)}) collective-permute-start(bf16[384,256]{1,0:T(8,128)(2,1)S(1)} %convert_element_type.69), channel_id=1, source_target_pairs={{0,4},{1,5},{2,6},{3,7},{4,0},{5,1},{6,2},{7,3},{8,12},{9,13},{10,... | collective-permute-start | bytes 589832 | tf_op jit(solution)/shard_map/ppermute | solution.py:130
  25.0 5.0 %collective-permute-start.6 = (bf16[2,128,256]{2,1,0:T(8,128)(2,1)S(1)}, bf16[2,128,256]{2,1,0:T(8,128)(2,1)S(1)}, u32[]{:S(2)}, u32[]{:S(2)}) collective-permute-start(bf16[2,128,256]{2,1,0:T(8,128)(2,1)S(1)} %convolution_convert_fusion.5), channel_id=1, source_target_pairs={{0,1},{1,0},{2,3},{3,2},{4,6},{5,7},{6,4},{7,5},{8,9},{9,8},{10,11... | collective-permute-start | bytes 393224 | tf_op jit(solution)/shard_map/ppermute | solution.py:130
  27.6 8.3 %collective-permute-start.10 = (bf16[2,128,256]{2,1,0:T(8,128)(2,1)S(1)}, bf16[2,128,256]{2,1,0:T(8,128)(2,1)S(1)}, u32[]{:S(2)}, u32[]{:S(2)}) collective-permute-start(bf16[2,128,256]{2,1,0:T(8,128)(2,1)S(1)} %convolution_convert_fusion.1), channel_id=1, source_target_pairs={{0,2},{1,3},{2,0},{3,1},{4,5},{5,4},{6,7},{7,6},{8,10},{9,11},{10,... | collective-permute-start | bytes 393224 | tf_op jit(solution)/shard_map/ppermute | solution.py:130
  29.4 7.4 %collective-permute-start.11 = (bf16[2,128,256]{2,1,0:T(8,128)(2,1)S(1)}, bf16[2,128,256]{2,1,0:T(8,128)(2,1)S(1)}, u32[]{:S(2)}, u32[]{:S(2)}) collective-permute-start(bf16[2,128,256]{2,1,0:T(8,128)(2,1)S(1)} %convolution_convert_fusion), channel_id=1, source_target_pairs={{0,3},{1,2},{2,1},{3,0},{4,7},{5,6},{6,5},{7,4},{8,11},{9,10},{10,... | collective-permute-start | bytes 393224 | tf_op jit(solution)/shard_map/ppermute | solution.py:130
  30.3 10.6 %collective-permute-start.7 = (bf16[2,128,256]{2,1,0:T(8,128)(2,1)S(1)}, bf16[2,128,256]{2,1,0:T(8,128)(2,1)S(1)}, u32[]{:S(2)}, u32[]{:S(2)}) collective-permute-start(bf16[2,128,256]{2,1,0:T(8,128)(2,1)S(1)} %convolution_convert_fusion.4), channel_id=1, source_target_pairs={{0,1},{1,0},{2,3},{3,2},{4,6},{5,7},{6,4},{7,5},{8,9},{9,8},{10,11... | collective-permute-start | bytes 393224 | tf_op jit(solution)/shard_map/ppermute | solution.py:130
  32.6 13.9 %copy-start.3 = (f32[128,256]{1,0:T(8,128)S(1)}, f32[128,256]{1,0:T(8,128)}, u32[]{:S(2)}) copy-start(f32[128,256]{1,0:T(8,128)} %param.9) | copy-start | bytes 393220
  32.6 13.9 %copy-start.4 = (f32[128,256]{1,0:T(8,128)S(1)}, f32[128,256]{1,0:T(8,128)}, u32[]{:S(2)}) copy-start(f32[128,256]{1,0:T(8,128)} %param.8) | copy-start | bytes 393220
  32.8 8.1 %collective-permute-start.8 = (bf16[2,128,256]{2,1,0:T(8,128)(2,1)S(1)}, bf16[2,128,256]{2,1,0:T(8,128)(2,1)S(1)}, u32[]{:S(2)}, u32[]{:S(2)}) collective-permute-start(bf16[2,128,256]{2,1,0:T(8,128)(2,1)S(1)} %convolution_convert_fusion.3), channel_id=1, source_target_pairs={{0,2},{1,3},{2,0},{3,1},{4,5},{5,4},{6,7},{7,6},{8,10},{9,11},{10,... | collective-permute-start | bytes 393224 | tf_op jit(solution)/shard_map/ppermute | solution.py:130
  35.7 5.9 %collective-permute-start.9 = (bf16[2,128,256]{2,1,0:T(8,128)(2,1)S(1)}, bf16[2,128,256]{2,1,0:T(8,128)(2,1)S(1)}, u32[]{:S(2)}, u32[]{:S(2)}) collective-permute-start(bf16[2,128,256]{2,1,0:T(8,128)(2,1)S(1)} %convolution_convert_fusion.2), channel_id=1, source_target_pairs={{0,3},{1,2},{2,1},{3,0},{4,7},{5,6},{6,5},{7,4},{8,11},{9,10},{10,... | collective-permute-start | bytes 393224 | tf_op jit(solution)/shard_map/ppermute | solution.py:130
  36.9 6.8 %collective-permute-start.12 = (bf16[128,256]{1,0:T(8,128)(2,1)S(1)}, bf16[128,256]{1,0:T(8,128)(2,1)S(1)}, u32[]{:S(2)}, u32[]{:S(2)}) collective-permute-start(bf16[128,256]{1,0:T(8,128)(2,1)S(1)} %get-tuple-element.51), channel_id=1, source_target_pairs={{0,16},{1,17},{2,18},{3,19},{4,20},{5,21},{6,22},{7,23},{8,24},{9,... | collective-permute-start | bytes 196616 | tf_op jit(solution)/shard_map/ppermute | solution.py:130
  39.6 6.5 %collective-permute-start.14 = (bf16[128,256]{1,0:T(8,128)(2,1)S(1)}, bf16[128,256]{1,0:T(8,128)(2,1)S(1)}, u32[]{:S(2)}, u32[]{:S(2)}) collective-permute-start(bf16[128,256]{1,0:T(8,128)(2,1)S(1)} %get-tuple-element.52), channel_id=1, source_target_pairs={{0,24},{1,25},{2,26},{3,27},{4,28},{5,29},{6,30},{7,31},{8,16},{9,... | collective-permute-start | bytes 196616 | tf_op jit(solution)/shard_map/ppermute | solution.py:130
  41.7 4.8 %collective-permute-start.13 = (bf16[128,256]{1,0:T(8,128)(2,1)S(1)}, bf16[128,256]{1,0:T(8,128)(2,1)S(1)}, u32[]{:S(2)}, u32[]{:S(2)}) collective-permute-start(bf16[128,256]{1,0:T(8,128)(2,1)S(1)} %fusion.20), channel_id=1, source_target_pairs={{0,8},{1,9},{2,10},{3,11},{4,12},{5,13},{6,14},{7,15},{8,0},{9,1},... | collective-permute-start | bytes 196616 | tf_op jit(solution)/shard_map/ppermute | solution.py:130
  46.7 5.2 %collective-permute-start.15 = (bf16[128,256]{1,0:T(8,128)(2,1)S(1)}, bf16[128,256]{1,0:T(8,128)(2,1)S(1)}, u32[]{:S(2)}, u32[]{:S(2)}) collective-permute-start(bf16[128,256]{1,0:T(8,128)(2,1)S(1)} %get-tuple-element.35.refs_0_), channel_id=1, source_target_pairs={{0,3},{1,2},{2,1},{3,0},{4,7},{5,6},{6,5},{7,4},{8,11},{9,10},{10,... | collective-permute-start | bytes 196616 | tf_op jit(solution)/shard_map/ppermute | solution.py:130
  48.4 4.3 %collective-permute-start.16 = (bf16[128,256]{1,0:T(8,128)(2,1)S(1)}, bf16[128,256]{1,0:T(8,128)(2,1)S(1)}, u32[]{:S(2)}, u32[]{:S(2)}) collective-permute-start(bf16[128,256]{1,0:T(8,128)(2,1)S(1)} %get-tuple-element.35.refs_0_), channel_id=1, source_target_pairs={{0,2},{1,3},{2,0},{3,1},{4,5},{5,4},{6,7},{7,6},{8,10},{9,11},{10,... | collective-permute-start | bytes 196616 | tf_op jit(solution)/shard_map/ppermute | solution.py:130
  49.0 4.3 %collective-permute-start.17 = (bf16[128,256]{1,0:T(8,128)(2,1)S(1)}, bf16[128,256]{1,0:T(8,128)(2,1)S(1)}, u32[]{:S(2)}, u32[]{:S(2)}) collective-permute-start(bf16[128,256]{1,0:T(8,128)(2,1)S(1)} %get-tuple-element.35.refs_0_), channel_id=1, source_target_pairs={{0,1},{1,0},{2,3},{3,2},{4,6},{5,7},{6,4},{7,5},{8,9},{9,8},{10,11... | collective-permute-start | bytes 196616 | tf_op jit(solution)/shard_map/ppermute | solution.py:130

commit v7 on v6

--- a/solution.py
+++ b/solution.py
@@ -179,17 +179,17 @@
         def term(side, k, value):
             return dot(features[side, k].reshape(-1, 2 * tokens), value).reshape(pairs // 2, rows, rank)
 
-        masks, middle = range(1, fsdp), pairs // 2
+        masks, middle = list(range(1, fsdp)), pairs // 2
         arrivals, arrived, plane, value = [], {}, {}, projected
         for side in (1, 0):
-            terms = {k: term(side, k, value).astype(jnp.bfloat16) for k in masks}
+            terms = {k: term(side, k, value).astype(jnp.bfloat16) for k in masks[::-1]}
             arrived[side] = {k: swap(v, across_fsdp=hops[k]) for k, v in terms.items()}
             value, arrived[side][1] = lax.optimization_barrier((value, arrived[side][1]))
-        for side in (0, 1):
+        for side in (1, 0):
             plane[side] = term(side, 0, projected)
-            for k in masks:
+            for k in masks[1:] + masks[:1]:
                 plane[side] += arrived[side][k].astype(jnp.float32)
-        for k in [middle] + [k for k in range(1, pairs) if k != middle]:
+        for k in range(1, pairs):
             block = plane[k // middle][k % middle].astype(jnp.bfloat16)
             arrivals.append(swap(block, across_pairs=k))
         grad = plane[0][0]
@@ -205,8 +205,8 @@
         step = (new_first / bias_one / (jnp.sqrt(new_second / bias_two) + 1e-08)).astype(jnp.bfloat16)
         step, kept = lax.optimization_barrier((step, grad))
         new_first, new_second = moments(kept)
-        steps = {k: swap(step, across_fsdp=hops[k]) for k in masks}
-        late = [0, *masks[::-1]]
+        late = [0, masks[-1], *masks[:-1]]
+        steps = {k: swap(step, across_fsdp=hops[k]) for k in late[1:]}
 
         def places():
             here, core = lax.axis_index("fsdp"), lax.rem(lax.axis_index("dp"), 2)

time: 55.2 us -> 55.1 us (level)
  no operation moved by 1% of the time
where the time goes in v7:
time: 55.1 us; the launch traced here: 54.9 us
  starting transfers between devices  24.4 us (44%)
  waiting for transfers between devices  16.5 us (30%)
  Pallas kernels  5.58 us (10%)
  matrix products  3.26 us (6%)
  local copies, waits for them, and re-layouts  2.87 us (5%)
  other arithmetic  1.35 us (2%)
  between operations  0.84 us (2%)
    ppermute x18, starting transfers between devices, swap(): return lax.ppermute(value, ('dp', 'fsdp'), steps)  24.4 us
    ppermute x18, waiting for transfers between devices, swap(): return lax.ppermute(value, ('dp', 'fsdp'), steps)  16.5 us
    dot_general x12, matrix products, dot(): return jnp.dot(a, b, preferred_element_type=jnp.float32)  3.26 us
    unnamed x10, local copies, waits for them, and re-layouts  2.52 us
    pallas_call x1, Pallas kernels, pack(): pl.pallas_call(functools.partial(pack_kernel, tokens), out_shape=[pltpu.V...  2.03 us
    pallas_call x1, Pallas kernels, turn(): pl.pallas_call(functools.partial(turn_kernel, rows), out_shape=pltpu.VMEM...  1.88 us
    pallas_call x1, Pallas kernels, update_of(): pl.pallas_call(functools.partial(update_kernel, tiles, places), out_shape...  1.67 us
  transfers between devices with their start and end apart: 18, of which 14 were waited for; matrix products, arithmetic and copies ran while one was open for 7% of the time, Pallas kernels for 7%

profile of v7, /device:TPU:0, one launch (start us, length us, event | category | flops | bytes accessed | tf_op | source)
XLA Modules:
  0.0 54.9 jit_solution(10179437753347269754)
XLA Ops:
  0.6 0.5 collective-permute-start
  1.2 0.6 %copy-done = bf16[2048,256]{1,0:T(8,128)(2,1)S(1)} copy-done((bf16[2048,256]{1,0:T(8,128)(2,1)S(1)}, bf16[2048,256]{1,0:T(8,128)(2,1)}, u32[]{:S(2)}) %copy-start) | copy-done | bytes 1048600
  1.9 3.0 %collective-permute-start.2 = (bf16[1024,256]{1,0:T(8,128)(2,1)S(1)}, bf16[1024,256]{1,0:T(8,128)(2,1)S(1)}, u32[]{:S(2)}, u32[]{:S(2)}) collective-permute-start(bf16[1024,256]{1,0:T(8,128)(2,1)S(1)} %constant_dynamic-slice_fusion.1.first), channel_id=1, source_target_pairs={{0,1},{1,0},{2,3},{3,2},{4,6},{5,7},{6,4},{7,5},{8,9},{9,8},{10,11... | collective-permute-start | bytes 1572872 | tf_op jit(solution)/shard_map/ppermute | solution.py:130
  5.4 1.4 %collective-permute-done.other = bf16[192,8192]{1,0:T(8,128)(2,1)} collective-permute-done((bf16[192,8192]{1,0:T(8,128)(2,1)}, bf16[192,8192]{1,0:T(8,128)(2,1)}, u32[]{:S(2)}, u32[]{:S(2)}) %collective-permute-start) | collective-permute-done | bytes 3145760 | tf_op jit(solution)/shard_map/ppermute | solution.py:130
  6.8 1.9 %copy-done.1 = bf16[192,8192]{1,0:T(8,128)(2,1)S(1)} copy-done((bf16[192,8192]{1,0:T(8,128)(2,1)S(1)}, bf16[192,8192]{1,0:T(8,128)(2,1)}, u32[]{:S(2)}) %copy-start.1) | copy-done | bytes 3145752
  8.7 2.0 %pack_activations.1 = (bf16[384,1024]{1,0:T(8,128)(2,1)S(1)}, bf16[384,1024]{1,0:T(8,128)(2,1)S(1)}, bf16[384,1024]{1,0:T(8,128)(2,1)S(1)}, bf16[384,1024]{1,0:T(8,128)(2,1)S(1)}) custom-call(s32[4]{0:T(128)S(1)} %pad_add_fusion.starts, bf16[192,8192]{1,0:T(8,128)(2,1)S(1)} %copy-done.1, bf16[192,8192]{1,0:T(8,128)(2,1)} %collective-permute-done.other), custom_call_target="tpu_custom_call" | custom-call | tf_op jit(solution)/shard_map/pack_activations/pallas_call | solution.py:42
  10.7 1.3 %collective-permute-done.2 = bf16[1024,256]{1,0:T(8,128)(2,1)S(1)} collective-permute-done((bf16[1024,256]{1,0:T(8,128)(2,1)S(1)}, bf16[1024,256]{1,0:T(8,128)(2,1)S(1)}, u32[]{:S(2)}, u32[]{:S(2)}) %collective-permute-start.2) | collective-permute-done | bytes 524320 | tf_op jit(solution)/shard_map/ppermute | solution.py:130
  12.1 2.0 %collective-permute-start.4 = (bf16[1024,256]{1,0:T(8,128)(2,1)S(1)}, bf16[1024,256]{1,0:T(8,128)(2,1)S(1)}, u32[]{:S(2)}, u32[]{:S(2)}) collective-permute-start(bf16[1024,256]{1,0:T(8,128)(2,1)S(1)} %collective-permute-done.2), channel_id=1, source_target_pairs={{0,2},{1,3},{2,0},{3,1},{4,5},{5,4},{6,7},{7,6},{8,10},{9,11},{10,... | collective-permute-start | bytes 1572872 | tf_op jit(solution)/shard_map/ppermute | solution.py:130
  14.1 1.9 %turn_cotangent.1 = bf16[16,128,384]{2,1,0:T(8,128)(2,1)S(1)} custom-call(s32[16]{0:T(128)S(1)} %add.132.order, bf16[192,4096]{1,0:T(8,128)(2,1)S(1)} %copy-done.2, bf16[192,4096]{1,0:T(8,128)(2,1)} %collective-permute-done.1.other), custom_call_target="tpu_custom_call" | custom-call | tf_op jit(solution)/shard_map/turn_cotangent/pallas_call | solution.py:64
  16.8 3.9 %collective-permute-done.3 = bf16[1024,256]{1,0:T(8,128)(2,1)S(1)} collective-permute-done((bf16[1024,256]{1,0:T(8,128)(2,1)S(1)}, bf16[1024,256]{1,0:T(8,128)(2,1)S(1)}, u32[]{:S(2)}, u32[]{:S(2)}) %collective-permute-start.3) | collective-permute-done | bytes 524320 | tf_op jit(solution)/shard_map/ppermute | solution.py:130
  21.0 1.4 %collective-permute-done.4 = bf16[1024,256]{1,0:T(8,128)(2,1)S(1)} collective-permute-done((bf16[1024,256]{1,0:T(8,128)(2,1)S(1)}, bf16[1024,256]{1,0:T(8,128)(2,1)S(1)}, u32[]{:S(2)}, u32[]{:S(2)}) %collective-permute-start.4) | collective-permute-done | bytes 524320 | tf_op jit(solution)/shard_map/ppermute | solution.py:130
  23.0 0.7 %collective-permute-start.5 = (bf16[384,256]{1,0:T(8,128)(2,1)S(1)}, bf16[384,256]{1,0:T(8,128)(2,1)S(1)}, u32[]{:S(2)}, u32[]{:S(2)}) collective-permute-start(bf16[384,256]{1,0:T(8,128)(2,1)S(1)} %convert_element_type.69), channel_id=1, source_target_pairs={{0,4},{1,5},{2,6},{3,7},{4,0},{5,1},{6,2},{7,3},{8,12},{9,13},{10,... | collective-permute-start | bytes 589832 | tf_op jit(solution)/shard_map/ppermute | solution.py:130
  23.8 0.9 %collective-permute-done.5 = bf16[384,256]{1,0:T(8,128)(2,1)S(1)} collective-permute-done((bf16[384,256]{1,0:T(8,128)(2,1)S(1)}, bf16[384,256]{1,0:T(8,128)(2,1)S(1)}, u32[]{:S(2)}, u32[]{:S(2)}) %collective-permute-start.5) | collective-permute-done | bytes 196640 | tf_op jit(solution)/shard_map/ppermute | solution.py:130
  25.0 2.1 %collective-permute-start.6 = (bf16[2,128,256]{2,1,0:T(8,128)(2,1)S(1)}, bf16[2,128,256]{2,1,0:T(8,128)(2,1)S(1)}, u32[]{:S(2)}, u32[]{:S(2)}) collective-permute-start(bf16[2,128,256]{2,1,0:T(8,128)(2,1)S(1)} %convolution_convert_fusion.5), channel_id=1, source_target_pairs={{0,1},{1,0},{2,3},{3,2},{4,6},{5,7},{6,4},{7,5},{8,9},{9,8},{10,11... | collective-permute-start | bytes 393224 | tf_op jit(solution)/shard_map/ppermute | solution.py:130
  27.6 1.6 %collective-permute-start.11 = (bf16[2,128,256]{2,1,0:T(8,128)(2,1)S(1)}, bf16[2,128,256]{2,1,0:T(8,128)(2,1)S(1)}, u32[]{:S(2)}, u32[]{:S(2)}) collective-permute-start(bf16[2,128,256]{2,1,0:T(8,128)(2,1)S(1)} %convolution_convert_fusion.1), channel_id=1, source_target_pairs={{0,2},{1,3},{2,0},{3,1},{4,5},{5,4},{6,7},{7,6},{8,10},{9,11},{10,... | collective-permute-start | bytes 393224 | tf_op jit(solution)/shard_map/ppermute | solution.py:130
  30.3 3.5 %collective-permute-start.7 = (bf16[2,128,256]{2,1,0:T(8,128)(2,1)S(1)}, bf16[2,128,256]{2,1,0:T(8,128)(2,1)S(1)}, u32[]{:S(2)}, u32[]{:S(2)}) collective-permute-start(bf16[2,128,256]{2,1,0:T(8,128)(2,1)S(1)} %convolution_convert_fusion.4), channel_id=1, source_target_pairs={{0,2},{1,3},{2,0},{3,1},{4,5},{5,4},{6,7},{7,6},{8,10},{9,11},{10,... | collective-permute-start | bytes 393224 | tf_op jit(solution)/shard_map/ppermute | solution.py:130
  34.0 0.9 %collective-permute-start.8 = (bf16[2,128,256]{2,1,0:T(8,128)(2,1)S(1)}, bf16[2,128,256]{2,1,0:T(8,128)(2,1)S(1)}, u32[]{:S(2)}, u32[]{:S(2)}) collective-permute-start(bf16[2,128,256]{2,1,0:T(8,128)(2,1)S(1)} %convolution_convert_fusion.3), channel_id=1, source_target_pairs={{0,3},{1,2},{2,1},{3,0},{4,7},{5,6},{6,5},{7,4},{8,11},{9,10},{10,... | collective-permute-start | bytes 393224 | tf_op jit(solution)/shard_map/ppermute | solution.py:130
  35.2 0.7 %collective-permute-start.9 = (bf16[2,128,256]{2,1,0:T(8,128)(2,1)S(1)}, bf16[2,128,256]{2,1,0:T(8,128)(2,1)S(1)}, u32[]{:S(2)}, u32[]{:S(2)}) collective-permute-start(bf16[2,128,256]{2,1,0:T(8,128)(2,1)S(1)} %convolution_convert_fusion.2), channel_id=1, source_target_pairs={{0,1},{1,0},{2,3},{3,2},{4,6},{5,7},{6,4},{7,5},{8,9},{9,8},{10,11... | collective-permute-start | bytes 393224 | tf_op jit(solution)/shard_map/ppermute | solution.py:130
  35.9 0.9 %collective-permute-done.12 = bf16[2,128,256]{2,1,0:T(8,128)(2,1)S(1)} collective-permute-done((bf16[2,128,256]{2,1,0:T(8,128)(2,1)S(1)}, bf16[2,128,256]{2,1,0:T(8,128)(2,1)S(1)}, u32[]{:S(2)}, u32[]{:S(2)}) %collective-permute-start.12) | collective-permute-done | bytes 131104 | tf_op jit(solution)/shard_map/ppermute | solution.py:130
  36.9 2.7 %collective-permute-start.13 = (bf16[128,256]{1,0:T(8,128)(2,1)S(1)}, bf16[128,256]{1,0:T(8,128)(2,1)S(1)}, u32[]{:S(2)}, u32[]{:S(2)}) collective-permute-start(bf16[128,256]{1,0:T(8,128)(2,1)S(1)} %get-tuple-element.51), channel_id=1, source_target_pairs={{0,16},{1,17},{2,18},{3,19},{4,20},{5,21},{6,22},{7,23},{8,24},{9,... | collective-permute-start | bytes 196616 | tf_op jit(solution)/shard_map/ppermute | solution.py:130
  39.5 1.3 %collective-permute-start.14 = (bf16[128,256]{1,0:T(8,128)(2,1)S(1)}, bf16[128,256]{1,0:T(8,128)(2,1)S(1)}, u32[]{:S(2)}, u32[]{:S(2)}) collective-permute-start(bf16[128,256]{1,0:T(8,128)(2,1)S(1)} %get-tuple-element.52), channel_id=1, source_target_pairs={{0,24},{1,25},{2,26},{3,27},{4,28},{5,29},{6,30},{7,31},{8,16},{9,... | collective-permute-start | bytes 196616 | tf_op jit(solution)/shard_map/ppermute | solution.py:130
  40.9 0.5 collective-permute-done.7
  41.4 1.5 %collective-permute-start.10 = (bf16[128,256]{1,0:T(8,128)(2,1)S(1)}, bf16[128,256]{1,0:T(8,128)(2,1)S(1)}, u32[]{:S(2)}, u32[]{:S(2)}) collective-permute-start(bf16[128,256]{1,0:T(8,128)(2,1)S(1)} %fusion.20), channel_id=1, source_target_pairs={{0,8},{1,9},{2,10},{3,11},{4,12},{5,13},{6,14},{7,15},{8,0},{9,1},... | collective-permute-start | bytes 196616 | tf_op jit(solution)/shard_map/ppermute | solution.py:130
  43.0 0.8 %collective-permute-done.13 = bf16[128,256]{1,0:T(8,128)(2,1)S(1)} collective-permute-done((bf16[128,256]{1,0:T(8,128)(2,1)S(1)}, bf16[128,256]{1,0:T(8,128)(2,1)S(1)}, u32[]{:S(2)}, u32[]{:S(2)}) %collective-permute-start.13) | collective-permute-done | bytes 65568 | tf_op jit(solution)/shard_map/ppermute | solution.py:130
  43.7 2.0 %collective-permute-done.14 = bf16[128,256]{1,0:T(8,128)(2,1)S(1)} collective-permute-done((bf16[128,256]{1,0:T(8,128)(2,1)S(1)}, bf16[128,256]{1,0:T(8,128)(2,1)S(1)}, u32[]{:S(2)}, u32[]{:S(2)}) %collective-permute-start.14) | collective-permute-done | bytes 65568 | tf_op jit(solution)/shard_map/ppermute | solution.py:130
  45.7 1.0 %collective-permute-done.10 = bf16[128,256]{1,0:T(8,128)(2,1)S(1)} collective-permute-done((bf16[128,256]{1,0:T(8,128)(2,1)S(1)}, bf16[128,256]{1,0:T(8,128)(2,1)S(1)}, u32[]{:S(2)}, u32[]{:S(2)}) %collective-permute-start.10) | collective-permute-done | bytes 65568 | tf_op jit(solution)/shard_map/ppermute | solution.py:130
  46.8 1.6 %collective-permute-start.15 = (bf16[128,256]{1,0:T(8,128)(2,1)S(1)}, bf16[128,256]{1,0:T(8,128)(2,1)S(1)}, u32[]{:S(2)}, u32[]{:S(2)}) collective-permute-start(bf16[128,256]{1,0:T(8,128)(2,1)S(1)} %get-tuple-element.35.refs_0_), channel_id=1, source_target_pairs={{0,3},{1,2},{2,1},{3,0},{4,7},{5,6},{6,5},{7,4},{8,11},{9,10},{10,... | collective-permute-start | bytes 196616 | tf_op jit(solution)/shard_map/ppermute | solution.py:130
  48.4 0.5 collective-permute-start.16
  48.9 1.4 %collective-permute-start.17 = (bf16[128,256]{1,0:T(8,128)(2,1)S(1)}, bf16[128,256]{1,0:T(8,128)(2,1)S(1)}, u32[]{:S(2)}, u32[]{:S(2)}) collective-permute-start(bf16[128,256]{1,0:T(8,128)(2,1)S(1)} %get-tuple-element.35.refs_0_), channel_id=1, source_target_pairs={{0,2},{1,3},{2,0},{3,1},{4,5},{5,4},{6,7},{7,6},{8,10},{9,11},{10,... | collective-permute-start | bytes 196616 | tf_op jit(solution)/shard_map/ppermute | solution.py:130
  50.3 0.7 %fusion.15 = (f32[128,256]{1,0:T(8,128)}, f32[128,256]{1,0:T(8,128)}) fusion(f32[128,256]{1,0:T(8,128)S(1)} %get-tuple-element.36, f32[128,256]{1,0:T(8,128)S(1)} %copy-done.3, f32[128,256]{1,0:T(8,128)S(1)} %copy-done.4), kind=kLoop, calls=%fused_computation.28 | loop fusion | flops 229376 | bytes 655360 | tf_op jit(solution)/shard_map/add | solution.py:200
  51.1 1.3 %collective-permute-done.15.refs_1_ = bf16[128,256]{1,0:T(8,128)(2,1)S(1)} collective-permute-done((bf16[128,256]{1,0:T(8,128)(2,1)S(1)}, bf16[128,256]{1,0:T(8,128)(2,1)S(1)}, u32[]{:S(2)}, u32[]{:S(2)}) %collective-permute-start.15) | collective-permute-done | bytes 65568 | tf_op jit(solution)/shard_map/ppermute | solution.py:130
  53.2 1.7 %update.1 = bf16[2048,512]{1,0:T(8,128)(2,1)} custom-call(bf16[1024,256]{1,0:T(8,128)(2,1)S(1)} %constant_dynamic-slice_fusion.1.first, bf16[1024,256]{1,0:T(8,128)(2,1)S(1)} %constant_dynamic-slice_fusion.second, bf16[128,256]{1,0:T(8,128)(2,1)S(1)} %get-tuple-element.35.refs_0_, bf16[128,256]{1,0:T(8,128)(2,1)S(1)} %collective-permute-done.15.refs_1_, ...), custom_call_target="tpu_custom_call" | custom-call | tf_op jit(solution)/shard_map/update/pallas_call | solution.py:104
  (47 shorter events, 5.6 us)
Async XLA Ops:
  0.6 1.2 %copy-start = (bf16[2048,256]{1,0:T(8,128)(2,1)S(1)}, bf16[2048,256]{1,0:T(8,128)(2,1)}, u32[]{:S(2)}) copy-start(bf16[2048,256]{1,0:T(8,128)(2,1)} %param.7) | copy-start | bytes 3145732
  0.6 6.1 %collective-permute-start = (bf16[192,8192]{1,0:T(8,128)(2,1)}, bf16[192,8192]{1,0:T(8,128)(2,1)}, u32[]{:S(2)}, u32[]{:S(2)}) collective-permute-start(bf16[192,8192]{1,0:T(8,128)(2,1)} %own.2), channel_id=1, source_target_pairs={{0,4},{1,5},{2,6},{3,7},{4,0},{5,1},{6,2},{7,3},{8,12},{9,13},{10,... | collective-permute-start | bytes 9437192 | tf_op jit(solution)/shard_map/ppermute | solution.py:130
  1.2 13.0 %collective-permute-start.1 = (bf16[192,4096]{1,0:T(8,128)(2,1)}, bf16[192,4096]{1,0:T(8,128)(2,1)}, u32[]{:S(2)}, u32[]{:S(2)}) collective-permute-start(bf16[192,4096]{1,0:T(8,128)(2,1)} %own.3), channel_id=1, source_target_pairs={{0,4},{1,5},{2,6},{3,7},{4,0},{5,1},{6,2},{7,3},{8,12},{9,13},{10,... | collective-permute-start | bytes 4718600 | tf_op jit(solution)/shard_map/ppermute | solution.py:130
  1.9 10.2 %collective-permute-start.2 = (bf16[1024,256]{1,0:T(8,128)(2,1)S(1)}, bf16[1024,256]{1,0:T(8,128)(2,1)S(1)}, u32[]{:S(2)}, u32[]{:S(2)}) collective-permute-start(bf16[1024,256]{1,0:T(8,128)(2,1)S(1)} %constant_dynamic-slice_fusion.1.first), channel_id=1, source_target_pairs={{0,1},{1,0},{2,3},{3,2},{4,6},{5,7},{6,4},{7,5},{8,9},{9,8},{10,11... | collective-permute-start | bytes 1572872 | tf_op jit(solution)/shard_map/ppermute | solution.py:130
  4.9 15.7 %collective-permute-start.3 = (bf16[1024,256]{1,0:T(8,128)(2,1)S(1)}, bf16[1024,256]{1,0:T(8,128)(2,1)S(1)}, u32[]{:S(2)}, u32[]{:S(2)}) collective-permute-start(bf16[1024,256]{1,0:T(8,128)(2,1)S(1)} %constant_dynamic-slice_fusion.second), channel_id=1, source_target_pairs={{0,1},{1,0},{2,3},{3,2},{4,6},{5,7},{6,4},{7,5},{8,9},{9,8},{10,11... | collective-permute-start | bytes 1572872 | tf_op jit(solution)/shard_map/ppermute | solution.py:130
  6.8 1.9 %copy-start.1 = (bf16[192,8192]{1,0:T(8,128)(2,1)S(1)}, bf16[192,8192]{1,0:T(8,128)(2,1)}, u32[]{:S(2)}) copy-start(bf16[192,8192]{1,0:T(8,128)(2,1)} %own.2) | copy-start | bytes 9437188
  8.7 5.4 %copy-start.2 = (bf16[192,4096]{1,0:T(8,128)(2,1)S(1)}, bf16[192,4096]{1,0:T(8,128)(2,1)}, u32[]{:S(2)}) copy-start(bf16[192,4096]{1,0:T(8,128)(2,1)} %own.3) | copy-start | bytes 4718596
  12.1 10.4 %collective-permute-start.4 = (bf16[1024,256]{1,0:T(8,128)(2,1)S(1)}, bf16[1024,256]{1,0:T(8,128)(2,1)S(1)}, u32[]{:S(2)}, u32[]{:S(2)}) collective-permute-start(bf16[1024,256]{1,0:T(8,128)(2,1)S(1)} %collective-permute-done.2), channel_id=1, source_target_pairs={{0,2},{1,3},{2,0},{3,1},{4,5},{5,4},{6,7},{7,6},{8,10},{9,11},{10,... | collective-permute-start | bytes 1572872 | tf_op jit(solution)/shard_map/ppermute | solution.py:130
  23.0 1.8 %collective-permute-start.5 = (bf16[384,256]{1,0:T(8,128)(2,1)S(1)}, bf16[384,256]{1,0:T(8,128)(2,1)S(1)}, u32[]{:S(2)}, u32[]{:S(2)}) collective-permute-start(bf16[384,256]{1,0:T(8,128)(2,1)S(1)} %convert_element_type.69), channel_id=1, source_target_pairs={{0,4},{1,5},{2,6},{3,7},{4,0},{5,1},{6,2},{7,3},{8,12},{9,13},{10,... | collective-permute-start | bytes 589832 | tf_op jit(solution)/shard_map/ppermute | solution.py:130
  25.0 5.0 %collective-permute-start.6 = (bf16[2,128,256]{2,1,0:T(8,128)(2,1)S(1)}, bf16[2,128,256]{2,1,0:T(8,128)(2,1)S(1)}, u32[]{:S(2)}, u32[]{:S(2)}) collective-permute-start(bf16[2,128,256]{2,1,0:T(8,128)(2,1)S(1)} %convolution_convert_fusion.5), channel_id=1, source_target_pairs={{0,1},{1,0},{2,3},{3,2},{4,6},{5,7},{6,4},{7,5},{8,9},{9,8},{10,11... | collective-permute-start | bytes 393224 | tf_op jit(solution)/shard_map/ppermute | solution.py:130
  27.6 8.3 %collective-permute-start.11 = (bf16[2,128,256]{2,1,0:T(8,128)(2,1)S(1)}, bf16[2,128,256]{2,1,0:T(8,128)(2,1)S(1)}, u32[]{:S(2)}, u32[]{:S(2)}) collective-permute-start(bf16[2,128,256]{2,1,0:T(8,128)(2,1)S(1)} %convolution_convert_fusion.1), channel_id=1, source_target_pairs={{0,2},{1,3},{2,0},{3,1},{4,5},{5,4},{6,7},{7,6},{8,10},{9,11},{10,... | collective-permute-start | bytes 393224 | tf_op jit(solution)/shard_map/ppermute | solution.py:130
  29.4 7.4 %collective-permute-start.12 = (bf16[2,128,256]{2,1,0:T(8,128)(2,1)S(1)}, bf16[2,128,256]{2,1,0:T(8,128)(2,1)S(1)}, u32[]{:S(2)}, u32[]{:S(2)}) collective-permute-start(bf16[2,128,256]{2,1,0:T(8,128)(2,1)S(1)} %convolution_convert_fusion), channel_id=1, source_target_pairs={{0,3},{1,2},{2,1},{3,0},{4,7},{5,6},{6,5},{7,4},{8,11},{9,10},{10,... | collective-permute-start | bytes 393224 | tf_op jit(solution)/shard_map/ppermute | solution.py:130
  30.3 11.1 %collective-permute-start.7 = (bf16[2,128,256]{2,1,0:T(8,128)(2,1)S(1)}, bf16[2,128,256]{2,1,0:T(8,128)(2,1)S(1)}, u32[]{:S(2)}, u32[]{:S(2)}) collective-permute-start(bf16[2,128,256]{2,1,0:T(8,128)(2,1)S(1)} %convolution_convert_fusion.4), channel_id=1, source_target_pairs={{0,2},{1,3},{2,0},{3,1},{4,5},{5,4},{6,7},{7,6},{8,10},{9,11},{10,... | collective-permute-start | bytes 393224 | tf_op jit(solution)/shard_map/ppermute | solution.py:130
  33.8 12.8 %copy-start.3 = (f32[128,256]{1,0:T(8,128)S(1)}, f32[128,256]{1,0:T(8,128)}, u32[]{:S(2)}) copy-start(f32[128,256]{1,0:T(8,128)} %param.9) | copy-start | bytes 393220
  33.8 12.8 %copy-start.4 = (f32[128,256]{1,0:T(8,128)S(1)}, f32[128,256]{1,0:T(8,128)}, u32[]{:S(2)}) copy-start(f32[128,256]{1,0:T(8,128)} %param.8) | copy-start | bytes 393220
  34.0 7.3 %collective-permute-start.8 = (bf16[2,128,256]{2,1,0:T(8,128)(2,1)S(1)}, bf16[2,128,256]{2,1,0:T(8,128)(2,1)S(1)}, u32[]{:S(2)}, u32[]{:S(2)}) collective-permute-start(bf16[2,128,256]{2,1,0:T(8,128)(2,1)S(1)} %convolution_convert_fusion.3), channel_id=1, source_target_pairs={{0,3},{1,2},{2,1},{3,0},{4,7},{5,6},{6,5},{7,4},{8,11},{9,10},{10,... | collective-permute-start | bytes 393224 | tf_op jit(solution)/shard_map/ppermute | solution.py:130
  35.2 5.7 %collective-permute-start.9 = (bf16[2,128,256]{2,1,0:T(8,128)(2,1)S(1)}, bf16[2,128,256]{2,1,0:T(8,128)(2,1)S(1)}, u32[]{:S(2)}, u32[]{:S(2)}) collective-permute-start(bf16[2,128,256]{2,1,0:T(8,128)(2,1)S(1)} %convolution_convert_fusion.2), channel_id=1, source_target_pairs={{0,1},{1,0},{2,3},{3,2},{4,6},{5,7},{6,4},{7,5},{8,9},{9,8},{10,11... | collective-permute-start | bytes 393224 | tf_op jit(solution)/shard_map/ppermute | solution.py:130
  36.9 6.9 %collective-permute-start.13 = (bf16[128,256]{1,0:T(8,128)(2,1)S(1)}, bf16[128,256]{1,0:T(8,128)(2,1)S(1)}, u32[]{:S(2)}, u32[]{:S(2)}) collective-permute-start(bf16[128,256]{1,0:T(8,128)(2,1)S(1)} %get-tuple-element.51), channel_id=1, source_target_pairs={{0,16},{1,17},{2,18},{3,19},{4,20},{5,21},{6,22},{7,23},{8,24},{9,... | collective-permute-start | bytes 196616 | tf_op jit(solution)/shard_map/ppermute | solution.py:130
  39.5 6.2 %collective-permute-start.14 = (bf16[128,256]{1,0:T(8,128)(2,1)S(1)}, bf16[128,256]{1,0:T(8,128)(2,1)S(1)}, u32[]{:S(2)}, u32[]{:S(2)}) collective-permute-start(bf16[128,256]{1,0:T(8,128)(2,1)S(1)} %get-tuple-element.52), channel_id=1, source_target_pairs={{0,24},{1,25},{2,26},{3,27},{4,28},{5,29},{6,30},{7,31},{8,16},{9,... | collective-permute-start | bytes 196616 | tf_op jit(solution)/shard_map/ppermute | solution.py:130
  41.4 5.2 %collective-permute-start.10 = (bf16[128,256]{1,0:T(8,128)(2,1)S(1)}, bf16[128,256]{1,0:T(8,128)(2,1)S(1)}, u32[]{:S(2)}, u32[]{:S(2)}) collective-permute-start(bf16[128,256]{1,0:T(8,128)(2,1)S(1)} %fusion.20), channel_id=1, source_target_pairs={{0,8},{1,9},{2,10},{3,11},{4,12},{5,13},{6,14},{7,15},{8,0},{9,1},... | collective-permute-start | bytes 196616 | tf_op jit(solution)/shard_map/ppermute | solution.py:130
  46.8 5.6 %collective-permute-start.15 = (bf16[128,256]{1,0:T(8,128)(2,1)S(1)}, bf16[128,256]{1,0:T(8,128)(2,1)S(1)}, u32[]{:S(2)}, u32[]{:S(2)}) collective-permute-start(bf16[128,256]{1,0:T(8,128)(2,1)S(1)} %get-tuple-element.35.refs_0_), channel_id=1, source_target_pairs={{0,3},{1,2},{2,1},{3,0},{4,7},{5,6},{6,5},{7,4},{8,11},{9,10},{10,... | collective-permute-start | bytes 196616 | tf_op jit(solution)/shard_map/ppermute | solution.py:130
  48.4 4.3 %collective-permute-start.16 = (bf16[128,256]{1,0:T(8,128)(2,1)S(1)}, bf16[128,256]{1,0:T(8,128)(2,1)S(1)}, u32[]{:S(2)}, u32[]{:S(2)}) collective-permute-start(bf16[128,256]{1,0:T(8,128)(2,1)S(1)} %get-tuple-element.35.refs_0_), channel_id=1, source_target_pairs={{0,1},{1,0},{2,3},{3,2},{4,6},{5,7},{6,4},{7,5},{8,9},{9,8},{10,11... | collective-permute-start | bytes 196616 | tf_op jit(solution)/shard_map/ppermute | solution.py:130
  48.9 4.3 %collective-permute-start.17 = (bf16[128,256]{1,0:T(8,128)(2,1)S(1)}, bf16[128,256]{1,0:T(8,128)(2,1)S(1)}, u32[]{:S(2)}, u32[]{:S(2)}) collective-permute-start(bf16[128,256]{1,0:T(8,128)(2,1)S(1)} %get-tuple-element.35.refs_0_), channel_id=1, source_target_pairs={{0,2},{1,3},{2,0},{3,1},{4,5},{5,4},{6,7},{7,6},{8,10},{9,11},{10,... | collective-permute-start | bytes 196616 | tf_op jit(solution)/shard_map/ppermute | solution.py:130
